TPU v7x, 32 devices: a whole 2x2x4 slice. The times are simulated.
32 devices in a mesh: slab: 8 (over z, y), pen: 4 (over x, core).
Axes of the slice: x: 2, y: 2, z: 4, core: 2. Of those that a mesh axis runs over, the one named last changes fastest.
Arguments:
- counts: int32 [256, 16], P('slab', 'pen'), may hold values from 0 to 512, as said below
- row_base: int32 [256, 16, 512], P('slab', 'pen'), may hold values from 0 to 15
- z_base: int32 [256, 16, 512], P('slab', 'pen'), may hold values from 0 to 255
- fractions: float32 [3, 256, 16, 512], P(None, 'slab', 'pen'), may hold values from 0 to 0.999
- strength: float32 [3, 256, 16, 512], P(None, 'slab', 'pen'), may hold values from -72 to 72
Outputs:
- vorticity: float32 [3, 256, 256, 256], P(None, 'slab', 'pen')
- velocity: float32 [3, 256, 256, 256], P(None, 'slab', 'pen')
- stretching: float32 [3, 256, 256, 256], P(None, 'slab', 'pen')
Inputs may be any that keep to these rules, and one draw needn't show every extreme that they name: Slots s < counts[q, b] of group (q, b) hold particles, the others are unused; some group holds exactly 512 particles.
All inputs are finite; a program needn't handle non-finite values.
Results may differ from a plain program's by a relative error of at most 0.0052.
Values sent between devices are 32-bit elements; how exact they have to be, the bound alone decides.
No kernel may reach another device: no remote copies, remote signals or barrier semaphores. Data moves between devices by JAX's collectives and lax.ppermute only.
A program may use at most 192 MiB of HBM per device.

v0:
```python
import math

import jax
import jax.numpy as jnp
from jax import lax
from jax.sharding import PartitionSpec as P

NX = 256
NY = 256
NZ = 256
BLOCK_ROWS = 16


PRECISE = lax.Precision.HIGHEST


def from_behind(block, axis, distance):
    devices = range(lax.axis_size(axis))
    route = [((i - distance) % len(devices), i) for i in devices]
    return lax.ppermute(block, axis, route)


def padded_2(cells, sides, width):
    for axis, dim in sides:
        count = lax.axis_size(axis)
        head = lax.slice_in_dim(cells, 0, width, axis=dim)
        tail = lax.slice_in_dim(cells, cells.shape[dim] - width, cells.shape[dim], axis=dim)
        cells = jnp.concatenate(
            [
                lax.ppermute(tail, axis, [(i, (i + 1) % count) for i in range(count)]),
                cells,
                lax.ppermute(head, axis, [((i + 1) % count, i) for i in range(count)]),
            ],
            axis=dim,
        )
    return cells


def kernel_weight(distance):
    magnitude = jnp.abs(distance)
    inner_part = 1.0 - 2.5 * magnitude * magnitude + 1.5 * magnitude * magnitude * magnitude
    outer_part = 0.5 * (2.0 - magnitude) * (2.0 - magnitude) * (1.0 - magnitude)
    return jnp.where(magnitude < 1.0, inner_part, jnp.where(magnitude < 2.0, outer_part, 0.0))


def wavenumbers(frequency, length):
    signed_index = jnp.where(frequency < length // 2, frequency, frequency - length)
    full_wave = 2.0 * math.pi / length * signed_index.astype(jnp.float32)
    curl_wave = jnp.where(frequency == length // 2, 0.0, full_wave)
    return (full_wave, curl_wave)


def tables(row_values, length, sign_value):
    columns = jnp.arange(length, dtype=jnp.int32)
    turn_count = row_values[:, None] * columns[None, :] % length
    angles = 2.0 * math.pi / length * turn_count.astype(jnp.float32)
    return (jnp.cos(angles), sign_value * jnp.sin(angles))


def complex_apply(real_part, imaginary, table_pair, pattern):
    cosine_table, sine_table = table_pair
    real_out = jnp.einsum(pattern, real_part, cosine_table, precision=PRECISE) - jnp.einsum(
        pattern, imaginary, sine_table, precision=PRECISE
    )
    imaginary_out = jnp.einsum(pattern, real_part, sine_table, precision=PRECISE) + jnp.einsum(
        pattern, imaginary, cosine_table, precision=PRECISE
    )
    return (real_out, imaginary_out)


def natural_order():
    return jnp.arange(NZ, dtype=jnp.int32)


def deposit(counts, row_base, z_base, fractions, strength):
    planes = counts.shape[0]
    blocks_here = counts.shape[1]
    slot_total = row_base.shape[2]
    rows_local = blocks_here * BLOCK_ROWS
    ext_rows = BLOCK_ROWS + 3
    active = (jnp.arange(slot_total, dtype=jnp.int32)[None, None, :] < counts[:, :, None]).astype(
        jnp.float32
    )
    z_column = jnp.arange(NZ, dtype=jnp.int32)
    row_index = jnp.arange(ext_rows, dtype=jnp.int32)
    offsets = jnp.arange(4, dtype=jnp.int32)

    def one_plane(plane_index, grid_sum):
        fraction_here = lax.dynamic_index_in_dim(fractions, plane_index, 1, keepdims=False)
        charge = lax.dynamic_index_in_dim(strength, plane_index, 1, keepdims=False)
        row_cells = lax.dynamic_index_in_dim(row_base, plane_index, 0, keepdims=False)
        z_cells = lax.dynamic_index_in_dim(z_base, plane_index, 0, keepdims=False)
        active_here = lax.dynamic_index_in_dim(active, plane_index, 0, keepdims=False)
        weight_x = kernel_weight(
            (offsets[:, None, None] - 1).astype(jnp.float32) - fraction_here[0][None]
        )
        weight_y = kernel_weight(
            (row_index[:, None, None] - 1 - row_cells[None]).astype(jnp.float32)
            - fraction_here[1][None]
        )
        z_offset = (z_column[None, None, :] - z_cells[:, :, None]) % NZ
        weight_z = kernel_weight(
            (z_offset - 1).astype(jnp.float32) - fraction_here[2][:, :, None]
        ).astype(jnp.bfloat16)
        coefs = (
            charge[:, None, None] * weight_x[None, :, None] * weight_y[None, None, :] * active_here
        ).astype(jnp.bfloat16)
        spread = jnp.einsum("cajbs,bsz->bcajz", coefs, weight_z, preferred_element_type=jnp.float32)
        plane_sum = jnp.zeros((3, 4, rows_local + 3, NZ), jnp.float32)
        for block_index in range(blocks_here):
            low_row = block_index * BLOCK_ROWS
            plane_sum = plane_sum.at[:, :, low_row : low_row + ext_rows].add(spread[block_index])
        window = lax.dynamic_slice_in_dim(grid_sum, plane_index, 4, 1)
        return lax.dynamic_update_slice_in_dim(grid_sum, window + plane_sum, plane_index, 1)

    start_sum = jnp.zeros((3, planes + 3, rows_local + 3, NZ), jnp.float32)
    grid_sum = lax.fori_loop(0, planes, one_plane, start_sum)
    ghost_tail = from_behind(grid_sum[:, planes:], "slab", 1)
    interior = grid_sum[:, :planes].at[:, :3].add(ghost_tail)
    ghost_side = from_behind(interior[:, :, rows_local:], "pen", 1)
    return interior[:, :, :rows_local].at[:, :, :3].add(ghost_side)


def grid_inverse(real_part, imaginary, slab_count, pen_count, order):
    real_part, imaginary = complex_apply(
        real_part, imaginary, tables(jnp.arange(NX, dtype=jnp.int32), NX, 1.0), "ckny,nm->ckmy"
    )
    real_part, imaginary = complex_apply(
        real_part, imaginary, tables(jnp.arange(NY, dtype=jnp.int32), NY, 1.0), "ckxn,nm->ckxm"
    )
    real_part, imaginary = (
        lax.all_to_all(
            lax.all_to_all(real_part, "slab", split_axis=2, concat_axis=1, tiled=True),
            "pen",
            split_axis=3,
            concat_axis=1,
            tiled=True,
        ),
        lax.all_to_all(
            lax.all_to_all(imaginary, "slab", split_axis=2, concat_axis=1, tiled=True),
            "pen",
            split_axis=3,
            concat_axis=1,
            tiled=True,
        ),
    )
    pen_block = NZ // pen_count
    z_depth = pen_block // slab_count
    position = jnp.arange(NZ, dtype=jnp.int32)
    forward_position = (
        position % pen_block // z_depth * (NZ // slab_count)
        + position // pen_block * z_depth
        + position % z_depth
    )
    frequency = order[forward_position]
    cosine_table, sine_table = tables(frequency, NZ, 1.0)
    real_out = jnp.einsum("cnxy,nm->cxym", real_part, cosine_table, precision=PRECISE) - jnp.einsum(
        "cnxy,nm->cxym", imaginary, sine_table, precision=PRECISE
    )
    imaginary_out = jnp.einsum(
        "cnxy,nm->cxym", real_part, sine_table, precision=PRECISE
    ) + jnp.einsum("cnxy,nm->cxym", imaginary, cosine_table, precision=PRECISE)
    return (real_out, imaginary_out)


def invert_all(spectra, slab_count, pen_count, order):
    fields = []
    packed_real = []
    packed_imaginary = []
    for first_index in range(0, len(spectra), 2):
        left_field = spectra[first_index]
        if first_index + 1 < len(spectra):
            right_field = spectra[first_index + 1]
            packed_real.append(left_field[0] - right_field[1])
            packed_imaginary.append(left_field[1] + right_field[0])
        else:
            packed_real.append(left_field[0])
            packed_imaginary.append(left_field[1])
    grid_real, grid_imaginary = grid_inverse(
        jnp.stack(packed_real), jnp.stack(packed_imaginary), slab_count, pen_count, order
    )
    for first_index in range(0, len(spectra), 2):
        fields.append(grid_real[first_index // 2])
        if first_index + 1 < len(spectra):
            fields.append(grid_imaginary[first_index // 2])
    return fields


def per_device(counts, row_base, z_base, fractions, strength):
    vorticity = deposit(counts, row_base, z_base, fractions, strength)
    slab_count = lax.axis_size("slab")
    pen_count = lax.axis_size("pen")
    x_tables = tables(jnp.arange(NX, dtype=jnp.int32), NX, -1.0)
    y_tables = tables(jnp.arange(NY, dtype=jnp.int32), NY, -1.0)
    order = natural_order()
    cosine_z, sine_z = tables(order, NZ, -1.0)
    real_part = jnp.einsum("cxyn,kn->ckxy", vorticity, cosine_z, precision=PRECISE)
    imaginary = jnp.einsum("cxyn,kn->ckxy", vorticity, sine_z, precision=PRECISE)
    real_part, imaginary = (
        lax.all_to_all(
            lax.all_to_all(real_part, "slab", split_axis=1, concat_axis=2, tiled=True),
            "pen",
            split_axis=1,
            concat_axis=3,
            tiled=True,
        ),
        lax.all_to_all(
            lax.all_to_all(imaginary, "slab", split_axis=1, concat_axis=2, tiled=True),
            "pen",
            split_axis=1,
            concat_axis=3,
            tiled=True,
        ),
    )
    real_part, imaginary = complex_apply(real_part, imaginary, x_tables, "ckny,nm->ckmy")
    real_part, imaginary = complex_apply(real_part, imaginary, y_tables, "ckxn,nm->ckxm")
    z_depth = real_part.shape[1]
    z_position = (
        lax.axis_index("slab") * (NZ // slab_count)
        + lax.axis_index("pen") * z_depth
        + jnp.arange(z_depth, dtype=jnp.int32)
    )
    z_frequency = order[z_position]
    full_z, curl_z = wavenumbers(z_frequency, NZ)
    full_x, curl_x = wavenumbers(jnp.arange(NX, dtype=jnp.int32), NX)
    full_y, curl_y = wavenumbers(jnp.arange(NY, dtype=jnp.int32), NY)
    full_z, curl_z = (full_z[:, None, None], curl_z[:, None, None])
    full_x, curl_x = (full_x[None, :, None], curl_x[None, :, None])
    full_y, curl_y = (full_y[None, None, :], curl_y[None, None, :])
    wave_squared = full_x * full_x + full_y * full_y + full_z * full_z
    scaling = jnp.where(
        wave_squared > 0.0, 1.0 / jnp.where(wave_squared > 0.0, wave_squared, 1.0), 0.0
    ) / float(NX * NY * NZ)

    def cross_with(parts):
        return (
            curl_y * parts[2] - curl_z * parts[1],
            curl_z * parts[0] - curl_x * parts[2],
            curl_x * parts[1] - curl_y * parts[0],
        )

    cross_real = cross_with(real_part)
    cross_imaginary = cross_with(imaginary)
    spectra = []
    for component in range(3):
        spectra.append((-cross_imaginary[component] * scaling, cross_real[component] * scaling))
    fields = invert_all(spectra, slab_count, pen_count, order)
    velocity = jnp.stack(fields)
    planes = velocity.shape[1]
    rows_local = velocity.shape[2]
    padded = padded_2(velocity, (("slab", 1), ("pen", 2)), 2)
    middle_x = padded[:, :, 2 : rows_local + 2]
    middle_y = padded[:, 2 : planes + 2]
    along_x = (
        8.0 * (middle_x[:, 3 : planes + 3] - middle_x[:, 1 : planes + 1])
        - (middle_x[:, 4 : planes + 4] - middle_x[:, 0:planes])
    ) / 12.0
    along_y = (
        8.0 * (middle_y[:, :, 3 : rows_local + 3] - middle_y[:, :, 1 : rows_local + 1])
        - (middle_y[:, :, 4 : rows_local + 4] - middle_y[:, :, 0:rows_local])
    ) / 12.0
    along_z = (
        8.0 * (jnp.roll(velocity, -1, 3) - jnp.roll(velocity, 1, 3))
        - (jnp.roll(velocity, -2, 3) - jnp.roll(velocity, 2, 3))
    ) / 12.0
    stretching = vorticity[0][None] * along_x
    stretching = stretching + vorticity[1][None] * along_y
    stretching = stretching + vorticity[2][None] * along_z
    return (vorticity, velocity, stretching)


def solution(mesh):
    in_specs = (
        P("slab", "pen"),
        P("slab", "pen", None),
        P("slab", "pen", None),
        P(None, "slab", "pen", None),
        P(None, "slab", "pen", None),
    )
    out_specs = (
        P(None, "slab", "pen", None),
        P(None, "slab", "pen", None),
        P(None, "slab", "pen", None),
    )
    return jax.shard_map(
        per_device, mesh=mesh, in_specs=in_specs, out_specs=out_specs, check_vma=False
    )
```

profile of v0, /device:TPU:17, one launch (start us, length us, event | category | flops | bytes accessed | tf_op | source)
XLA Modules:
  0.0 1396.1 jit_solution(5848487260318765652)
XLA Ops:
  5.0 299.4 %while.23 = (s32[]{:T(128)}, f32[3,35,67,256]{3,2,1,0:T(8,128)}, f32[3,32,4,512]{3,2,1,0:T(4,128)}, f32[3,32,4,512]{3,2,1,0:T(4,128)}, s32[32,4,512]{2,1,0:T(4,1...) while((s32[]{:T(128)}, f32[3,35,67,256]{3,2,1,0:T(8,128)}, ...), condition=%wide.region_1.2_spmd.clone, body=%wide.region_0.1_spmd.clone.sunk | while | flops 259108896 | bytes 9114489 | solution.py:117
  323.8 13.4 scatter-add.24
  361.1 12.7 copy.148
  373.8 12.6 reshape.744
  404.1 12.7 copy.139
  416.8 12.6 reshape.742
  429.5 97.6 %all-to-all-done.2 = f32[8,1,196608]{2,1,0:T(1,128)} async-done(((f32[8,1,196608]{2,1,0:T(1,128)}), f32[8,1,196608]{2,1,0:T(1,128)}, u32[]{:S(2)}, u32[]{:S(2)}) %all-to-all-start.2) | async-done | bytes 6291488 | tf_op jit(solution)/shard_map/all_to_all | solution.py:208
  536.1 19.5 %reduce.39 = f32[8,196608]{1,0:T(8,128)} reduce(f32[8,1,196608]{2,1,0:T(1,128)} %all-to-all-done.2, f32[]{:T(128)} %broadcast.1357), dimensions={1}, to_apply=%all_to_all.112.reduce_sub_computation | reduce | bytes 12582916 | tf_op jit(solution)/shard_map/all_to_all | solution.py:208
  555.6 12.3 reshape.745
  588.9 80.0 %all-to-all-done = f32[8,1,196608]{2,1,0:T(1,128)} async-done(((f32[8,1,196608]{2,1,0:T(1,128)}), f32[8,1,196608]{2,1,0:T(1,128)}, u32[]{:S(2)}, u32[]{:S(2)}) %all-to-all-start) | async-done | bytes 6291488 | tf_op jit(solution)/shard_map/all_to_all | solution.py:201
  677.2 19.5 %reduce.38 = f32[8,196608]{1,0:T(8,128)} reduce(f32[8,1,196608]{2,1,0:T(1,128)} %all-to-all-done, f32[]{:T(128)} %broadcast.1357), dimensions={1}, to_apply=%all_to_all.104.reduce_sub_computation | reduce | bytes 12582916 | tf_op jit(solution)/shard_map/all_to_all | solution.py:201
  696.7 12.3 reshape.743
  730.1 17.0 %all-to-all-done.3 = f32[3,32,256,64]{2,3,0,1:T(8,128)} async-done(((f32[3,32,256,64]{2,3,0,1:T(8,128)}), f32[3,32,256,64]{2,3,0,1:T(8,128)}, u32[]{:S(2)}, u32[]{:S(2)}) %all-to-all-start.3) | async-done | bytes 6291488 | tf_op jit(solution)/shard_map/all_to_all | solution.py:207
  757.7 13.9 fusion.148
  771.6 14.5 %fusion.145 = f32[256,3,8,256]{3,0,2,1:T(8,128)} fusion(f32[3,8,256,256]{2,3,1,0:T(8,128)S(1)} %bitcast.223), kind=kOutput, calls=%fused_computation.203 | convolution fusion | flops 4832821248 | bytes 12582912 | tf_op jit(solution)/shard_map/ckny,nm->ckmy/dot_general | solution.py:62
  786.1 37.1 %all-to-all-done.1 = f32[3,32,256,64]{2,3,0,1:T(8,128)} async-done(((f32[3,32,256,64]{2,3,0,1:T(8,128)}), f32[3,32,256,64]{2,3,0,1:T(8,128)}, u32[]{:S(2)}, u32[]{:S(2)}) %all-to-all-start.1) | async-done | bytes 6291488 | tf_op jit(solution)/shard_map/all_to_all | solution.py:200
  939.6 73.1 %all-to-all-done.4 = f32[2,8,256,256]{3,1,0,2:T(8,128)} async-done(((f32[2,8,256,256]{3,1,0,2:T(8,128)}), f32[2,8,256,256]{3,1,0,2:T(8,128)}, u32[]{:S(2)}, u32[]{:S(2)}) %all-to-all-start.4) | async-done | bytes 4194336 | tf_op jit(solution)/shard_map/all_to_all | solution.py:133
  1045.2 64.2 %all-to-all-done.6 = f32[2,8,256,256]{3,1,0,2:T(8,128)} async-done(((f32[2,8,256,256]{3,1,0,2:T(8,128)}), f32[2,8,256,256]{3,1,0,2:T(8,128)}, u32[]{:S(2)}, u32[]{:S(2)}) %all-to-all-start.6) | async-done | bytes 4194336 | tf_op jit(solution)/shard_map/all_to_all | solution.py:140
  1141.1 22.9 %all-to-all-done.5 = f32[4,1,262144]{2,1,0:T(1,128)} async-done(((f32[4,1,262144]{2,1,0:T(1,128)}), f32[4,1,262144]{2,1,0:T(1,128)}, u32[]{:S(2)}, u32[]{:S(2)}) %all-to-all-start.5) | async-done | bytes 4194336 | tf_op jit(solution)/shard_map/all_to_all | solution.py:132
  1183.4 15.4 %reduce.40 = f32[4,262144]{1,0:T(4,128)} reduce(f32[4,1,262144]{2,1,0:T(1,128)} %all-to-all-done.5, f32[]{:T(128)} %broadcast.1357), dimensions={1}, to_apply=%all_to_all.124.reduce_sub_computation | reduce | bytes 8388612 | tf_op jit(solution)/shard_map/all_to_all | solution.py:132
  1208.1 12.1 copy.222
  1244.9 15.6 %reduce.41 = f32[4,262144]{1,0:T(4,128)} reduce(f32[4,1,262144]{2,1,0:T(1,128)} %all-to-all-done.7, f32[]{:T(128)} %broadcast.1357), dimensions={1}, to_apply=%all_to_all.132.reduce_sub_computation | reduce | bytes 8388612 | tf_op jit(solution)/shard_map/all_to_all | solution.py:139
  1331.3 13.5 collective-permute-done.2
  1362.7 33.2 %fusion.70 = f32[3,32,64,256]{3,2,1,0:T(8,128)} fusion(f32[3,36,66,256]{3,2,1,0:T(8,128)} %get-tuple-element.494, f32[3,36,66,256]{3,2,1,0:T(8,128)} %get-tuple-element.493, f32[3,34,64,256]{3,2,1,0:T(8,128)} %get-tuple-element.511, f32[3,34,64,256]{3,2,1,0:T(8,128)} %get-tuple-element.510, f32[3,32,64,1]{3,2,1,0:T(8,128)} %get-tuple-element.507, ...), kind=kLoop, calls=%fused_computation.107 | loop fusion | flops 33030144 | bytes 88080384 | tf_op jit(solution)/shard_map/add | solution.py:268
  (763 shorter events, 754.0 us)
Async XLA Ops:
  305.5 16.7 %collective-permute-start = (f32[3,3,67,256]{3,2,1,0:T(8,128)S(1)}, f32[3,3,67,256]{3,2,1,0:T(8,128)S(1)}, u32[]{:S(2)}, u32[]{:S(2)}) collective-permute-start(f32[3,3,67,256]{3,2,1,0:T(8,128)S(1)} %slice.487), channel_id=1, source_target_pairs={{28,0},{0,4},{4,8},{8,12},{12,16},{16,20},{20,24},{24,28},{29,1},{... | collective-permute-start | bytes 1852424 | tf_op jit(solution)/shard_map/ppermute | solution.py:20
  338.2 6.5 collective-permute-start.1
  386.4 140.6 %all-to-all-start.2 = ((f32[8,1,196608]{2,1,0:T(1,128)}), f32[8,1,196608]{2,1,0:T(1,128)}, u32[]{:S(2)}, u32[]{:S(2)}) async-start(f32[8,1,196608]{2,1,0:T(1,128)} %reshape.744), calls=%async_computation.2 | async-start | bytes 12582912 | tf_op jit(solution)/shard_map/all_to_all | solution.py:208
  527.0 141.9 %all-to-all-start = ((f32[8,1,196608]{2,1,0:T(1,128)}), f32[8,1,196608]{2,1,0:T(1,128)}, u32[]{:S(2)}, u32[]{:S(2)}) async-start(f32[8,1,196608]{2,1,0:T(1,128)} %reshape.742), calls=%async_computation | async-start | bytes 12582912 | tf_op jit(solution)/shard_map/all_to_all | solution.py:201
  668.9 78.2 %all-to-all-start.3 = ((f32[3,32,256,64]{2,3,0,1:T(8,128)}), f32[3,32,256,64]{2,3,0,1:T(8,128)}, u32[]{:S(2)}, u32[]{:S(2)}) async-start(f32[3,32,256,64]{2,3,0,1:T(8,128)} %copy.151), calls=%async_computation.3 | async-start | bytes 12582912 | tf_op jit(solution)/shard_map/all_to_all | solution.py:207
  747.1 76.1 %all-to-all-start.1 = ((f32[3,32,256,64]{2,3,0,1:T(8,128)}), f32[3,32,256,64]{2,3,0,1:T(8,128)}, u32[]{:S(2)}, u32[]{:S(2)}) async-start(f32[3,32,256,64]{2,3,0,1:T(8,128)} %copy.142), calls=%async_computation.1 | async-start | bytes 12582912 | tf_op jit(solution)/shard_map/all_to_all | solution.py:200
  826.8 22.2 %slice-start.2 = ((s8[6291456]{0:T(1024)(128)(4,1)}), s8[4194304]{0:T(1024)(128)(4,1)S(1)}, s32[]{:S(2)}) async-start(s8[6291456]{0:T(1024)(128)(4,1)} %bitcast.220), calls=%async_computation.10 | async-start | bytes 8388608
  838.1 10.9 slice-start.3
  849.0 15.6 %slice-start = ((s8[6291456]{0:T(1024)(128)(4,1)}), s8[4194304]{0:T(1024)(128)(4,1)S(1)}, s32[]{:S(2)}) async-start(s8[6291456]{0:T(1024)(128)(4,1)} %bitcast.218), calls=%async_computation.8 | async-start | bytes 8388608
  855.3 9.3 slice-start.1
  897.1 9.6 copy-start.11
  915.6 97.1 %all-to-all-start.4 = ((f32[2,8,256,256]{3,1,0,2:T(8,128)}), f32[2,8,256,256]{3,1,0,2:T(8,128)}, u32[]{:S(2)}, u32[]{:S(2)}) async-start(f32[2,8,256,256]{3,1,0,2:T(8,128)} %copy.164), calls=%async_computation.4 | async-start | bytes 8388608 | tf_op jit(solution)/shard_map/all_to_all | solution.py:133
  1012.7 96.6 %all-to-all-start.6 = ((f32[2,8,256,256]{3,1,0,2:T(8,128)}), f32[2,8,256,256]{3,1,0,2:T(8,128)}, u32[]{:S(2)}, u32[]{:S(2)}) async-start(f32[2,8,256,256]{3,1,0,2:T(8,128)} %copy.170), calls=%async_computation.6 | async-start | bytes 8388608 | tf_op jit(solution)/shard_map/all_to_all | solution.py:140
  1109.3 54.6 %all-to-all-start.5 = ((f32[4,1,262144]{2,1,0:T(1,128)}), f32[4,1,262144]{2,1,0:T(1,128)}, u32[]{:S(2)}, u32[]{:S(2)}) async-start(f32[4,1,262144]{2,1,0:T(1,128)} %reshape.746), calls=%async_computation.5 | async-start | bytes 8388608 | tf_op jit(solution)/shard_map/all_to_all | solution.py:132
  1164.0 80.9 %all-to-all-start.7 = ((f32[4,1,262144]{2,1,0:T(1,128)}), f32[4,1,262144]{2,1,0:T(1,128)}, u32[]{:S(2)}, u32[]{:S(2)}) async-start(f32[4,1,262144]{2,1,0:T(1,128)} %reshape.748), calls=%async_computation.7 | async-start | bytes 8388608 | tf_op jit(solution)/shard_map/all_to_all | solution.py:139
  1306.8 20.7 %copy-start = (f32[3,32,64,256]{3,2,1,0:T(8,128)}, f32[3,32,64,256]{3,2,1,0:T(8,128)S(1)}, u32[]{:S(2)}) copy-start(f32[3,32,64,256]{3,2,1,0:T(8,128)S(1)} %pad_maximum_fusion.2) | copy-start | bytes 18874372
  1325.7 19.1 %collective-permute-start.2 = (f32[3,2,64,256]{3,2,1,0:T(8,128)S(1)}, f32[3,2,64,256]{3,2,1,0:T(8,128)S(1)}, u32[]{:S(2)}, u32[]{:S(2)}) collective-permute-start(f32[3,2,64,256]{3,2,1,0:T(8,128)S(1)} %copy-done.21), channel_id=1, source_target_pairs={{4,0},{8,4},{12,8},{16,12},{20,16},{24,20},{28,24},{0,28},{5,1},{9... | collective-permute-start | bytes 1179656 | tf_op jit(solution)/shard_map/ppermute | solution.py:32
  1326.9 18.0 %copy-start.4 = (f32[1,32,64,256]{3,2,1,0:T(8,128)S(1)}, f32[1,32,64,256]{3,2,1,0:T(8,128)}, u32[]{:S(2)}) copy-start(f32[1,32,64,256]{3,2,1,0:T(8,128)} %copy-done.3) | copy-start | bytes 6291460
  1326.9 18.0 %copy-start.6 = (f32[1,32,64,256]{3,2,1,0:T(8,128)S(1)}, f32[1,32,64,256]{3,2,1,0:T(8,128)}, u32[]{:S(2)}) copy-start(f32[1,32,64,256]{3,2,1,0:T(8,128)} %copy-done.5) | copy-start | bytes 6291460
  1326.9 18.0 %copy-start.9 = (f32[1,32,64,256]{3,2,1,0:T(8,128)S(1)}, f32[1,32,64,256]{3,2,1,0:T(8,128)}, u32[]{:S(2)}) copy-start(f32[1,32,64,256]{3,2,1,0:T(8,128)} %copy-done.8) | copy-start | bytes 6291460
  1326.9 17.9 %collective-permute-start.3 = (f32[3,2,64,256]{3,2,1,0:T(8,128)S(1)}, f32[3,2,64,256]{3,2,1,0:T(8,128)S(1)}, u32[]{:S(2)}, u32[]{:S(2)}) collective-permute-start(f32[3,2,64,256]{3,2,1,0:T(8,128)S(1)} %copy-done.20), channel_id=1, source_target_pairs={{0,4},{4,8},{8,12},{12,16},{16,20},{20,24},{24,28},{28,0},{1,5},{5... | collective-permute-start | bytes 1179656 | tf_op jit(solution)/shard_map/ppermute | solution.py:30
  1345.0 8.2 collective-permute-start.4
  1345.9 8.0 collective-permute-start.5
  1352.7 10.0 copy-start.17
  (17 other events, 87.4 us)
where the time goes:
time: 1410 us; the launch traced here: 1400 us
  local copies, waits for them, and re-layouts  417 us (30%)
  waiting for transfers between devices  412 us (29%)
  matrix products  280 us (20%)
  other arithmetic  215 us (15%)
  starting transfers between devices  67.2 us (5%)
    dot_general x32, matrix products, one_plane(): jnp.einsum('cajbs,bsz->bcajz', coefs, weight_z, preferred_element_type=jn...  111 us
    all_to_all x1, waiting for transfers between devices, per_device(): lax.all_to_all(imaginary, 'slab', split_axis=1, concat_axis=2, tiled=True)  97.6 us
    unnamed x64, local copies, waits for them, and re-layouts  95.5 us
    all_to_all x1, waiting for transfers between devices, per_device(): lax.all_to_all(real_part, 'slab', split_axis=1, concat_axis=2, tiled=True)  80 us
    all_to_all x1, waiting for transfers between devices, grid_inverse(): lax.all_to_all(real_part, 'slab', split_axis=2, concat_axis=1, tiled=True)  73.1 us
    dynamic_update_slice x32, other arithmetic, one_plane(): lax.dynamic_update_slice_in_dim(grid_sum, window + plane_sum, plane_index...  71.4 us
    all_to_all x1, waiting for transfers between devices, grid_inverse(): lax.all_to_all(imaginary, 'slab', split_axis=2, concat_axis=1, tiled=True)  64.2 us
    all_to_all x1, waiting for transfers between devices, per_device(): lax.all_to_all(lax.all_to_all(real_part, 'slab', split_axis=1, concat_axi...  37.1 us
  transfers between devices with their start and end apart: 14, of which 11 were waited for; matrix products, arithmetic and copies ran while one was open for 24% of the time, Pallas kernels for 0%

commit v1 on v0

v1 whole, which is shorter than its diff:
```python
import functools
import math

import jax
import jax.numpy as jnp
import numpy as np
from jax import lax
from jax.experimental import pallas as pl
from jax.experimental.pallas import tpu as pltpu
from jax.sharding import PartitionSpec as P

NZ = 256
BLOCK_ROWS = 16
HALF = NZ // 2
STEP = 8
SLOTS_AT_ONCE = 256
MIB = 1024 * 1024
ORDER = (1, 2, 0)
AXES = ("slab", "pen")


def kernel_weight(distance):
    magnitude = jnp.abs(distance)
    inner_part = 1.0 - 2.5 * magnitude * magnitude + 1.5 * magnitude * magnitude * magnitude
    outer_part = 0.5 * (2.0 - magnitude) * (2.0 - magnitude) * (1.0 - magnitude)
    return jnp.where(magnitude < 1.0, inner_part, jnp.where(magnitude < 2.0, outer_part, 0.0))


def vmem(limit=48, **extra):
    return pltpu.CompilerParams(vmem_limit_bytes=limit * MIB, **extra)


def cost(flops, moved):
    return pl.CostEstimate(flops=int(flops), bytes_accessed=int(moved), transcendentals=0)


def two_parts(table):
    table = np.asarray(table, np.float32)
    high = table.astype(jnp.bfloat16)
    low = (table - high.astype(np.float32)).astype(jnp.bfloat16)
    return high, low


def right_table(table):
    high, low = two_parts(table)
    return jnp.asarray(np.concatenate([high, high, low], axis=0))


def left_table(table):
    high, low = two_parts(table)
    return jnp.asarray(np.concatenate([high, high, low], axis=1))


def waves(length):
    index = np.arange(length)
    angle = 2.0 * np.pi / length * (index[:, None] * index[None, :] % length)
    return np.cos(angle), np.sin(angle)


def z_forward_table():
    cosine, sine = waves(NZ)
    real_part, imaginary = cosine[:, :HALF].copy(), -sine[:, :HALF]
    imaginary[:, 0] = cosine[:, HALF]
    return np.concatenate([real_part, imaginary], axis=1)


def z_inverse_table():
    cosine, sine = waves(NZ)
    real_part, imaginary = 2.0 * cosine[:HALF], -2.0 * sine[:HALF]
    real_part[0] = 1.0
    imaginary[0] = cosine[HALF]
    return np.concatenate([real_part, imaginary], axis=0)


def y_forward_table(length, parts):
    cosine, sine = waves(length)
    width = length // parts
    rows = []
    for part in range(parts):
        here = slice(part * width, (part + 1) * width)
        rows.append(np.concatenate([cosine[here], -sine[here]], axis=1))
        rows.append(np.concatenate([sine[here], cosine[here]], axis=1))
    return np.concatenate(rows, axis=0)


def y_inverse_table(length, parts):
    cosine, sine = waves(length)
    width = length // parts
    columns = []
    for part in range(parts):
        here = slice(part * width, (part + 1) * width)
        columns.append(np.concatenate([cosine[:, here], -sine[:, here]], axis=0))
        columns.append(np.concatenate([sine[:, here], cosine[:, here]], axis=0))
    return np.concatenate(columns, axis=1)


def x_table(length, sign):
    cosine, sine = waves(length)
    return np.concatenate(
        [
            np.concatenate([cosine, -sign * sine], axis=1),
            np.concatenate([sign * sine, cosine], axis=1),
        ],
        axis=0,
    )


def split_values(values):
    high = values.astype(jnp.bfloat16)
    low = (values - high.astype(jnp.float32)).astype(jnp.bfloat16)
    return high, low


def times_right(values, table):
    high, low = split_values(values)
    return jnp.dot(
        jnp.concatenate([high, low, high], axis=1), table, preferred_element_type=jnp.float32
    )


def times_left(table, values):
    high, low = split_values(values)
    return jnp.dot(
        table, jnp.concatenate([high, low, high], axis=0), preferred_element_type=jnp.float32
    )


def deposit_kernel(
    counts, row_base, z_base, fractions, strength, grid, ghost_x, ghost_y, ghost_xy, rows
):
    planes, blocks, slots = row_base.shape
    width = min(SLOTS_AT_ONCE, slots)
    rows_local = blocks * BLOCK_ROWS
    ext = BLOCK_ROWS + 8

    def clear(plane, _):
        grid[:, plane] = jnp.zeros((3,) + grid.shape[2:], jnp.float32)
        return 0

    lax.fori_loop(0, planes + 3, clear, 0)
    z_rows = 16
    z_iota = lax.broadcasted_iota(jnp.int32, (z_rows, width), 0)
    j_iota = lax.broadcasted_iota(jnp.int32, (ext, width), 0).astype(jnp.float32)
    z_tiles = [(z_iota + z_rows * t).astype(jnp.float32).astype(jnp.bfloat16) for t in range(NZ // z_rows)]

    def one_plane(plane, _):
        slot = lax.broadcasted_iota(jnp.int32, (blocks, slots), 1)
        group = lax.broadcasted_iota(jnp.int32, (blocks, slots), 0)
        count = jnp.zeros((blocks, slots), jnp.int32)
        for block in range(blocks):
            count = jnp.where(group == block, counts[plane, block], count)
        live = slot < count
        row_cell = row_base[plane].astype(jnp.float32)
        z_cell = z_base[plane]
        for offset in range(4):
            weight_x = kernel_weight(float(offset - 1) - fractions[0, plane])
            for part in range(3):
                rows[part * 4 + offset] = jnp.where(live, strength[part, plane] * weight_x, 0.0)
            rows[12 + offset] = kernel_weight(float(offset - 1) - fractions[1, plane])
            rows[16 + offset] = row_cell + float(offset)
            rows[20 + offset] = kernel_weight(float(offset - 1) - fractions[2, plane])
            rows[24 + offset] = jnp.bitwise_and(z_cell + offset, NZ - 1).astype(jnp.float32)

        def spread(block, first):
            here = slice(first, first + width)

            def row(index):
                return rows[index, block : block + 1, here]

            weight_y = jnp.zeros((ext, width), jnp.float32)
            for offset in range(4):
                weight_y = jnp.where(j_iota == row(16 + offset), row(12 + offset), weight_y)
            coefs = jnp.concatenate([row(index) * weight_y for index in range(12)], axis=0)
            coefs = coefs.astype(jnp.bfloat16)
            z_weight = [
                jnp.broadcast_to(row(20 + offset), (z_rows, width)).astype(jnp.bfloat16)
                for offset in range(4)
            ]
            z_place = [
                jnp.broadcast_to(row(24 + offset), (z_rows, width)).astype(jnp.bfloat16)
                for offset in range(4)
            ]
            tiles = []
            for z_tile in z_tiles:
                tile = jnp.zeros((z_rows, width), jnp.bfloat16)
                for offset in range(4):
                    tile = jnp.where(z_tile == z_place[offset], z_weight[offset], tile)
                tiles.append(tile)
            weight_z = jnp.concatenate(tiles, axis=0)
            result = lax.dot_general(
                coefs, weight_z, (((1,), (1,)), ((), ())), preferred_element_type=jnp.float32
            )
            low = block * BLOCK_ROWS
            for part in range(3):
                for offset in range(4):
                    index = part * 4 + offset
                    grid[part, plane + offset, low : low + ext, :] += result[
                        index * ext : (index + 1) * ext
                    ]

        for block in range(blocks):
            spread(block, 0)
        for first in range(width, slots, width):
            for block in range(blocks):
                pl.when(counts[plane, block] > first)(functools.partial(spread, block, first))
        return 0

    lax.fori_loop(0, planes, one_plane, 0)
    for part in range(3):
        for offset in range(3):
            ghost_x[part, offset] = grid[part, planes + offset, :rows_local, :]
            ghost_xy[part, offset] = grid[part, planes + offset, rows_local : rows_local + 3, :]

    def side(plane, _):
        ghost_y[:, plane] = grid[:, plane, rows_local : rows_local + 3, :]
        return 0

    lax.fori_loop(0, planes, side, 0)


def deposit(counts, row_base, z_base, fractions, strength):
    planes, blocks, slots = row_base.shape
    rows_local = blocks * BLOCK_ROWS
    whole = pl.BlockSpec(memory_space=pltpu.VMEM)
    return pl.pallas_call(
        deposit_kernel,
        out_shape=(
            jax.ShapeDtypeStruct((3, planes + 3, rows_local + 8, NZ), jnp.float32),
            jax.ShapeDtypeStruct((3, 3, rows_local, NZ), jnp.float32),
            jax.ShapeDtypeStruct((3, planes, 3, NZ), jnp.float32),
            jax.ShapeDtypeStruct((3, 3, 3, NZ), jnp.float32),
        ),
        in_specs=[pl.BlockSpec(memory_space=pltpu.SMEM)] + [whole] * 4,
        out_specs=(whole,) * 4,
        scratch_shapes=[
            pltpu.VMEM((28, blocks, slots), jnp.float32),
        ],
        compiler_params=vmem(),
        cost_estimate=cost(2 * planes * blocks * 288 * slots * NZ, 12 * MIB),
        name="deposit",
    )(counts, row_base, z_base, fractions, strength)


def next_over(block, axes):
    counts = [lax.axis_size(axis) for axis in AXES]
    route = []
    for slab in range(counts[0]):
        for pen in range(counts[1]):
            to_slab = (slab + 1) % counts[0] if "slab" in axes else slab
            to_pen = (pen + 1) % counts[1] if "pen" in axes else pen
            route.append((slab * counts[1] + pen, to_slab * counts[1] + to_pen))
    return lax.ppermute(block, AXES, route)


def shifted(block, axis, distance):
    count = lax.axis_size(axis)
    return lax.ppermute(block, axis, [(i, (i + distance) % count) for i in range(count)])


def z_forward_kernel(grid, ghost_x, ghost_y, ghost_xy, table, *refs):
    vorticity, send = refs[-2:]
    rows_local = vorticity.shape[2]
    vorticity[0] = grid[0, :, :rows_local, :]
    vorticity[0, :, 0:3, :] += ghost_y[0]

    @pl.when(pl.program_id(0) == 0)
    def _():
        vorticity[0, 0:3] += ghost_x[0]
        vorticity[0, 0:3, 0:3, :] += ghost_xy[0]

    spectrum = times_right(vorticity[0].reshape(STEP * rows_local, NZ), table[...])
    lines = send.reshape(HALF * STEP, 2 * rows_local)
    for plane in range(STEP):
        here = spectrum[plane * rows_local : (plane + 1) * rows_local]
        stacked = jnp.concatenate([here[:, :HALF], here[:, HALF:]], axis=0)
        lines[pl.ds(plane, HALF, stride=STEP), :] = stacked.T


def z_forward(part, grid, ghosts, vorticity, devices):
    ghost_x, ghost_y, ghost_xy = ghosts
    planes = ghost_y.shape[1]
    rows_local = ghost_x.shape[2]
    depth = HALF // devices
    table = right_table(z_forward_table())
    specs = [
        pl.BlockSpec((1, STEP, rows_local + 8, NZ), lambda i: (part, i, 0, 0)),
        pl.BlockSpec((1, 3, rows_local, NZ), lambda i: (part, 0, 0, 0)),
        pl.BlockSpec((1, STEP, 3, NZ), lambda i: (part, i, 0, 0)),
        pl.BlockSpec((1, 3, 3, NZ), lambda i: (part, 0, 0, 0)),
        pl.BlockSpec(table.shape, lambda i: (0, 0)),
    ]
    operands = [grid, ghost_x, ghost_y, ghost_xy, table]
    aliases = {}
    if vorticity is not None:
        aliases = {len(operands): 0}
        specs.append(pl.BlockSpec(memory_space=pl.ANY))
        operands.append(vorticity)
    return pl.pallas_call(
        z_forward_kernel,
        grid=(planes // STEP,),
        in_specs=specs,
        out_specs=(
            pl.BlockSpec((1, STEP, rows_local, NZ), lambda i: (part, i, 0, 0)),
            pl.BlockSpec((devices, depth, STEP, 2 * rows_local), lambda i: (0, 0, i, 0)),
        ),
        out_shape=(
            jax.ShapeDtypeStruct((3, planes, rows_local, NZ), jnp.float32),
            jax.ShapeDtypeStruct((devices, depth, planes, 2 * rows_local), jnp.float32),
        ),
        input_output_aliases=aliases,
        compiler_params=vmem(),
        cost_estimate=cost(6 * planes * rows_local * NZ * NZ, 3 * planes * rows_local * NZ * 4),
        name="z_forward",
    )(*operands)


def z_inverse_kernel(received, table, velocity, low_x, high_x, low_y, high_y):
    rows_local = velocity.shape[1]
    lines = received.reshape(HALF * STEP, 2 * rows_local)
    pieces = []
    for plane in range(STEP):
        turned = lines[pl.ds(plane, HALF, stride=STEP), :].T
        pieces.append(jnp.concatenate([turned[:rows_local], turned[rows_local:]], axis=1))
    values = times_right(jnp.concatenate(pieces, axis=0), table[...])
    velocity[...] = values.reshape(STEP, rows_local, NZ)
    low_y[...] = velocity[:, 0:2, :]
    high_y[...] = velocity[:, rows_local - 2 : rows_local, :]

    @pl.when(pl.program_id(0) == 0)
    def _():
        low_x[...] = velocity[0:2]

    @pl.when(pl.program_id(0) == pl.num_programs(0) - 1)
    def _():
        high_x[...] = velocity[STEP - 2 : STEP]


def z_inverse(received):
    devices, depth, planes, width = received.shape
    rows_local = width // 2
    table = right_table(z_inverse_table())
    layer = pl.BlockSpec((2, rows_local, NZ), lambda i: (0, 0, 0))
    edge = pl.BlockSpec((STEP, 2, NZ), lambda i: (i, 0, 0))
    return pl.pallas_call(
        z_inverse_kernel,
        grid=(planes // STEP,),
        in_specs=[
            pl.BlockSpec((devices, depth, STEP, width), lambda i: (0, 0, i, 0)),
            pl.BlockSpec(table.shape, lambda i: (0, 0)),
        ],
        out_specs=(
            pl.BlockSpec((STEP, rows_local, NZ), lambda i: (i, 0, 0)),
            layer,
            layer,
            edge,
            edge,
        ),
        out_shape=(
            jax.ShapeDtypeStruct((planes, rows_local, NZ), jnp.float32),
            jax.ShapeDtypeStruct((2, rows_local, NZ), jnp.float32),
            jax.ShapeDtypeStruct((2, rows_local, NZ), jnp.float32),
            jax.ShapeDtypeStruct((planes, 2, NZ), jnp.float32),
            jax.ShapeDtypeStruct((planes, 2, NZ), jnp.float32),
        ),
        compiler_params=vmem(),
        cost_estimate=cost(6 * planes * rows_local * NZ * NZ, 2 * planes * rows_local * NZ * 4),
        name="z_inverse",
    )(received, table)


def plane_forward_kernel(start, received, y_table, x_table_ref, spectrum):
    step = pl.program_id(0)
    depth = pl.num_programs(0) - 1
    has_first = start[0] == 0

    @pl.when(jnp.logical_or(step < depth, has_first))
    def _():
        slabs, pens, _, planes, width = received.shape
        pieces = [received[:, pen, 0].reshape(slabs * planes, width) for pen in range(pens)]
        lane = lax.broadcasted_iota(jnp.int32, (1, width), 1)
        real_side = lane < width // 2
        keep_real = jnp.logical_or(real_side, jnp.logical_not(jnp.logical_and(has_first, step == 0)))
        keep_imaginary = jnp.logical_or(jnp.logical_not(real_side), step < depth)
        keep = jnp.logical_and(keep_real, keep_imaginary).astype(jnp.float32)
        lines = jnp.concatenate([piece * keep for piece in pieces], axis=1)
        along_y = times_right(lines, y_table[...])
        rows_y = along_y.shape[1] // 2
        stacked = jnp.concatenate([along_y[:, :rows_y], along_y[:, rows_y:]], axis=0)
        spectrum[0] = times_left(x_table_ref[...], stacked)


def plane_forward(start, received):
    slabs, pens, depth, planes, width = received.shape
    size_x = slabs * planes
    size_y = pens * (width // 2)
    y_table = right_table(y_forward_table(size_y, pens))
    x_matrix = left_table(x_table(size_x, -1.0))
    return pl.pallas_call(
        plane_forward_kernel,
        grid=(depth + 1,),
        in_specs=[
            pl.BlockSpec(memory_space=pltpu.SMEM),
            pl.BlockSpec(
                (slabs, pens, 1, planes, width), lambda j: (0, 0, jnp.where(j < depth, j, 0), 0, 0)
            ),
            pl.BlockSpec(y_table.shape, lambda j: (0, 0)),
            pl.BlockSpec(x_matrix.shape, lambda j: (0, 0)),
        ],
        out_specs=pl.BlockSpec((1, 2 * size_x, size_y), lambda j: (j, 0, 0)),
        out_shape=jax.ShapeDtypeStruct((depth + 1, 2 * size_x, size_y), jnp.float32),
        compiler_params=vmem(),
        cost_estimate=cost(
            24 * depth * size_x * size_y * (size_x + size_y), 4 * depth * size_x * size_y * 4
        ),
        name="plane_forward",
    )(start, received, y_table, x_matrix)


def wave_pair(shape, dim, length):
    index = lax.broadcasted_iota(jnp.int32, shape, dim)
    signed_index = jnp.where(index < length // 2, index, index - length)
    full_wave = (2.0 * math.pi / length) * signed_index.astype(jnp.float32)
    return full_wave, jnp.where(index == length // 2, 0.0, full_wave)


def plane_inverse_kernel(
    part, start, first, second, first_extra, second_extra, y_table, x_table_ref, back, turned
):
    step = pl.program_id(0)
    size_y = first.shape[2]
    size_x = first.shape[1] // 2
    full_x, curl_x = wave_pair((size_x, 1), 0, size_x)
    full_y, curl_y = wave_pair((1, size_y), 1, size_y)

    def curl(left, right, full_z, curl_z):
        curls = (curl_x, curl_y, curl_z)
        wave_left, wave_right = curls[(part + 1) % 3], curls[(part + 2) % 3]
        wave_squared = full_x * full_x + full_y * full_y + full_z * full_z
        present = wave_squared > 0.0
        scaling = jnp.where(present, 1.0 / jnp.where(present, wave_squared, 1.0), 0.0)
        scaling = scaling * (1.0 / float(size_x * size_y * NZ))
        real_part = wave_left * right[0, :size_x] - wave_right * left[0, :size_x]
        imaginary = wave_left * right[0, size_x:] - wave_right * left[0, size_x:]
        return -imaginary * scaling, real_part * scaling

    index_z = (start[0] + step).astype(jnp.float32)
    wave_z = (2.0 * math.pi / NZ) * index_z
    real_part, imaginary = curl(first, second, wave_z, wave_z)
    turned[:size_x] = real_part
    turned[size_x:] = imaginary

    @pl.when(jnp.logical_and(start[0] == 0, step == 0))
    def _():
        extra_real, extra_imaginary = curl(first_extra, second_extra, -math.pi, 0.0)
        turned[:size_x] += extra_real
        turned[size_x:] += extra_imaginary

    along_x = times_left(x_table_ref[...], turned[...])
    lines = jnp.concatenate([along_x[:size_x], along_x[size_x:]], axis=1)
    result = times_right(lines, y_table[...])
    slabs, pens, _, planes, width = back.shape
    for pen in range(pens):
        back[:, pen, 0] = result[:, pen * width : (pen + 1) * width].reshape(slabs, planes, width)


def plane_inverse(part, start, first, second, shape):
    slabs, pens, depth, planes, width = shape
    size_x = slabs * planes
    size_y = pens * (width // 2)
    y_table = right_table(y_inverse_table(size_y, pens))
    x_matrix = left_table(x_table(size_x, 1.0))
    now = pl.BlockSpec((1, 2 * size_x, size_y), lambda j: (j, 0, 0))
    extra = pl.BlockSpec((1, 2 * size_x, size_y), lambda j: (depth, 0, 0))
    return pl.pallas_call(
        functools.partial(plane_inverse_kernel, part),
        grid=(depth,),
        in_specs=[
            pl.BlockSpec(memory_space=pltpu.SMEM),
            now,
            now,
            extra,
            extra,
            pl.BlockSpec(y_table.shape, lambda j: (0, 0)),
            pl.BlockSpec(x_matrix.shape, lambda j: (0, 0)),
        ],
        out_specs=pl.BlockSpec((slabs, pens, 1, planes, width), lambda j: (0, 0, j, 0, 0)),
        out_shape=jax.ShapeDtypeStruct(shape, jnp.float32),
        scratch_shapes=[pltpu.VMEM((2 * size_x, size_y), jnp.float32)],
        compiler_params=vmem(),
        cost_estimate=cost(
            24 * depth * size_x * size_y * (size_x + size_y), 6 * depth * size_x * size_y * 4
        ),
        name="plane_inverse",
    )(start, first, second, first, second, y_table, x_matrix)


def stretch_kernel(vorticity, field, low_x, high_x, low_y, high_y, *refs):
    velocity, stretching, padded = refs[-3:]
    step = pl.program_id(0)
    planes, rows_local, _ = field.shape

    @pl.when(step == 0)
    def _():
        padded[0:2, 8 : 8 + rows_local, :] = low_x[...]
        padded[planes + 2 : planes + 4, 8 : 8 + rows_local, :] = high_x[...]

        def fill(plane, _):
            padded[plane + 2, 8 : 8 + rows_local, :] = field[plane]
            padded[plane + 2, 6:8, :] = low_y[plane]
            padded[plane + 2, 8 + rows_local : 10 + rows_local, :] = high_y[plane]
            return 0

        lax.fori_loop(0, planes, fill, 0)

    own = slice(8, 8 + rows_local)

    def difference(ahead, behind, ahead_2, behind_2):
        return (2.0 / 3.0) * (ahead - behind) - (1.0 / 12.0) * (ahead_2 - behind_2)

    def one(plane, _):
        at = step * STEP + plane + 2
        here = padded[at, own, :]
        along_x = difference(
            padded[at + 1, own, :], padded[at - 1, own, :], padded[at + 2, own, :], padded[at - 2, own, :]
        )
        along_y = difference(
            *(padded[at, 8 + shift : 8 + shift + rows_local, :] for shift in (1, -1, 2, -2))
        )
        along_z = difference(*(pltpu.roll(here, shift % NZ, 1) for shift in (-1, 1, -2, 2)))
        velocity[0, plane] = here
        stretching[0, plane] = (
            vorticity[0, plane] * along_x + vorticity[1, plane] * along_y + vorticity[2, plane] * along_z
        )
        return 0

    lax.fori_loop(0, STEP, one, 0)


def stretch(part, vorticity, field, halos, outputs):
    planes, rows_local, _ = field.shape
    specs = [
        pl.BlockSpec((3, STEP, rows_local, NZ), lambda i: (0, i, 0, 0)),
        pl.BlockSpec(field.shape, lambda i: (0, 0, 0)),
    ] + [pl.BlockSpec(halo.shape, lambda i: (0, 0, 0)) for halo in halos]
    operands = [vorticity, field, *halos]
    aliases = {}
    if outputs is not None:
        aliases = {len(operands): 0, len(operands) + 1: 1}
        specs += [pl.BlockSpec(memory_space=pl.ANY)] * 2
        operands += list(outputs)
    shape = jax.ShapeDtypeStruct((3, planes, rows_local, NZ), jnp.float32)
    block = pl.BlockSpec((1, STEP, rows_local, NZ), lambda i: (part, i, 0, 0))
    return pl.pallas_call(
        stretch_kernel,
        grid=(planes // STEP,),
        in_specs=specs,
        out_specs=(block, block),
        out_shape=(shape, shape),
        input_output_aliases=aliases,
        scratch_shapes=[pltpu.VMEM((planes + 4, rows_local + 16, NZ), jnp.float32)],
        compiler_params=vmem(),
        cost_estimate=cost(20 * planes * rows_local * NZ, 6 * planes * rows_local * NZ * 4),
        name="stretch",
    )(*operands)


def per_device(counts, row_base, z_base, fractions, strength):
    slabs, pens = lax.axis_size("slab"), lax.axis_size("pen")
    devices = slabs * pens
    depth = HALF // devices
    planes, blocks, _ = row_base.shape
    rows_local = blocks * BLOCK_ROWS
    shape = (slabs, pens, depth, planes, 2 * rows_local)
    place = lax.axis_index("slab") * pens + lax.axis_index("pen")
    start = (place * depth).astype(jnp.int32).reshape(1)

    grid, ghost_x, ghost_y, ghost_xy = deposit(counts, row_base, z_base, fractions, strength)
    ghosts = (
        next_over(ghost_x, ("slab",)),
        next_over(ghost_y, ("pen",)),
        next_over(ghost_xy, ("slab", "pen")),
    )

    def exchange(blocks_out):
        flat = blocks_out.reshape(devices, depth, planes, 2 * rows_local)
        return lax.all_to_all(flat, AXES, 0, 0, tiled=True)

    vorticity = None
    spectra = {}
    for part in ORDER:
        vorticity, send = z_forward(part, grid, ghosts, vorticity, devices)
        spectra[part] = plane_forward(start, exchange(send).reshape(shape))

    outputs = None
    for part in (0, 1, 2):
        back = plane_inverse(part, start, spectra[(part + 1) % 3], spectra[(part + 2) % 3], shape)
        field, low_x, high_x, low_y, high_y = z_inverse(exchange(back))
        halos = (
            shifted(high_x, "slab", 1),
            shifted(low_x, "slab", -1),
            shifted(high_y, "pen", 1),
            shifted(low_y, "pen", -1),
        )
        outputs = stretch(part, vorticity, field, halos, outputs)
    return (vorticity, outputs[0], outputs[1])


def solution(mesh):
    in_specs = (
        P("slab", "pen"),
        P("slab", "pen", None),
        P("slab", "pen", None),
        P(None, "slab", "pen", None),
        P(None, "slab", "pen", None),
    )
    out_specs = (
        P(None, "slab", "pen", None),
        P(None, "slab", "pen", None),
        P(None, "slab", "pen", None),
    )
    return jax.shard_map(
        per_device, mesh=mesh, in_specs=in_specs, out_specs=out_specs, check_vma=False
    )
```

time: 1410 us -> 422 us (0.30)
  local copies, waits for them, and re-layouts: 417 us -> 18.3 us
  matrix products: 280 us -> 0 us
  waiting for transfers between devices: 412 us -> 133 us
  other arithmetic: 215 us -> 0 us
  Pallas kernels: 0 us -> 124 us
  blocking collectives: 0 us -> 104 us
  starting transfers between devices: 67.2 us -> 36.2 us
    dot_general x54 -> x0, matrix products: 280 us -> none  [the longest x32 111 us: one_plane(): jnp.einsum('cajbs,bsz->bcajz', coefs, weight_z, preferred_element_type=jn...]
    all_to_all x8 -> x4, waiting for transfers between devices: 392 us -> 116 us  [exchange(): return lax.all_to_all(flat, AXES, 0, 0, tiled=True)]
    pallas_call x0 -> x16, Pallas kernels: none -> 124 us  [the longest x1 30.5 us: deposit(): pl.pallas_call(deposit_kernel, out_shape=(jax.ShapeDtypeStruct((3, planes...]
    all_to_all x15 -> x0, local copies, waits for them, and re-layouts: 123 us -> none  [the longest x3 21.6 us: per_device(): lax.all_to_all(real_part, 'slab', split_axis=1, concat_axis=2, tiled=True)]
    all_to_all x0 -> x2, blocking collectives: none -> 104 us  [exchange(): return lax.all_to_all(flat, AXES, 0, 0, tiled=True)]
    unnamed x64 -> x45, local copies, waits for them, and re-layouts: 95.5 us -> 18.3 us
    dynamic_update_slice x32 -> x0, other arithmetic: 71.4 us -> none  [one_plane(): lax.dynamic_update_slice_in_dim(grid_sum, window + plane_sum, plane_index...]
    all_to_all x4 -> x0, other arithmetic: 70 us -> none  [the longest x1 19.5 us: per_device(): lax.all_to_all(real_part, 'slab', split_axis=1, concat_axis=2, tiled=True)]
  transfers between devices with their start and end apart: 14 -> 19, of which waited for: 11 -> 6; matrix products, arithmetic and copies ran while one was open for 24% -> 0% of each run, Pallas kernels for 0% -> 17%
where the time goes in v1:
time: 422 us; the launch traced here: 417 us
  waiting for transfers between devices  133 us (32%)
  Pallas kernels  124 us (29%)
  blocking collectives  104 us (25%)
  starting transfers between devices  36.2 us (9%)
  local copies, waits for them, and re-layouts  18.3 us (4%)
    all_to_all x4, waiting for transfers between devices, exchange(): return lax.all_to_all(flat, AXES, 0, 0, tiled=True)  116 us
    all_to_all x2, blocking collectives, exchange(): return lax.all_to_all(flat, AXES, 0, 0, tiled=True)  104 us
    pallas_call x1, Pallas kernels, deposit(): pl.pallas_call(deposit_kernel, out_shape=(jax.ShapeDtypeStruct((3, planes...  30.5 us
    pallas_call x3, Pallas kernels, plane_inverse(): pl.pallas_call(functools.partial(plane_inverse_kernel, part), grid=(depth...  28.1 us
    pallas_call x3, Pallas kernels, stretch(): pl.pallas_call(stretch_kernel, grid=(planes // STEP,), in_specs=specs, ou...  24.6 us
    all_to_all x4, starting transfers between devices, exchange(): return lax.all_to_all(flat, AXES, 0, 0, tiled=True)  22 us
    unnamed x45, local copies, waits for them, and re-layouts  18.3 us
    pallas_call x3, Pallas kernels, plane_forward(): pl.pallas_call(plane_forward_kernel, grid=(depth + 1,), in_specs=[pl.Bloc...  18.1 us
  transfers between devices with their start and end apart: 19, of which 6 were waited for; matrix products, arithmetic and copies ran while one was open for 0% of the time, Pallas kernels for 17%

profile of v1, /device:TPU:17, one launch (start us, length us, event | category | flops | bytes accessed | tf_op | source)
XLA Modules:
  0.0 417.1 jit_solution(14433263254402808810)
XLA Ops:
  5.6 30.5 %deposit.1 = (f32[3,35,72,256]{3,2,1,0:T(8,128)}, f32[3,3,64,256]{3,2,1,0:T(8,128)S(1)}, f32[3,32,3,256]{3,2,1,0:T(4,128)S(1)}, f32[3,3,3,256]{3,2,1,0:T(4,128)S(1)}) custom-call(s32[32,4]{1,0:T(8,128)S(1)} %copy.32.counts, s32[32,4,512]{2,1,0:T(4,128)S(1)} %copy-done.13, s32[32,4,512]{2,1,0:T(4,128)S(1)} %copy-done.14, f32[3,32,4,512]{3,2,1,0:T(4,128)S(1)} %copy-done.11, ...), custom_call_target="tpu_custom_call" | custom-call | flops 9663676416 | bytes 12582912 | tf_op jit(solution)/shard_map/deposit/pallas_call | solution.py:225
  37.5 15.5 %collective-permute-done.2.ghost_xy = f32[3,3,3,256]{3,2,1,0:T(4,128)S(1)} collective-permute-done((f32[3,3,3,256]{3,2,1,0:T(4,128)S(1)}, f32[3,3,3,256]{3,2,1,0:T(4,128)S(1)}, u32[]{:S(2)}, u32[]{:S(2)}) %collective-permute-start.2) | collective-permute-done | bytes 27680 | tf_op jit(solution)/shard_map/ppermute | solution.py:252
  53.0 5.0 %z_forward.3 = (f32[3,32,64,256]{3,2,1,0:T(8,128)}, f32[32,4,32,128]{3,2,1,0:T(8,128)}) custom-call(f32[3,35,72,256]{3,2,1,0:T(8,128)} %get-tuple-element.34.grid, f32[3,3,64,256]{3,2,1,0:T(8,128)S(1)} %collective-permute-done.ghost_x, f32[3,32,3,256]{3,2,1,0:T(4,128)S(1)} %collective-permute-done.1.ghost_y, ...), custom_call_target="tpu_custom_call" | custom-call | flops 805306368 | bytes 6291456 | tf_op jit(solution)/shard_map/z_forward/pallas_call | solution.py:298
  58.0 4.4 %z_forward.4 = (f32[3,32,64,256]{3,2,1,0:T(8,128)}, f32[32,4,32,128]{3,2,1,0:T(8,128)S(1)}) custom-call(f32[3,35,72,256]{3,2,1,0:T(8,128)} %get-tuple-element.34.grid, f32[3,3,64,256]{3,2,1,0:T(8,128)S(1)} %collective-permute-done.ghost_x, f32[3,32,3,256]{3,2,1,0:T(4,128)S(1)} %collective-permute-done.1.ghost_y, ...), custom_call_target="tpu_custom_call", output_to_operand_aliasing={{0}: (5, {})} | custom-call | flops 805306368 | bytes 6291456 | tf_op jit(solution)/shard_map/z_forward/pallas_call | solution.py:298
  62.3 4.4 %z_forward.5 = (f32[3,32,64,256]{3,2,1,0:T(8,128)}, f32[32,4,32,128]{3,2,1,0:T(8,128)S(1)}) custom-call(f32[3,35,72,256]{3,2,1,0:T(8,128)} %get-tuple-element.34.grid, f32[3,3,64,256]{3,2,1,0:T(8,128)S(1)} %collective-permute-done.ghost_x, f32[3,32,3,256]{3,2,1,0:T(4,128)S(1)} %collective-permute-done.1.ghost_y, ...), custom_call_target="tpu_custom_call", output_to_operand_aliasing={{0}: (5, {})} | custom-call | flops 805306368 | bytes 6291456 | tf_op jit(solution)/shard_map/z_forward/pallas_call | solution.py:298
  66.7 51.9 %all_to_all.30 = f32[32,4,32,128]{3,2,1,0:T(8,128)} all-to-all(f32[32,4,32,128]{3,2,1,0:T(8,128)S(1)} %get-tuple-element.41), channel_id=1, replica_groups=mesh['slab'=8,'pen'=4] {'slab','pen'}, dimensions={0} | all-to-all | bytes 4194304 | tf_op jit(solution)/shard_map/all_to_all | solution.py:586
  118.7 52.2 %all_to_all.31 = f32[32,4,32,128]{3,2,1,0:T(8,128)S(1)} all-to-all(f32[32,4,32,128]{3,2,1,0:T(8,128)S(1)} %get-tuple-element.48), channel_id=1, replica_groups=mesh['slab'=8,'pen'=4] {'slab','pen'}, dimensions={0} | all-to-all | bytes 4194304 | tf_op jit(solution)/shard_map/all_to_all | solution.py:586
  170.8 5.0 %all-to-all-start.1 = ((f32[32,4,32,128]{3,2,1,0:T(8,128)}), f32[32,4,32,128]{3,2,1,0:T(8,128)}, u32[]{:S(2)}, u32[]{:S(2)}) async-start(f32[32,4,32,128]{3,2,1,0:T(8,128)} %get-tuple-element.42), calls=%async_computation.1 | async-start | bytes 4194304 | tf_op jit(solution)/shard_map/all_to_all | solution.py:586
  178.6 5.7 %plane_forward.5.first.first_extra.second.second_extra = f32[5,512,256]{2,1,0:T(8,128)} custom-call(s32[1]{0:T(128)} %bitcast.start, f32[8,4,4,32,128]{4,3,2,1,0:T(8,128)S(1)} %bitcast.11, bf16[1536,512]{1,0:T(8,128)(2,1)S(1)} %copy-done.17, bf16[512,1536]{1,0:T(8,128)(2,1)S(1)} %copy-done.15), custom_call_target="tpu_custom_call" | custom-call | flops 3221225472 | bytes 4194304 | tf_op jit(solution)/shard_map/plane_forward/pallas_call | solution.py:398
  184.4 5.7 %plane_forward.3.first.first_extra.second.second_extra = f32[5,512,256]{2,1,0:T(8,128)} custom-call(s32[1]{0:T(128)} %bitcast.start, f32[8,4,4,32,128]{4,3,2,1,0:T(8,128)S(1)} %bitcast.10, bf16[1536,512]{1,0:T(8,128)(2,1)S(1)} %copy-done.17, bf16[512,1536]{1,0:T(8,128)(2,1)S(1)} %copy-done.15), custom_call_target="tpu_custom_call" | custom-call | flops 3221225472 | bytes 4194304 | tf_op jit(solution)/shard_map/plane_forward/pallas_call | solution.py:398
  190.1 9.4 %plane_inverse.4 = f32[8,4,4,32,128]{4,3,2,1,0:T(8,128)S(1)} custom-call(s32[1]{0:T(128)} %bitcast.start, f32[5,512,256]{2,1,0:T(8,128)} %plane_forward.5.first.first_extra.second.second_extra, f32[5,512,256]{2,1,0:T(8,128)} %plane_forward.3.first.first_extra.second.second_extra, f32[5,512,256]{2,1,0:T(8,128)} %plane_forward.5.first.first_extra.second.second_extra, ...), custom_call_target="tpu_custom_call" | custom-call | flops 3221225472 | bytes 6291456 | tf_op jit(solution)/shard_map/plane_inverse/pallas_call | solution.py:474
  200.9 22.2 %all-to-all-done.1 = f32[32,4,32,128]{3,2,1,0:T(8,128)} async-done(((f32[32,4,32,128]{3,2,1,0:T(8,128)}), f32[32,4,32,128]{3,2,1,0:T(8,128)}, u32[]{:S(2)}, u32[]{:S(2)}) %all-to-all-start.1) | async-done | bytes 2097184 | tf_op jit(solution)/shard_map/all_to_all | solution.py:586
  223.1 5.7 %all-to-all-start.4 = ((f32[32,4,32,128]{3,2,1,0:T(8,128)}), f32[32,4,32,128]{3,2,1,0:T(8,128)}, u32[]{:S(2)}, u32[]{:S(2)}) async-start(f32[32,4,32,128]{3,2,1,0:T(8,128)} %bitcast.9), calls=%async_computation.4 | async-start | bytes 4194304 | tf_op jit(solution)/shard_map/all_to_all | solution.py:586
  231.6 6.7 %plane_forward.4.second.second_extra.first.first_extra = f32[5,512,256]{2,1,0:T(8,128)} custom-call(s32[1]{0:T(128)} %bitcast.start, f32[8,4,4,32,128]{4,3,2,1,0:T(8,128)} %bitcast.2.received, bf16[1536,512]{1,0:T(8,128)(2,1)S(1)} %copy-done.18, bf16[512,1536]{1,0:T(8,128)(2,1)S(1)} %copy-done.16), custom_call_target="tpu_custom_call" | custom-call | flops 3221225472 | bytes 4194304 | tf_op jit(solution)/shard_map/plane_forward/pallas_call | solution.py:398
  238.3 9.3 %plane_inverse.5 = f32[8,4,4,32,128]{4,3,2,1,0:T(8,128)S(1)} custom-call(s32[1]{0:T(128)} %bitcast.start, f32[5,512,256]{2,1,0:T(8,128)} %plane_forward.4.second.second_extra.first.first_extra, f32[5,512,256]{2,1,0:T(8,128)} %plane_forward.5.first.first_extra.second.second_extra, f32[5,512,256]{2,1,0:T(8,128)} %plane_forward.4.second.second_extra.first.first_extra, ...), custom_call_target="tpu_custom_call" | custom-call | flops 3221225472 | bytes 6291456 | tf_op jit(solution)/shard_map/plane_inverse/pallas_call | solution.py:474
  249.0 27.1 %all-to-all-done.4.received = f32[32,4,32,128]{3,2,1,0:T(8,128)} async-done(((f32[32,4,32,128]{3,2,1,0:T(8,128)}), f32[32,4,32,128]{3,2,1,0:T(8,128)}, u32[]{:S(2)}, u32[]{:S(2)}) %all-to-all-start.4) | async-done | bytes 2097184 | tf_op jit(solution)/shard_map/all_to_all | solution.py:586
  276.2 5.7 %all-to-all-start.5 = ((f32[32,4,32,128]{3,2,1,0:T(8,128)}), f32[32,4,32,128]{3,2,1,0:T(8,128)}, u32[]{:S(2)}, u32[]{:S(2)}) async-start(f32[32,4,32,128]{3,2,1,0:T(8,128)} %bitcast.8), calls=%async_computation.5 | async-start | bytes 4194304 | tf_op jit(solution)/shard_map/all_to_all | solution.py:586
  281.8 9.4 %plane_inverse.3 = f32[8,4,4,32,128]{4,3,2,1,0:T(8,128)S(1)} custom-call(s32[1]{0:T(128)} %bitcast.start, f32[5,512,256]{2,1,0:T(8,128)} %plane_forward.3.first.first_extra.second.second_extra, f32[5,512,256]{2,1,0:T(8,128)} %plane_forward.4.second.second_extra.first.first_extra, f32[5,512,256]{2,1,0:T(8,128)} %plane_forward.3.first.first_extra.second.second_extra, ...), custom_call_target="tpu_custom_call" | custom-call | flops 3221225472 | bytes 6291456 | tf_op jit(solution)/shard_map/plane_inverse/pallas_call | solution.py:474
  292.6 36.6 %all-to-all-done.5.received = f32[32,4,32,128]{3,2,1,0:T(8,128)} async-done(((f32[32,4,32,128]{3,2,1,0:T(8,128)}), f32[32,4,32,128]{3,2,1,0:T(8,128)}, u32[]{:S(2)}, u32[]{:S(2)}) %all-to-all-start.5) | async-done | bytes 2097184 | tf_op jit(solution)/shard_map/all_to_all | solution.py:586
  329.2 5.6 %all-to-all-start.2 = ((f32[32,4,32,128]{3,2,1,0:T(8,128)}), f32[32,4,32,128]{3,2,1,0:T(8,128)S(1)}, u32[]{:S(2)}, u32[]{:S(2)}) async-start(f32[32,4,32,128]{3,2,1,0:T(8,128)} %bitcast.7), calls=%async_computation.2 | async-start | bytes 4194304 | tf_op jit(solution)/shard_map/all_to_all | solution.py:586
  354.2 30.5 %all-to-all-done.2.received = f32[32,4,32,128]{3,2,1,0:T(8,128)S(1)} async-done(((f32[32,4,32,128]{3,2,1,0:T(8,128)}), f32[32,4,32,128]{3,2,1,0:T(8,128)S(1)}, u32[]{:S(2)}, u32[]{:S(2)}) %all-to-all-start.2) | async-done | bytes 2097184 | tf_op jit(solution)/shard_map/all_to_all | solution.py:586
  392.4 8.3 %stretch.3 = (f32[3,32,64,256]{3,2,1,0:T(8,128)}, f32[3,32,64,256]{3,2,1,0:T(8,128)}) custom-call(f32[3,32,64,256]{3,2,1,0:T(8,128)} %get-tuple-element.31.vorticity, f32[32,64,256]{2,1,0:T(8,128)S(1)} %copy-done.8, f32[2,64,256]{2,1,0:T(8,128)S(1)} %collective-permute-done.11.low_x, f32[2,64,256]{2,1,0:T(8,128)S(1)} %collective-permute-done.12.high_x, ...), custom_call_target="tpu_custom_call" | custom-call | flops 10485760 | bytes 12582912 | tf_op jit(solution)/shard_map/stretch/pallas_call | solution.py:553
  400.7 8.2 %stretch.4 = (f32[3,32,64,256]{3,2,1,0:T(8,128)}, f32[3,32,64,256]{3,2,1,0:T(8,128)}) custom-call(f32[3,32,64,256]{3,2,1,0:T(8,128)} %get-tuple-element.31.vorticity, f32[32,64,256]{2,1,0:T(8,128)S(1)} %copy-done.10, f32[2,64,256]{2,1,0:T(8,128)S(1)} %collective-permute-done.7.low_x, ...), custom_call_target="tpu_custom_call", output_to_operand_aliasing={{0}: (6, {}), {1}: (7, {})} | custom-call | flops 10485760 | bytes 12582912 | tf_op jit(solution)/shard_map/stretch/pallas_call | solution.py:553
  408.9 8.2 %stretch.5 = (f32[3,32,64,256]{3,2,1,0:T(8,128)}, f32[3,32,64,256]{3,2,1,0:T(8,128)}) custom-call(f32[3,32,64,256]{3,2,1,0:T(8,128)} %get-tuple-element.31.vorticity, f32[32,64,256]{2,1,0:T(8,128)S(1)} %get-tuple-element.43.field, f32[2,64,256]{2,1,0:T(8,128)S(1)} %collective-permute-done.3.low_x, ...), custom_call_target="tpu_custom_call", output_to_operand_aliasing={{0}: (6, {}), {1}: (7, {})} | custom-call | flops 10485760 | bytes 12582912 | tf_op jit(solution)/shard_map/stretch/pallas_call | solution.py:553
  (77 shorter events, 43.1 us)
Async XLA Ops:
  5.6 47.4 %copy-start.5 = (bf16[768,256]{1,0:T(8,128)(2,1)S(1)}, bf16[768,256]{1,0:T(8,128)(2,1)}, u32[]{:S(2)}) copy-start(bf16[768,256]{1,0:T(8,128)(2,1)} %constant.23.clone.table) | copy-start | bytes 1179652
  36.1 16.9 %collective-permute-start = (f32[3,3,64,256]{3,2,1,0:T(8,128)S(1)}, f32[3,3,64,256]{3,2,1,0:T(8,128)S(1)}, u32[]{:S(2)}, u32[]{:S(2)}) collective-permute-start(f32[3,3,64,256]{3,2,1,0:T(8,128)S(1)} %get-tuple-element.35), channel_id=1, source_target_pairs={{0,4},{1,5},{2,6},{3,7},{4,8},{5,9},{6,10},{7,11},{8,12},{9,13},{1... | collective-permute-start | bytes 1769480 | tf_op jit(solution)/shard_map/ppermute | solution.py:252
  36.1 16.9 %collective-permute-start.1 = (f32[3,32,3,256]{3,2,1,0:T(4,128)S(1)}, f32[3,32,3,256]{3,2,1,0:T(4,128)S(1)}, u32[]{:S(2)}, u32[]{:S(2)}) collective-permute-start(f32[3,32,3,256]{3,2,1,0:T(4,128)S(1)} %get-tuple-element.36), channel_id=1, source_target_pairs={{0,1},{1,2},{2,3},{3,0},{4,5},{5,6},{6,7},{7,4},{8,9},{9,10},{10,1... | collective-permute-start | bytes 884744 | tf_op jit(solution)/shard_map/ppermute | solution.py:252
  37.3 15.7 %collective-permute-start.2 = (f32[3,3,3,256]{3,2,1,0:T(4,128)S(1)}, f32[3,3,3,256]{3,2,1,0:T(4,128)S(1)}, u32[]{:S(2)}, u32[]{:S(2)}) collective-permute-start(f32[3,3,3,256]{3,2,1,0:T(4,128)S(1)} %get-tuple-element.37), channel_id=1, source_target_pairs={{0,5},{1,6},{2,7},{3,4},{4,9},{5,10},{6,11},{7,8},{8,13},{9,14},{1... | collective-permute-start | bytes 82952 | tf_op jit(solution)/shard_map/ppermute | solution.py:252
  170.8 52.3 %all-to-all-start.1 = ((f32[32,4,32,128]{3,2,1,0:T(8,128)}), f32[32,4,32,128]{3,2,1,0:T(8,128)}, u32[]{:S(2)}, u32[]{:S(2)}) async-start(f32[32,4,32,128]{3,2,1,0:T(8,128)} %get-tuple-element.42), calls=%async_computation.1 | async-start | bytes 4194304 | tf_op jit(solution)/shard_map/all_to_all | solution.py:586
  178.6 5.7 %copy-start.6 = (f32[32,4,32,128]{3,2,1,0:T(8,128)S(1)}, f32[32,4,32,128]{3,2,1,0:T(8,128)}, u32[]{:S(2)}) copy-start(f32[32,4,32,128]{3,2,1,0:T(8,128)} %all_to_all.30) | copy-start | bytes 6291460
  223.1 53.0 %all-to-all-start.4 = ((f32[32,4,32,128]{3,2,1,0:T(8,128)}), f32[32,4,32,128]{3,2,1,0:T(8,128)}, u32[]{:S(2)}, u32[]{:S(2)}) async-start(f32[32,4,32,128]{3,2,1,0:T(8,128)} %bitcast.9), calls=%async_computation.4 | async-start | bytes 4194304 | tf_op jit(solution)/shard_map/all_to_all | solution.py:586
  276.2 53.0 %all-to-all-start.5 = ((f32[32,4,32,128]{3,2,1,0:T(8,128)}), f32[32,4,32,128]{3,2,1,0:T(8,128)}, u32[]{:S(2)}, u32[]{:S(2)}) async-start(f32[32,4,32,128]{3,2,1,0:T(8,128)} %bitcast.8), calls=%async_computation.5 | async-start | bytes 4194304 | tf_op jit(solution)/shard_map/all_to_all | solution.py:586
  329.2 55.5 %all-to-all-start.2 = ((f32[32,4,32,128]{3,2,1,0:T(8,128)}), f32[32,4,32,128]{3,2,1,0:T(8,128)S(1)}, u32[]{:S(2)}, u32[]{:S(2)}) async-start(f32[32,4,32,128]{3,2,1,0:T(8,128)} %bitcast.7), calls=%async_computation.2 | async-start | bytes 4194304 | tf_op jit(solution)/shard_map/all_to_all | solution.py:586
  334.8 6.4 %copy-start.20 = (bf16[768,256]{1,0:T(8,128)(2,1)S(1)}, bf16[768,256]{1,0:T(8,128)(2,1)}, u32[]{:S(2)}) copy-start(bf16[768,256]{1,0:T(8,128)(2,1)} %constant.28.clone.table) | copy-start | bytes 1179652
  339.8 10.5 %collective-permute-start.13 = (f32[32,2,256]{2,1,0:T(2,128)S(1)}, f32[32,2,256]{2,1,0:T(2,128)S(1)}, u32[]{:S(2)}, u32[]{:S(2)}) collective-permute-start(f32[32,2,256]{2,1,0:T(2,128)S(1)} %get-tuple-element.57), channel_id=1, source_target_pairs={{0,1},{1,2},{2,3},{3,0},{4,5},{5,6},{6,7},{7,4},{8,9},{9,10},{10,1... | collective-permute-start | bytes 196616 | tf_op jit(solution)/shard_map/ppermute | solution.py:257
  341.2 10.6 %collective-permute-start.14 = (f32[32,2,256]{2,1,0:T(2,128)S(1)}, f32[32,2,256]{2,1,0:T(2,128)S(1)}, u32[]{:S(2)}, u32[]{:S(2)}) collective-permute-start(f32[32,2,256]{2,1,0:T(2,128)S(1)} %get-tuple-element.58), channel_id=1, source_target_pairs={{0,3},{1,0},{2,1},{3,2},{4,7},{5,4},{6,5},{7,6},{8,11},{9,8},{10,9... | collective-permute-start | bytes 196616 | tf_op jit(solution)/shard_map/ppermute | solution.py:257
  346.1 7.5 %collective-permute-start.9 = (f32[32,2,256]{2,1,0:T(2,128)S(1)}, f32[32,2,256]{2,1,0:T(2,128)S(1)}, u32[]{:S(2)}, u32[]{:S(2)}) collective-permute-start(f32[32,2,256]{2,1,0:T(2,128)S(1)} %get-tuple-element.52), channel_id=1, source_target_pairs={{0,1},{1,2},{2,3},{3,0},{4,5},{5,6},{6,7},{7,4},{8,9},{9,10},{10,1... | collective-permute-start | bytes 196616 | tf_op jit(solution)/shard_map/ppermute | solution.py:257
  347.9 42.2 %collective-permute-start.11 = (f32[2,64,256]{2,1,0:T(8,128)S(1)}, f32[2,64,256]{2,1,0:T(8,128)S(1)}, u32[]{:S(2)}, u32[]{:S(2)}) collective-permute-start(f32[2,64,256]{2,1,0:T(8,128)S(1)} %get-tuple-element.55), channel_id=1, source_target_pairs={{0,4},{4,8},{8,12},{12,16},{16,20},{20,24},{24,28},{28,0},{1,5},{5... | collective-permute-start | bytes 393224 | tf_op jit(solution)/shard_map/ppermute | solution.py:257
  349.1 41.3 %collective-permute-start.12 = (f32[2,64,256]{2,1,0:T(8,128)S(1)}, f32[2,64,256]{2,1,0:T(8,128)S(1)}, u32[]{:S(2)}, u32[]{:S(2)}) collective-permute-start(f32[2,64,256]{2,1,0:T(8,128)S(1)} %get-tuple-element.56), channel_id=1, source_target_pairs={{0,28},{4,0},{8,4},{12,8},{16,12},{20,16},{24,20},{28,24},{1,29},{... | collective-permute-start | bytes 393224 | tf_op jit(solution)/shard_map/ppermute | solution.py:257
  350.2 37.7 %collective-permute-start.10 = (f32[32,2,256]{2,1,0:T(2,128)S(1)}, f32[32,2,256]{2,1,0:T(2,128)S(1)}, u32[]{:S(2)}, u32[]{:S(2)}) collective-permute-start(f32[32,2,256]{2,1,0:T(2,128)S(1)} %get-tuple-element.53), channel_id=1, source_target_pairs={{0,3},{1,0},{2,1},{3,2},{4,7},{5,4},{6,5},{7,6},{8,11},{9,8},{10,9... | collective-permute-start | bytes 196616 | tf_op jit(solution)/shard_map/ppermute | solution.py:257
  351.9 40.5 %collective-permute-start.7 = (f32[2,64,256]{2,1,0:T(8,128)S(1)}, f32[2,64,256]{2,1,0:T(8,128)S(1)}, u32[]{:S(2)}, u32[]{:S(2)}) collective-permute-start(f32[2,64,256]{2,1,0:T(8,128)S(1)} %get-tuple-element.50), channel_id=1, source_target_pairs={{0,4},{4,8},{8,12},{12,16},{16,20},{20,24},{24,28},{28,0},{1,5},{5... | collective-permute-start | bytes 393224 | tf_op jit(solution)/shard_map/ppermute | solution.py:257
  353.6 47.1 %collective-permute-start.8 = (f32[2,64,256]{2,1,0:T(8,128)S(1)}, f32[2,64,256]{2,1,0:T(8,128)S(1)}, u32[]{:S(2)}, u32[]{:S(2)}) collective-permute-start(f32[2,64,256]{2,1,0:T(8,128)S(1)} %get-tuple-element.51), channel_id=1, source_target_pairs={{0,28},{4,0},{8,4},{12,8},{16,12},{20,16},{24,20},{28,24},{1,29},{... | collective-permute-start | bytes 393224 | tf_op jit(solution)/shard_map/ppermute | solution.py:257
  385.7 6.7 %copy-start.8 = (f32[32,64,256]{2,1,0:T(8,128)S(1)}, f32[32,64,256]{2,1,0:T(8,128)}, u32[]{:S(2)}) copy-start(f32[32,64,256]{2,1,0:T(8,128)} %copy-done.7) | copy-start | bytes 6291460
  387.9 21.0 %collective-permute-start.3 = (f32[2,64,256]{2,1,0:T(8,128)S(1)}, f32[2,64,256]{2,1,0:T(8,128)S(1)}, u32[]{:S(2)}, u32[]{:S(2)}) collective-permute-start(f32[2,64,256]{2,1,0:T(8,128)S(1)} %get-tuple-element.44), channel_id=1, source_target_pairs={{0,4},{4,8},{8,12},{12,16},{16,20},{20,24},{24,28},{28,0},{1,5},{5... | collective-permute-start | bytes 393224 | tf_op jit(solution)/shard_map/ppermute | solution.py:257
  390.1 18.8 %collective-permute-start.4 = (f32[2,64,256]{2,1,0:T(8,128)S(1)}, f32[2,64,256]{2,1,0:T(8,128)S(1)}, u32[]{:S(2)}, u32[]{:S(2)}) collective-permute-start(f32[2,64,256]{2,1,0:T(8,128)S(1)} %get-tuple-element.45), channel_id=1, source_target_pairs={{0,28},{4,0},{8,4},{12,8},{16,12},{20,16},{24,20},{28,24},{1,29},{... | collective-permute-start | bytes 393224 | tf_op jit(solution)/shard_map/ppermute | solution.py:257
  390.4 18.5 %collective-permute-start.5 = (f32[32,2,256]{2,1,0:T(2,128)S(1)}, f32[32,2,256]{2,1,0:T(2,128)S(1)}, u32[]{:S(2)}, u32[]{:S(2)}) collective-permute-start(f32[32,2,256]{2,1,0:T(2,128)S(1)} %get-tuple-element.46), channel_id=1, source_target_pairs={{0,1},{1,2},{2,3},{3,0},{4,5},{5,6},{6,7},{7,4},{8,9},{9,10},{10,1... | collective-permute-start | bytes 196616 | tf_op jit(solution)/shard_map/ppermute | solution.py:257
  392.4 16.5 %collective-permute-start.6 = (f32[32,2,256]{2,1,0:T(2,128)S(1)}, f32[32,2,256]{2,1,0:T(2,128)S(1)}, u32[]{:S(2)}, u32[]{:S(2)}) collective-permute-start(f32[32,2,256]{2,1,0:T(2,128)S(1)} %get-tuple-element.47), channel_id=1, source_target_pairs={{0,3},{1,0},{2,1},{3,2},{4,7},{5,4},{6,5},{7,6},{8,11},{9,8},{10,9... | collective-permute-start | bytes 196616 | tf_op jit(solution)/shard_map/ppermute | solution.py:257
  392.4 8.3 %copy-start.10 = (f32[32,64,256]{2,1,0:T(8,128)S(1)}, f32[32,64,256]{2,1,0:T(8,128)}, u32[]{:S(2)}) copy-start(f32[32,64,256]{2,1,0:T(8,128)} %copy-done.9) | copy-start | bytes 6291460
  (17 other events, 34.7 us)

commit v2 on v1

v2 whole, which is shorter than its diff:
```python
import functools
import math

import jax
import jax.numpy as jnp
import numpy as np
from jax import lax
from jax.experimental import pallas as pl
from jax.experimental.pallas import tpu as pltpu
from jax.sharding import PartitionSpec as P

NZ = 256
BLOCK_ROWS = 16
HALF = NZ // 2
STEP = 8
SLOTS_AT_ONCE = 256
MIB = 1024 * 1024
FORWARD = ((1, 2), (0,))
BACKWARD = ((0,), (1, 2))
AXES = ("slab", "pen")


def kernel_weight(distance):
    magnitude = jnp.abs(distance)
    inner_part = 1.0 - 2.5 * magnitude * magnitude + 1.5 * magnitude * magnitude * magnitude
    outer_part = 0.5 * (2.0 - magnitude) * (2.0 - magnitude) * (1.0 - magnitude)
    return jnp.where(magnitude < 1.0, inner_part, jnp.where(magnitude < 2.0, outer_part, 0.0))


def vmem(limit=48, **extra):
    return pltpu.CompilerParams(vmem_limit_bytes=limit * MIB, **extra)


def cost(flops, moved):
    return pl.CostEstimate(flops=int(flops), bytes_accessed=int(moved), transcendentals=0)


def two_parts(table):
    table = np.asarray(table, np.float32)
    high = table.astype(jnp.bfloat16)
    low = (table - high.astype(np.float32)).astype(jnp.bfloat16)
    return high, low


def right_table(table):
    high, low = two_parts(table)
    return jnp.asarray(np.concatenate([high, high, low], axis=0))


def left_table(table):
    high, low = two_parts(table)
    return jnp.asarray(np.concatenate([high, high, low], axis=1))


def waves(length):
    index = np.arange(length)
    angle = 2.0 * np.pi / length * (index[:, None] * index[None, :] % length)
    return np.cos(angle), np.sin(angle)


def z_forward_table():
    cosine, sine = waves(NZ)
    real_part, imaginary = cosine[:, :HALF].copy(), -sine[:, :HALF]
    imaginary[:, 0] = cosine[:, HALF]
    return np.concatenate([real_part, imaginary], axis=1)


def z_inverse_table():
    cosine, sine = waves(NZ)
    real_part, imaginary = 2.0 * cosine[:HALF], -2.0 * sine[:HALF]
    real_part[0] = 1.0
    imaginary[0] = cosine[HALF]
    return np.concatenate([real_part, imaginary], axis=0)


def y_forward_table(length, parts):
    cosine, sine = waves(length)
    width = length // parts
    rows = []
    for part in range(parts):
        here = slice(part * width, (part + 1) * width)
        rows.append(np.concatenate([cosine[here], -sine[here]], axis=1))
        rows.append(np.concatenate([sine[here], cosine[here]], axis=1))
    return np.concatenate(rows, axis=0)


def y_inverse_table(length, parts):
    cosine, sine = waves(length)
    width = length // parts
    columns = []
    for part in range(parts):
        here = slice(part * width, (part + 1) * width)
        columns.append(np.concatenate([cosine[:, here], -sine[:, here]], axis=0))
        columns.append(np.concatenate([sine[:, here], cosine[:, here]], axis=0))
    return np.concatenate(columns, axis=1)


def x_table(length, sign):
    cosine, sine = waves(length)
    return np.concatenate(
        [
            np.concatenate([cosine, -sign * sine], axis=1),
            np.concatenate([sign * sine, cosine], axis=1),
        ],
        axis=0,
    )


def split_values(values):
    high = values.astype(jnp.bfloat16)
    low = (values - high.astype(jnp.float32)).astype(jnp.bfloat16)
    return high, low


def times_right(values, table):
    high, low = split_values(values)
    return jnp.dot(
        jnp.concatenate([high, low, high], axis=1), table, preferred_element_type=jnp.float32
    )


def times_left(table, values):
    high, low = split_values(values)
    return jnp.dot(
        table, jnp.concatenate([high, low, high], axis=0), preferred_element_type=jnp.float32
    )


def deposit_plan(edges, planes, blocks):
    edge_planes = range(planes - 3, planes)
    if edges:
        return ((0, planes - 3, (blocks - 1,)), (edge_planes[0], planes, tuple(range(blocks))))
    return ((0, planes - 3, tuple(range(blocks - 1))),)


def deposit_kernel(edges, counts, row_base, z_base, fractions, strength, *refs):
    planes, blocks, slots = row_base.shape
    width = min(SLOTS_AT_ONCE, slots)
    rows_local = blocks * BLOCK_ROWS
    ext = BLOCK_ROWS + 8
    if edges:
        grid, ghost_x, ghost_y, ghost_xy, rows = refs
    else:
        begun, grid, rows = refs

    def clear(plane, _):
        if edges:
            grid[:, plane] = jnp.zeros((3,) + grid.shape[2:], jnp.float32)
        else:
            grid[:, plane] = begun[:, plane]
        return 0

    lax.fori_loop(0, grid.shape[1], clear, 0)
    z_rows = 16
    z_iota = lax.broadcasted_iota(jnp.int32, (z_rows, width), 0)
    j_iota = lax.broadcasted_iota(jnp.int32, (ext, width), 0).astype(jnp.float32)
    z_tiles = [
        (z_iota + z_rows * t).astype(jnp.float32).astype(jnp.bfloat16) for t in range(NZ // z_rows)
    ]

    def one_plane(here_blocks, plane, _):
        slot = lax.broadcasted_iota(jnp.int32, (blocks, slots), 1)
        group = lax.broadcasted_iota(jnp.int32, (blocks, slots), 0)
        count = jnp.zeros((blocks, slots), jnp.int32)
        for block in here_blocks:
            count = jnp.where(group == block, counts[plane, block], count)
        live = slot < count
        row_cell = row_base[plane].astype(jnp.float32)
        z_cell = z_base[plane]
        for offset in range(4):
            weight_x = kernel_weight(float(offset - 1) - fractions[0, plane])
            for part in range(3):
                rows[part * 4 + offset] = jnp.where(live, strength[part, plane] * weight_x, 0.0)
            rows[12 + offset] = kernel_weight(float(offset - 1) - fractions[1, plane])
            rows[16 + offset] = row_cell + float(offset)
            rows[20 + offset] = kernel_weight(float(offset - 1) - fractions[2, plane])
            rows[24 + offset] = jnp.bitwise_and(z_cell + offset, NZ - 1).astype(jnp.float32)

        def spread(block, first):
            here = slice(first, first + width)

            def row(index):
                return rows[index, block : block + 1, here]

            weight_y = jnp.zeros((ext, width), jnp.float32)
            for offset in range(4):
                weight_y = jnp.where(j_iota == row(16 + offset), row(12 + offset), weight_y)
            coefs = jnp.concatenate([row(index) * weight_y for index in range(12)], axis=0)
            coefs = coefs.astype(jnp.bfloat16)
            z_weight = [
                jnp.broadcast_to(row(20 + offset), (z_rows, width)).astype(jnp.bfloat16)
                for offset in range(4)
            ]
            z_place = [
                jnp.broadcast_to(row(24 + offset), (z_rows, width)).astype(jnp.bfloat16)
                for offset in range(4)
            ]
            tiles = []
            for z_tile in z_tiles:
                tile = jnp.zeros((z_rows, width), jnp.bfloat16)
                for offset in range(4):
                    tile = jnp.where(z_tile == z_place[offset], z_weight[offset], tile)
                tiles.append(tile)
            weight_z = jnp.concatenate(tiles, axis=0)
            result = lax.dot_general(
                coefs, weight_z, (((1,), (1,)), ((), ())), preferred_element_type=jnp.float32
            )
            low = block * BLOCK_ROWS
            for part in range(3):
                for offset in range(4):
                    index = part * 4 + offset
                    grid[part, plane + offset, low : low + ext, :] += result[
                        index * ext : (index + 1) * ext
                    ]

        for block in here_blocks:
            spread(block, 0)
        for first in range(width, slots, width):
            for block in here_blocks:
                pl.when(counts[plane, block] > first)(functools.partial(spread, block, first))
        return 0

    for begin, end, here_blocks in deposit_plan(edges, planes, blocks):
        if here_blocks:
            lax.fori_loop(begin, end, functools.partial(one_plane, here_blocks), 0)
    if not edges:
        return
    for part in range(3):
        for offset in range(3):
            ghost_x[part, offset] = grid[part, planes + offset, :rows_local, :]
            ghost_xy[part, offset] = grid[part, planes + offset, rows_local : rows_local + 3, :]

    def side(plane, _):
        ghost_y[:, plane] = grid[:, plane, rows_local : rows_local + 3, :]
        return 0

    lax.fori_loop(0, planes, side, 0)


def deposit(particles, begun):
    edges = begun is None
    planes, blocks, slots = particles[1].shape
    rows_local = blocks * BLOCK_ROWS
    whole = pl.BlockSpec(memory_space=pltpu.VMEM)
    grid_shape = (3, planes + 3, rows_local + 8, NZ)
    shapes = [grid_shape]
    if edges:
        shapes += [(3, 3, rows_local, NZ), (3, planes, 3, NZ), (3, 3, 3, NZ)]
    groups = sum((end - begin) * len(here) for begin, end, here in deposit_plan(edges, planes, blocks))
    operands = list(particles) + ([] if edges else [begun])
    return pl.pallas_call(
        functools.partial(deposit_kernel, edges),
        out_shape=[jax.ShapeDtypeStruct(shape, jnp.float32) for shape in shapes],
        in_specs=[pl.BlockSpec(memory_space=pltpu.SMEM)] + [whole] * (len(operands) - 1),
        out_specs=[whole] * len(shapes),
        scratch_shapes=[pltpu.VMEM((28, blocks, slots), jnp.float32)],
        compiler_params=vmem(),
        cost_estimate=cost(10 * groups * 288 * slots * NZ, 12 * MIB),
        name="deposit_edges" if edges else "deposit_rest",
    )(*operands)


def next_over(block, axes):
    counts = [lax.axis_size(axis) for axis in AXES]
    route = []
    for slab in range(counts[0]):
        for pen in range(counts[1]):
            to_slab = (slab + 1) % counts[0] if "slab" in axes else slab
            to_pen = (pen + 1) % counts[1] if "pen" in axes else pen
            route.append((slab * counts[1] + pen, to_slab * counts[1] + to_pen))
    return lax.ppermute(block, AXES, route)


def shifted(block, axis, distance):
    count = lax.axis_size(axis)
    return lax.ppermute(block, axis, [(i, (i + distance) % count) for i in range(count)])


def z_forward_kernel(grid, ghost_x, ghost_y, ghost_xy, table, *refs):
    vorticity, send = refs[-2:]
    rows_local = vorticity.shape[2]
    vorticity[0] = grid[0, :, :rows_local, :]
    vorticity[0, :, 0:3, :] += ghost_y[0]

    @pl.when(pl.program_id(1) == 0)
    def _():
        vorticity[0, 0:3] += ghost_x[0]
        vorticity[0, 0:3, 0:3, :] += ghost_xy[0]

    spectrum = times_right(vorticity[0].reshape(STEP * rows_local, NZ), table[...])
    lines = send.reshape(HALF * STEP, 2 * rows_local)
    for plane in range(STEP):
        here = spectrum[plane * rows_local : (plane + 1) * rows_local]
        stacked = jnp.concatenate([here[:, :HALF], here[:, HALF:]], axis=0)
        lines[pl.ds(plane, HALF, stride=STEP), :] = stacked.T


def z_forward(parts, grid, ghosts, vorticity, devices):
    ghost_x, ghost_y, ghost_xy = ghosts
    planes = ghost_y.shape[1]
    rows_local = ghost_x.shape[2]
    depth = HALF // devices
    count = len(parts)
    part = parts[0]
    table = right_table(z_forward_table())
    specs = [
        pl.BlockSpec((1, STEP, rows_local + 8, NZ), lambda c, i: (part + c, i, 0, 0)),
        pl.BlockSpec((1, 3, rows_local, NZ), lambda c, i: (part + c, 0, 0, 0)),
        pl.BlockSpec((1, STEP, 3, NZ), lambda c, i: (part + c, i, 0, 0)),
        pl.BlockSpec((1, 3, 3, NZ), lambda c, i: (part + c, 0, 0, 0)),
        pl.BlockSpec(table.shape, lambda c, i: (0, 0)),
    ]
    operands = [grid, ghost_x, ghost_y, ghost_xy, table]
    aliases = {}
    if vorticity is not None:
        aliases = {len(operands): 0}
        specs.append(pl.BlockSpec(memory_space=pl.ANY))
        operands.append(vorticity)
    return pl.pallas_call(
        z_forward_kernel,
        grid=(count, planes // STEP),
        in_specs=specs,
        out_specs=(
            pl.BlockSpec((1, STEP, rows_local, NZ), lambda c, i: (part + c, i, 0, 0)),
            pl.BlockSpec((devices, None, depth, STEP, 2 * rows_local), lambda c, i: (0, c, 0, i, 0)),
        ),
        out_shape=(
            jax.ShapeDtypeStruct((3, planes, rows_local, NZ), jnp.float32),
            jax.ShapeDtypeStruct((devices, count, depth, planes, 2 * rows_local), jnp.float32),
        ),
        input_output_aliases=aliases,
        compiler_params=vmem(),
        cost_estimate=cost(
            6 * count * planes * rows_local * NZ * NZ, 3 * count * planes * rows_local * NZ * 4
        ),
        name="z_forward",
    )(*operands)


def z_inverse_kernel(received, table, *refs):
    velocity, low_x, high_x, low_y, high_y = refs[-5:]
    rows_local = velocity.shape[2]
    lines = received.reshape(HALF * STEP, 2 * rows_local)
    pieces = []
    for plane in range(STEP):
        turned = lines[pl.ds(plane, HALF, stride=STEP), :].T
        pieces.append(jnp.concatenate([turned[:rows_local], turned[rows_local:]], axis=1))
    values = times_right(jnp.concatenate(pieces, axis=0), table[...])
    velocity[0] = values.reshape(STEP, rows_local, NZ)
    low_y[0] = velocity[0, :, 0:2, :]
    high_y[0] = velocity[0, :, rows_local - 2 : rows_local, :]

    @pl.when(pl.program_id(1) == 0)
    def _():
        low_x[0] = velocity[0, 0:2]

    @pl.when(pl.program_id(1) == pl.num_programs(1) - 1)
    def _():
        high_x[0] = velocity[0, STEP - 2 : STEP]


def z_inverse(parts, received, velocity):
    devices, count, depth, planes, width = received.shape
    rows_local = width // 2
    part = parts[0]
    table = right_table(z_inverse_table())
    layer = pl.BlockSpec((1, 2, rows_local, NZ), lambda c, i: (c, 0, 0, 0))
    edge = pl.BlockSpec((1, STEP, 2, NZ), lambda c, i: (c, i, 0, 0))
    specs = [
        pl.BlockSpec((devices, None, depth, STEP, width), lambda c, i: (0, c, 0, i, 0)),
        pl.BlockSpec(table.shape, lambda c, i: (0, 0)),
    ]
    operands = [received, table]
    aliases = {}
    if velocity is not None:
        aliases = {len(operands): 0}
        specs.append(pl.BlockSpec(memory_space=pl.ANY))
        operands.append(velocity)
    return pl.pallas_call(
        z_inverse_kernel,
        grid=(count, planes // STEP),
        in_specs=specs,
        out_specs=(
            pl.BlockSpec((1, STEP, rows_local, NZ), lambda c, i: (part + c, i, 0, 0)),
            layer,
            layer,
            edge,
            edge,
        ),
        out_shape=(
            jax.ShapeDtypeStruct((3, planes, rows_local, NZ), jnp.float32),
            jax.ShapeDtypeStruct((count, 2, rows_local, NZ), jnp.float32),
            jax.ShapeDtypeStruct((count, 2, rows_local, NZ), jnp.float32),
            jax.ShapeDtypeStruct((count, planes, 2, NZ), jnp.float32),
            jax.ShapeDtypeStruct((count, planes, 2, NZ), jnp.float32),
        ),
        input_output_aliases=aliases,
        compiler_params=vmem(),
        cost_estimate=cost(
            6 * count * planes * rows_local * NZ * NZ, 2 * count * planes * rows_local * NZ * 4
        ),
        name="z_inverse",
    )(*operands)


def plane_forward_kernel(start, received, y_table, x_table_ref, spectrum):
    step = pl.program_id(1)
    depth = pl.num_programs(1) - 1
    has_first = start[0] == 0

    @pl.when(jnp.logical_or(step < depth, has_first))
    def _():
        slabs, pens, planes, width = received.shape
        pieces = [received[:, pen].reshape(slabs * planes, width) for pen in range(pens)]
        lane = lax.broadcasted_iota(jnp.int32, (1, width), 1)
        real_side = lane < width // 2
        keep_real = jnp.logical_or(real_side, jnp.logical_not(jnp.logical_and(has_first, step == 0)))
        keep_imaginary = jnp.logical_or(jnp.logical_not(real_side), step < depth)
        keep = jnp.logical_and(keep_real, keep_imaginary).astype(jnp.float32)
        lines = jnp.concatenate([piece * keep for piece in pieces], axis=1)
        along_y = times_right(lines, y_table[...])
        rows_y = along_y.shape[1] // 2
        stacked = jnp.concatenate([along_y[:, :rows_y], along_y[:, rows_y:]], axis=0)
        spectrum[...] = times_left(x_table_ref[...], stacked)


def plane_forward(start, received):
    slabs, pens, count, depth, planes, width = received.shape
    size_x = slabs * planes
    size_y = pens * (width // 2)
    y_table = right_table(y_forward_table(size_y, pens))
    x_matrix = left_table(x_table(size_x, -1.0))
    return pl.pallas_call(
        plane_forward_kernel,
        grid=(count, depth + 1),
        in_specs=[
            pl.BlockSpec(memory_space=pltpu.SMEM),
            pl.BlockSpec(
                (slabs, pens, None, None, planes, width),
                lambda c, j: (0, 0, c, jnp.where(j < depth, j, 0), 0, 0),
            ),
            pl.BlockSpec(y_table.shape, lambda c, j: (0, 0)),
            pl.BlockSpec(x_matrix.shape, lambda c, j: (0, 0)),
        ],
        out_specs=pl.BlockSpec((None, None, 2 * size_x, size_y), lambda c, j: (c, j, 0, 0)),
        out_shape=jax.ShapeDtypeStruct((count, depth + 1, 2 * size_x, size_y), jnp.float32),
        compiler_params=vmem(),
        cost_estimate=cost(
            24 * count * depth * size_x * size_y * (size_x + size_y),
            4 * count * depth * size_x * size_y * 4,
        ),
        name="plane_forward",
    )(start, received, y_table, x_matrix)


def wave_pair(shape, dim, length):
    index = lax.broadcasted_iota(jnp.int32, shape, dim)
    signed_index = jnp.where(index < length // 2, index, index - length)
    full_wave = (2.0 * math.pi / length) * signed_index.astype(jnp.float32)
    return full_wave, jnp.where(index == length // 2, 0.0, full_wave)


def plane_inverse_kernel(parts, needs, start, *refs):
    spectra = dict(zip(needs, refs[: len(needs)]))
    extras = dict(zip(needs, refs[len(needs) : 2 * len(needs)]))
    y_table, x_table_ref, back, turned = refs[2 * len(needs) :]
    step = pl.program_id(0)
    size_x, size_y = turned.shape[1] // 2, turned.shape[2]
    full_x, curl_x = wave_pair((size_x, 1), 0, size_x)
    full_y, curl_y = wave_pair((1, size_y), 1, size_y)

    def curl(part, source, full_z, curl_z):
        curls = (curl_x, curl_y, curl_z)
        wave_left, wave_right = curls[(part + 1) % 3], curls[(part + 2) % 3]
        left, right = source[(part + 1) % 3], source[(part + 2) % 3]
        wave_squared = full_x * full_x + full_y * full_y + full_z * full_z
        present = wave_squared > 0.0
        scaling = jnp.where(present, 1.0 / jnp.where(present, wave_squared, 1.0), 0.0)
        scaling = scaling * (1.0 / float(size_x * size_y * NZ))
        real_part = wave_left * right[:size_x] - wave_right * left[:size_x]
        imaginary = wave_left * right[size_x:] - wave_right * left[size_x:]
        return -imaginary * scaling, real_part * scaling

    index_z = (start[0] + step).astype(jnp.float32)
    wave_z = (2.0 * math.pi / NZ) * index_z
    for at, part in enumerate(parts):
        real_part, imaginary = curl(part, spectra, wave_z, wave_z)
        turned[at, :size_x] = real_part
        turned[at, size_x:] = imaginary

    @pl.when(jnp.logical_and(start[0] == 0, step == 0))
    def _():
        for at, part in enumerate(parts):
            extra_real, extra_imaginary = curl(part, extras, -math.pi, 0.0)
            turned[at, :size_x] += extra_real
            turned[at, size_x:] += extra_imaginary

    slabs, pens, _, planes, width = back.shape
    for at in range(len(parts)):
        along_x = times_left(x_table_ref[...], turned[at])
        lines = jnp.concatenate([along_x[:size_x], along_x[size_x:]], axis=1)
        result = times_right(lines, y_table[...])
        for pen in range(pens):
            piece = result[:, pen * width : (pen + 1) * width]
            back[:, pen, at] = piece.reshape(slabs, planes, width)


def plane_inverse(parts, start, spectra, shape):
    slabs, pens, depth, planes, width = shape
    count = len(parts)
    size_x = slabs * planes
    size_y = pens * (width // 2)
    y_table = right_table(y_inverse_table(size_y, pens))
    x_matrix = left_table(x_table(size_x, 1.0))
    needs = [c for c in range(3) if any(c != part for part in parts)]

    def at(index, extra):
        return pl.BlockSpec(
            (None, None, 2 * size_x, size_y),
            lambda j: (index, depth if extra else j, 0, 0),
        )

    return pl.pallas_call(
        functools.partial(plane_inverse_kernel, parts, needs),
        grid=(depth,),
        in_specs=[pl.BlockSpec(memory_space=pltpu.SMEM)]
        + [at(spectra[c][1], False) for c in needs]
        + [at(spectra[c][1], True) for c in needs]
        + [
            pl.BlockSpec(y_table.shape, lambda j: (0, 0)),
            pl.BlockSpec(x_matrix.shape, lambda j: (0, 0)),
        ],
        out_specs=pl.BlockSpec(
            (slabs, pens, count, None, planes, width), lambda j: (0, 0, 0, j, 0, 0)
        ),
        out_shape=jax.ShapeDtypeStruct((slabs, pens, count, depth, planes, width), jnp.float32),
        scratch_shapes=[pltpu.VMEM((count, 2 * size_x, size_y), jnp.float32)],
        compiler_params=vmem(),
        cost_estimate=cost(
            24 * count * depth * size_x * size_y * (size_x + size_y),
            6 * count * depth * size_x * size_y * 4,
        ),
        name="plane_inverse",
    )(start, *([spectra[c][0] for c in needs] * 2), y_table, x_matrix)


def stretch_kernel(vorticity, field, before, after, low_x, high_x, low_y, high_y, *refs):
    stretching, padded = refs[-2:]
    step = pl.program_id(0)
    rows_local = field.shape[2]
    first = step == 0
    last = step == pl.num_programs(0) - 1
    own = slice(8, 8 + rows_local)
    for plane in range(STEP):
        padded[plane, own, :] = field[0, plane]
        padded[plane, 6:8, :] = low_y[0, plane]
        padded[plane, 8 + rows_local : 10 + rows_local, :] = high_y[0, plane]

    def difference(ahead, behind, ahead_2, behind_2):
        return (2.0 / 3.0) * (ahead - behind) - (1.0 / 12.0) * (ahead_2 - behind_2)

    def along(plane):
        if plane < 0:
            return jnp.where(first, low_x[0, plane + 2], before[0, plane + 2])
        if plane >= STEP:
            return jnp.where(last, high_x[0, plane - STEP], after[0, plane - STEP])
        return field[0, plane]

    for plane in range(STEP):
        here = field[0, plane]
        along_x = difference(*(along(plane + shift) for shift in (1, -1, 2, -2)))
        along_y = difference(
            *(padded[plane, 8 + shift : 8 + shift + rows_local, :] for shift in (1, -1, 2, -2))
        )
        along_z = difference(*(pltpu.roll(here, shift % NZ, 1) for shift in (-1, 1, -2, 2)))
        stretching[0, plane] = (
            vorticity[0, plane] * along_x + vorticity[1, plane] * along_y + vorticity[2, plane] * along_z
        )


def stretch(parts, vorticity, velocity, halos, stretching):
    _, planes, rows_local, _ = velocity.shape
    part = parts[0]
    count = len(parts)
    pairs = STEP // 2
    low_x, high_x, low_y, high_y = halos
    layer = pl.BlockSpec((1, 2, rows_local, NZ), lambda i, c: (c, 0, 0, 0))
    edge = pl.BlockSpec((1, STEP, 2, NZ), lambda i, c: (c, i, 0, 0))
    block = pl.BlockSpec((1, STEP, rows_local, NZ), lambda i, c: (part + c, i, 0, 0))
    specs = [
        pl.BlockSpec((3, STEP, rows_local, NZ), lambda i, c: (0, i, 0, 0)),
        block,
        pl.BlockSpec(
            (1, 2, rows_local, NZ), lambda i, c: (part + c, jnp.maximum(i * pairs - 1, 0), 0, 0)
        ),
        pl.BlockSpec(
            (1, 2, rows_local, NZ),
            lambda i, c: (part + c, jnp.minimum((i + 1) * pairs, planes // 2 - 1), 0, 0),
        ),
        layer,
        layer,
        edge,
        edge,
    ]
    operands = [vorticity, velocity, velocity, velocity, *halos]
    aliases = {}
    if stretching is not None:
        aliases = {len(operands): 0}
        specs.append(pl.BlockSpec(memory_space=pl.ANY))
        operands.append(stretching)
    return pl.pallas_call(
        stretch_kernel,
        grid=(planes // STEP, count),
        in_specs=specs,
        out_specs=block,
        out_shape=jax.ShapeDtypeStruct((3, planes, rows_local, NZ), jnp.float32),
        input_output_aliases=aliases,
        scratch_shapes=[pltpu.VMEM((STEP, rows_local + 16, NZ), jnp.float32)],
        compiler_params=vmem(),
        cost_estimate=cost(
            40 * count * planes * rows_local * NZ, (3 + 3 * count) * planes * rows_local * NZ * 4
        ),
        name="stretch",
    )(*operands)


def per_device(counts, row_base, z_base, fractions, strength):
    slabs, pens = lax.axis_size("slab"), lax.axis_size("pen")
    devices = slabs * pens
    depth = HALF // devices
    planes, blocks, _ = row_base.shape
    rows_local = blocks * BLOCK_ROWS
    width = 2 * rows_local
    place = lax.axis_index("slab") * pens + lax.axis_index("pen")
    start = (place * depth).astype(jnp.int32).reshape(1)

    particles = (counts, row_base, z_base, fractions, strength)
    begun, ghost_x, ghost_y, ghost_xy = deposit(particles, None)
    ghosts = (
        next_over(ghost_x, ("slab",)),
        next_over(ghost_y, ("pen",)),
        next_over(ghost_xy, ("slab", "pen")),
    )
    (grid,) = deposit(particles, begun)

    def exchange(blocks_out):
        return lax.all_to_all(blocks_out, AXES, 0, 0, tiled=True)

    vorticity = received = None
    spectra = {}
    for parts in FORWARD:
        vorticity, send = z_forward(parts, grid, ghosts, vorticity, devices)
        if received is not None:
            send, _ = lax.optimization_barrier((send, received))
        received = exchange(send)
        spectrum = plane_forward(
            start, received.reshape(slabs, pens, len(parts), depth, planes, width)
        )
        for index, part in enumerate(parts):
            spectra[part] = (spectrum, index)

    velocity = stretching = None
    for parts in BACKWARD:
        back = plane_inverse(parts, start, spectra, (slabs, pens, depth, planes, width))
        received = exchange(back.reshape(devices, len(parts), depth, planes, width))
        if stretching is not None:
            received, stretching = lax.optimization_barrier((received, stretching))
        velocity, low_x, high_x, low_y, high_y = z_inverse(parts, received, velocity)
        halos = (
            shifted(high_x, "slab", 1),
            shifted(low_x, "slab", -1),
            shifted(high_y, "pen", 1),
            shifted(low_y, "pen", -1),
        )
        stretching = stretch(parts, vorticity, velocity, halos, stretching)
    return (vorticity, velocity, stretching)


def solution(mesh):
    in_specs = (
        P("slab", "pen"),
        P("slab", "pen", None),
        P("slab", "pen", None),
        P(None, "slab", "pen", None),
        P(None, "slab", "pen", None),
    )
    out_specs = (
        P(None, "slab", "pen", None),
        P(None, "slab", "pen", None),
        P(None, "slab", "pen", None),
    )
    return jax.shard_map(
        per_device, mesh=mesh, in_specs=in_specs, out_specs=out_specs, check_vma=False
    )
```

time: 422 us -> 409 us (0.969)
  blocking collectives: 104 us -> 0 us
  waiting for transfers between devices: 133 us -> 223 us
  Pallas kernels: 124 us -> 129 us
    all_to_all x2 -> x0, blocking collectives: 104 us -> none  [exchange(): return lax.all_to_all(flat, AXES, 0, 0, tiled=True)]
    ppermute x12 -> x8, waiting for transfers between devices: 1.21 us -> 94.1 us  [shifted(): lax.ppermute(block, axis, [(i, (i + distance) % count) for i in range(cou...]
    ppermute x3, waiting for transfers between devices: 15.5 us -> 0.01 us  [next_over(): return lax.ppermute(block, AXES, route)]
    all_to_all x4, waiting for transfers between devices: 116 us -> 129 us  [exchange(): return lax.all_to_all(blocks_out, AXES, 0, 0, tiled=True)]
    pallas_call x16 -> x12, Pallas kernels: 124 us -> 129 us  [the longest x2 40.1 us: deposit(): pl.pallas_call(functools.partial(deposit_kernel, edges), out_shape=[jax.S...]
    unnamed x45 -> x29, local copies, waits for them, and re-layouts: 18.3 us -> 14.3 us
    ppermute x12 -> x8, starting transfers between devices: 12.8 us -> 9.39 us  [shifted(): lax.ppermute(block, axis, [(i, (i + distance) % count) for i in range(cou...]
  transfers between devices with their start and end apart: 19 -> 15, of which waited for: 6 -> 9; matrix products, arithmetic and copies ran while one was open for 0% -> 0% of each run, Pallas kernels for 17% -> 21%
where the time goes in v2:
time: 409 us; the launch traced here: 406 us
  waiting for transfers between devices  223 us (55%)
  Pallas kernels  129 us (32%)
  starting transfers between devices  38.1 us (9%)
  local copies, waits for them, and re-layouts  14.3 us (3%)
    all_to_all x4, waiting for transfers between devices, exchange(): return lax.all_to_all(blocks_out, AXES, 0, 0, tiled=True)  129 us
    ppermute x8, waiting for transfers between devices, shifted(): lax.ppermute(block, axis, [(i, (i + distance) % count) for i in range(cou...  94.1 us
    pallas_call x2, Pallas kernels, deposit(): pl.pallas_call(functools.partial(deposit_kernel, edges), out_shape=[jax.S...  40.1 us
    all_to_all x4, starting transfers between devices, exchange(): return lax.all_to_all(blocks_out, AXES, 0, 0, tiled=True)  24.6 us
    pallas_call x2, Pallas kernels, plane_inverse(): pl.pallas_call(functools.partial(plane_inverse_kernel, parts, needs), gri...  24.2 us
    pallas_call x2, Pallas kernels, plane_forward(): pl.pallas_call(plane_forward_kernel, grid=(count, depth + 1), in_specs=[p...  19.7 us
    pallas_call x2, Pallas kernels, stretch(): pl.pallas_call(stretch_kernel, grid=(planes // STEP, count), in_specs=spe...  19 us
    unnamed x29, local copies, waits for them, and re-layouts  14.3 us
  transfers between devices with their start and end apart: 15, of which 9 were waited for; matrix products, arithmetic and copies ran while one was open for 0% of the time, Pallas kernels for 21%

profile of v2, /device:TPU:17, one launch (start us, length us, event | category | flops | bytes accessed | tf_op | source)
XLA Modules:
  0.0 405.5 jit_solution(9319215915925877522)
XLA Ops:
  5.6 16.8 %deposit_edges.1 = (f32[3,35,72,256]{3,2,1,0:T(8,128)}, f32[3,3,64,256]{3,2,1,0:T(8,128)S(1)}, f32[3,32,3,256]{3,2,1,0:T(4,128)S(1)}, f32[3,3,3,256]{3,2,1,0:T(4,128)S(1)}) custom-call(s32[32,4]{1,0:T(8,128)S(1)} %copy.24.counts, s32[32,4,512]{2,1,0:T(4,128)S(1)} %copy-done.8, s32[32,4,512]{2,1,0:T(4,128)S(1)} %copy-done.9, f32[3,32,4,512]{3,2,1,0:T(4,128)S(1)} %copy-done.6, ...), custom_call_target="tpu_custom_call" | custom-call | flops 15476981760 | bytes 12582912 | tf_op jit(solution)/shard_map/deposit_edges/pallas_call | solution.py:251
  22.3 3.4 collective-permute-start.2
  26.5 23.3 %deposit_rest.1.grid = f32[3,35,72,256]{3,2,1,0:T(8,128)} custom-call(s32[32,4]{1,0:T(8,128)S(1)} %copy.24.counts, s32[32,4,512]{2,1,0:T(4,128)S(1)} %copy-done.8, s32[32,4,512]{2,1,0:T(4,128)S(1)} %copy-done.9, f32[3,32,4,512]{3,2,1,0:T(4,128)S(1)} %copy-done.6, f32[3,32,4,512]{3,2,1,0:T(4,128)S(1)} %copy-done.7, f32[3,35,72,256]{3,2,1,0:T(8,128)} %get-tuple-element.24.refs_0_), custom_call_target="tpu_custom_call" | custom-call | flops 32841400320 | bytes 12582912 | tf_op jit(solution)/shard_map/deposit_rest/pallas_call | solution.py:251
  49.8 8.1 %z_forward.2 = (f32[3,32,64,256]{3,2,1,0:T(8,128)}, f32[32,2,4,32,128]{4,3,2,1,0:T(8,128)S(1)}) custom-call(f32[3,35,72,256]{3,2,1,0:T(8,128)} %deposit_rest.1.grid, f32[3,3,64,256]{3,2,1,0:T(8,128)S(1)} %collective-permute-done.ghost_x, f32[3,32,3,256]{3,2,1,0:T(4,128)S(1)} %collective-permute-done.1.ghost_y, ...), custom_call_target="tpu_custom_call" | custom-call | flops 1610612736 | bytes 12582912 | tf_op jit(solution)/shard_map/z_forward/pallas_call | solution.py:319
  60.0 6.1 %all-to-all-start = ((f32[32,2,4,32,128]{4,3,2,1,0:T(8,128)}), f32[32,2,4,32,128]{4,3,2,1,0:T(8,128)}, u32[]{:S(2)}, u32[]{:S(2)}) async-start(f32[32,2,4,32,128]{4,3,2,1,0:T(8,128)} %copy-done.3), calls=%async_computation | async-start | bytes 8388608 | tf_op jit(solution)/shard_map/all_to_all | solution.py:647
  66.1 5.0 %z_forward.3 = (f32[3,32,64,256]{3,2,1,0:T(8,128)}, f32[32,1,4,32,128]{4,3,2,1,0:T(8,128)}) custom-call(f32[3,35,72,256]{3,2,1,0:T(8,128)} %deposit_rest.1.grid, f32[3,3,64,256]{3,2,1,0:T(8,128)S(1)} %collective-permute-done.ghost_x, f32[3,32,3,256]{3,2,1,0:T(4,128)S(1)} %collective-permute-done.1.ghost_y, ...), custom_call_target="tpu_custom_call", output_to_operand_aliasing={{0}: (5, {})} | custom-call | flops 805306368 | bytes 6291456 | tf_op jit(solution)/shard_map/z_forward/pallas_call | solution.py:319
  71.1 85.9 %all-to-all-done = f32[32,2,4,32,128]{4,3,2,1,0:T(8,128)} async-done(((f32[32,2,4,32,128]{4,3,2,1,0:T(8,128)}), f32[32,2,4,32,128]{4,3,2,1,0:T(8,128)}, u32[]{:S(2)}, u32[]{:S(2)}) %all-to-all-start) | async-done | bytes 4194336 | tf_op jit(solution)/shard_map/all_to_all | solution.py:647
  157.0 7.1 %all-to-all-start.1 = ((f32[32,1,4,32,128]{4,3,2,1,0:T(8,128)}), f32[32,1,4,32,128]{4,3,2,1,0:T(8,128)}, u32[]{:S(2)}, u32[]{:S(2)}) async-start(f32[32,1,4,32,128]{4,3,2,1,0:T(8,128)} %get-tuple-element.32), calls=%async_computation.1 | async-start | bytes 4194304 | tf_op jit(solution)/shard_map/all_to_all | solution.py:647
  166.9 13.0 %plane_forward.3.refs_1_.refs_2_.refs_4_.refs_5_.refs_0_.refs_3_ = f32[2,5,512,256]{3,2,1,0:T(8,128)} custom-call(s32[1]{0:T(128)} %bitcast.start, f32[8,4,2,4,32,128]{5,4,3,2,1,0:T(8,128)} %bitcast.2.received, bf16[1536,512]{1,0:T(8,128)(2,1)S(1)} %copy-done.12, bf16[512,1536]{1,0:T(8,128)(2,1)S(1)} %copy-done.10), custom_call_target="tpu_custom_call" | custom-call | flops 6442450944 | bytes 8388608 | tf_op jit(solution)/shard_map/plane_forward/pallas_call | solution.py:433
  179.9 10.1 %plane_inverse.3 = f32[8,4,1,4,32,128]{5,4,3,2,1,0:T(8,128)} custom-call(s32[1]{0:T(128)} %bitcast.start, f32[2,5,512,256]{3,2,1,0:T(8,128)} %plane_forward.3.refs_1_.refs_2_.refs_4_.refs_5_.refs_0_.refs_3_, f32[2,5,512,256]{3,2,1,0:T(8,128)} %plane_forward.3.refs_1_.refs_2_.refs_4_.refs_5_.refs_0_.refs_3_, ...), custom_call_target="tpu_custom_call" | custom-call | flops 3221225472 | bytes 6291456 | tf_op jit(solution)/shard_map/plane_inverse/pallas_call | solution.py:523
  190.0 21.4 %all-to-all-done.1 = f32[32,1,4,32,128]{4,3,2,1,0:T(8,128)} async-done(((f32[32,1,4,32,128]{4,3,2,1,0:T(8,128)}), f32[32,1,4,32,128]{4,3,2,1,0:T(8,128)}, u32[]{:S(2)}, u32[]{:S(2)}) %all-to-all-start.1) | async-done | bytes 2097184 | tf_op jit(solution)/shard_map/all_to_all | solution.py:647
  211.4 5.7 %all-to-all-start.3 = ((f32[32,1,4,32,128]{4,3,2,1,0:T(8,128)}), f32[32,1,4,32,128]{4,3,2,1,0:T(8,128)}, u32[]{:S(2)}, u32[]{:S(2)}) async-start(f32[32,1,4,32,128]{4,3,2,1,0:T(8,128)} %bitcast.4), calls=%async_computation.3 | async-start | bytes 4194304 | tf_op jit(solution)/shard_map/all_to_all | solution.py:647
  219.9 6.7 %plane_forward.2.refs_0_.refs_3_ = f32[1,5,512,256]{3,2,1,0:T(8,128)} custom-call(s32[1]{0:T(128)} %bitcast.start, f32[8,4,1,4,32,128]{5,4,3,2,1,0:T(8,128)} %bitcast.1.received, bf16[1536,512]{1,0:T(8,128)(2,1)S(1)} %copy-done.13, bf16[512,1536]{1,0:T(8,128)(2,1)S(1)} %copy-done.11), custom_call_target="tpu_custom_call" | custom-call | flops 3221225472 | bytes 4194304 | tf_op jit(solution)/shard_map/plane_forward/pallas_call | solution.py:433
  228.3 14.1 %plane_inverse.2 = f32[8,4,2,4,32,128]{5,4,3,2,1,0:T(8,128)} custom-call(s32[1]{0:T(128)} %bitcast.start, f32[1,5,512,256]{3,2,1,0:T(8,128)S(1)} %copy-done, f32[2,5,512,256]{3,2,1,0:T(8,128)} %plane_forward.3.refs_1_.refs_2_.refs_4_.refs_5_.refs_0_.refs_3_, f32[2,5,512,256]{3,2,1,0:T(8,128)} %plane_forward.3.refs_1_.refs_2_.refs_4_.refs_5_.refs_0_.refs_3_, ...), custom_call_target="tpu_custom_call" | custom-call | flops 6442450944 | bytes 12582912 | tf_op jit(solution)/shard_map/plane_inverse/pallas_call | solution.py:523
  242.4 22.0 %all-to-all-done.3.received = f32[32,1,4,32,128]{4,3,2,1,0:T(8,128)} async-done(((f32[32,1,4,32,128]{4,3,2,1,0:T(8,128)}), f32[32,1,4,32,128]{4,3,2,1,0:T(8,128)}, u32[]{:S(2)}, u32[]{:S(2)}) %all-to-all-start.3) | async-done | bytes 2097184 | tf_op jit(solution)/shard_map/all_to_all | solution.py:647
  264.4 5.7 %all-to-all-start.2 = ((f32[32,2,4,32,128]{4,3,2,1,0:T(8,128)}), f32[32,2,4,32,128]{4,3,2,1,0:T(8,128)}, u32[]{:S(2)}, u32[]{:S(2)}) async-start(f32[32,2,4,32,128]{4,3,2,1,0:T(8,128)} %bitcast.5), calls=%async_computation.2 | async-start | bytes 8388608 | tf_op jit(solution)/shard_map/all_to_all | solution.py:647
  270.1 4.7 %z_inverse.2 = (f32[3,32,64,256]{3,2,1,0:T(8,128)}, f32[1,2,64,256]{3,2,1,0:T(8,128)S(1)}, f32[1,2,64,256]{3,2,1,0:T(8,128)S(1)}, f32[1,32,2,256]{3,2,1,0:T(2,128)S(1)}, f32[1,32,2,256]{3,2,1,0:T(2,128)S(1)}) custom-call(f32[32,1,4,32,128]{4,3,2,1,0:T(8,128)} %all-to-all-done.3.received, bf16[768,256]{1,0:T(8,128)(2,1)S(1)} %copy-done.5), custom_call_target="tpu_custom_call" | custom-call | flops 805306368 | bytes 4194304 | tf_op jit(solution)/shard_map/z_inverse/pallas_call | solution.py:379
  279.1 17.7 %collective-permute-done.5.low_y = f32[1,32,2,256]{3,2,1,0:T(2,128)S(1)} collective-permute-done((f32[1,32,2,256]{3,2,1,0:T(2,128)S(1)}, f32[1,32,2,256]{3,2,1,0:T(2,128)S(1)}, u32[]{:S(2)}, u32[]{:S(2)}) %collective-permute-start.5) | collective-permute-done | bytes 65568 | tf_op jit(solution)/shard_map/ppermute | solution.py:276
  299.7 65.5 %collective-permute-done.3.low_x = f32[1,2,64,256]{3,2,1,0:T(8,128)S(1)} collective-permute-done((f32[1,2,64,256]{3,2,1,0:T(8,128)S(1)}, f32[1,2,64,256]{3,2,1,0:T(8,128)S(1)}, u32[]{:S(2)}, u32[]{:S(2)}) %collective-permute-start.3) | collective-permute-done | bytes 131104 | tf_op jit(solution)/shard_map/ppermute | solution.py:276
  365.3 7.0 %stretch.2.refs_0_ = f32[3,32,64,256]{3,2,1,0:T(8,128)} custom-call(f32[3,32,64,256]{3,2,1,0:T(8,128)} %get-tuple-element.21.vorticity, f32[3,32,64,256]{3,2,1,0:T(8,128)} %get-tuple-element.33.field.before.after.refs_0_, f32[3,32,64,256]{3,2,1,0:T(8,128)} %get-tuple-element.33.field.before.after.refs_0_, ...), custom_call_target="tpu_custom_call" | custom-call | flops 20971520 | bytes 12582912 | tf_op jit(solution)/shard_map/stretch/pallas_call | solution.py:611
  372.3 8.2 %z_inverse.3 = (f32[3,32,64,256]{3,2,1,0:T(8,128)}, f32[2,2,64,256]{3,2,1,0:T(8,128)S(1)}, f32[2,2,64,256]{3,2,1,0:T(8,128)S(1)}, f32[2,32,2,256]{3,2,1,0:T(2,128)S(1)}, f32[2,32,2,256]{3,2,1,0:T(2,128)S(1)}) custom-call(f32[32,2,4,32,128]{4,3,2,1,0:T(8,128)} %all-to-all-done.2.received, ...), custom_call_target="tpu_custom_call", output_to_operand_aliasing={{0}: (2, {})} | custom-call | flops 1610612736 | bytes 8388608 | tf_op jit(solution)/shard_map/z_inverse/pallas_call | solution.py:379
  385.5 3.0 collective-permute-done.9.low_y
  390.2 3.3 collective-permute-done.8.high_x
  393.5 12.0 %stretch.3 = f32[3,32,64,256]{3,2,1,0:T(8,128)} custom-call(f32[3,32,64,256]{3,2,1,0:T(8,128)} %get-tuple-element.21.vorticity, f32[3,32,64,256]{3,2,1,0:T(8,128)} %get-tuple-element.22.field.before.after, f32[3,32,64,256]{3,2,1,0:T(8,128)} %get-tuple-element.22.field.before.after, ...), custom_call_target="tpu_custom_call", output_to_operand_aliasing={{}: (8, {})} | custom-call | flops 41943040 | bytes 18874368 | tf_op jit(solution)/shard_map/stretch/pallas_call | solution.py:611
  (47 shorter events, 29.1 us)
Async XLA Ops:
  22.3 27.5 %collective-permute-start.2 = (f32[3,3,3,256]{3,2,1,0:T(4,128)S(1)}, f32[3,3,3,256]{3,2,1,0:T(4,128)S(1)}, u32[]{:S(2)}, u32[]{:S(2)}) collective-permute-start(f32[3,3,3,256]{3,2,1,0:T(4,128)S(1)} %get-tuple-element.27), channel_id=1, source_target_pairs={{0,5},{1,6},{2,7},{3,4},{4,9},{5,10},{6,11},{7,8},{8,13},{9,14},{1... | collective-permute-start | bytes 82952 | tf_op jit(solution)/shard_map/ppermute | solution.py:271
  25.8 24.1 %collective-permute-start.1 = (f32[3,32,3,256]{3,2,1,0:T(4,128)S(1)}, f32[3,32,3,256]{3,2,1,0:T(4,128)S(1)}, u32[]{:S(2)}, u32[]{:S(2)}) collective-permute-start(f32[3,32,3,256]{3,2,1,0:T(4,128)S(1)} %get-tuple-element.26), channel_id=1, source_target_pairs={{0,1},{1,2},{2,3},{3,0},{4,5},{5,6},{6,7},{7,4},{8,9},{9,10},{10,1... | collective-permute-start | bytes 884744 | tf_op jit(solution)/shard_map/ppermute | solution.py:271
  25.8 24.1 %collective-permute-start = (f32[3,3,64,256]{3,2,1,0:T(8,128)S(1)}, f32[3,3,64,256]{3,2,1,0:T(8,128)S(1)}, u32[]{:S(2)}, u32[]{:S(2)}) collective-permute-start(f32[3,3,64,256]{3,2,1,0:T(8,128)S(1)} %get-tuple-element.25), channel_id=1, source_target_pairs={{0,4},{1,5},{2,6},{3,7},{4,8},{5,9},{6,10},{7,11},{8,12},{9,13},{1... | collective-permute-start | bytes 1769480 | tf_op jit(solution)/shard_map/ppermute | solution.py:271
  26.5 23.3 %copy-start.4 = (bf16[768,256]{1,0:T(8,128)(2,1)S(1)}, bf16[768,256]{1,0:T(8,128)(2,1)}, u32[]{:S(2)}) copy-start(bf16[768,256]{1,0:T(8,128)(2,1)} %constant.23.clone.table) | copy-start | bytes 1179652
  58.0 2.0 copy-start.3
  60.0 97.0 %all-to-all-start = ((f32[32,2,4,32,128]{4,3,2,1,0:T(8,128)}), f32[32,2,4,32,128]{4,3,2,1,0:T(8,128)}, u32[]{:S(2)}, u32[]{:S(2)}) async-start(f32[32,2,4,32,128]{4,3,2,1,0:T(8,128)} %copy-done.3), calls=%async_computation | async-start | bytes 8388608 | tf_op jit(solution)/shard_map/all_to_all | solution.py:647
  157.0 54.4 %all-to-all-start.1 = ((f32[32,1,4,32,128]{4,3,2,1,0:T(8,128)}), f32[32,1,4,32,128]{4,3,2,1,0:T(8,128)}, u32[]{:S(2)}, u32[]{:S(2)}) async-start(f32[32,1,4,32,128]{4,3,2,1,0:T(8,128)} %get-tuple-element.32), calls=%async_computation.1 | async-start | bytes 4194304 | tf_op jit(solution)/shard_map/all_to_all | solution.py:647
  164.1 1.4 copy-start.10
  165.5 1.4 copy-start.12
  166.9 13.0 %copy-start.1 = (bf16[512,1536]{1,0:T(8,128)(2,1)S(1)}, bf16[512,1536]{1,0:T(8,128)(2,1)}, u32[]{:S(2)}) copy-start(bf16[512,1536]{1,0:T(8,128)(2,1)} %constant.27.clone.refs_7_.refs_5_) | copy-start | bytes 4718596
  166.9 13.0 %copy-start.2 = (bf16[1536,512]{1,0:T(8,128)(2,1)S(1)}, bf16[1536,512]{1,0:T(8,128)(2,1)}, u32[]{:S(2)}) copy-start(bf16[1536,512]{1,0:T(8,128)(2,1)} %constant.26.clone.refs_6_.refs_4_) | copy-start | bytes 4718596
  211.4 53.0 %all-to-all-start.3 = ((f32[32,1,4,32,128]{4,3,2,1,0:T(8,128)}), f32[32,1,4,32,128]{4,3,2,1,0:T(8,128)}, u32[]{:S(2)}, u32[]{:S(2)}) async-start(f32[32,1,4,32,128]{4,3,2,1,0:T(8,128)} %bitcast.4), calls=%async_computation.3 | async-start | bytes 4194304 | tf_op jit(solution)/shard_map/all_to_all | solution.py:647
  217.1 1.4 copy-start.11
  226.6 1.7 copy-start
  264.4 5.7 %copy-start.5 = (bf16[768,256]{1,0:T(8,128)(2,1)S(1)}, bf16[768,256]{1,0:T(8,128)(2,1)}, u32[]{:S(2)}) copy-start(bf16[768,256]{1,0:T(8,128)(2,1)} %constant.28.clone.table) | copy-start | bytes 1179652
  264.4 107.9 %all-to-all-start.2 = ((f32[32,2,4,32,128]{4,3,2,1,0:T(8,128)}), f32[32,2,4,32,128]{4,3,2,1,0:T(8,128)}, u32[]{:S(2)}, u32[]{:S(2)}) async-start(f32[32,2,4,32,128]{4,3,2,1,0:T(8,128)} %bitcast.5), calls=%async_computation.2 | async-start | bytes 8388608 | tf_op jit(solution)/shard_map/all_to_all | solution.py:647
  274.8 90.5 %collective-permute-start.3 = (f32[1,2,64,256]{3,2,1,0:T(8,128)S(1)}, f32[1,2,64,256]{3,2,1,0:T(8,128)S(1)}, u32[]{:S(2)}, u32[]{:S(2)}) collective-permute-start(f32[1,2,64,256]{3,2,1,0:T(8,128)S(1)} %get-tuple-element.34), channel_id=1, source_target_pairs={{0,4},{4,8},{8,12},{12,16},{16,20},{20,24},{24,28},{28,0},{1,5},{5... | collective-permute-start | bytes 393224 | tf_op jit(solution)/shard_map/ppermute | solution.py:276
  276.0 89.3 %collective-permute-start.4 = (f32[1,2,64,256]{3,2,1,0:T(8,128)S(1)}, f32[1,2,64,256]{3,2,1,0:T(8,128)S(1)}, u32[]{:S(2)}, u32[]{:S(2)}) collective-permute-start(f32[1,2,64,256]{3,2,1,0:T(8,128)S(1)} %get-tuple-element.35), channel_id=1, source_target_pairs={{0,28},{4,0},{8,4},{12,8},{16,12},{20,16},{24,20},{28,24},{1,29},{... | collective-permute-start | bytes 393224 | tf_op jit(solution)/shard_map/ppermute | solution.py:276
  277.1 19.7 %collective-permute-start.5 = (f32[1,32,2,256]{3,2,1,0:T(2,128)S(1)}, f32[1,32,2,256]{3,2,1,0:T(2,128)S(1)}, u32[]{:S(2)}, u32[]{:S(2)}) collective-permute-start(f32[1,32,2,256]{3,2,1,0:T(2,128)S(1)} %get-tuple-element.36), channel_id=1, source_target_pairs={{0,1},{1,2},{2,3},{3,0},{4,5},{5,6},{6,7},{7,4},{8,9},{9,10},{10,1... | collective-permute-start | bytes 196616 | tf_op jit(solution)/shard_map/ppermute | solution.py:276
  279.1 20.6 %collective-permute-start.6 = (f32[1,32,2,256]{3,2,1,0:T(2,128)S(1)}, f32[1,32,2,256]{3,2,1,0:T(2,128)S(1)}, u32[]{:S(2)}, u32[]{:S(2)}) collective-permute-start(f32[1,32,2,256]{3,2,1,0:T(2,128)S(1)} %get-tuple-element.37), channel_id=1, source_target_pairs={{0,3},{1,0},{2,1},{3,2},{4,7},{5,4},{6,5},{7,6},{8,11},{9,8},{10,9... | collective-permute-start | bytes 196616 | tf_op jit(solution)/shard_map/ppermute | solution.py:276
  380.5 9.7 %collective-permute-start.7 = (f32[2,2,64,256]{3,2,1,0:T(8,128)S(1)}, f32[2,2,64,256]{3,2,1,0:T(8,128)S(1)}, u32[]{:S(2)}, u32[]{:S(2)}) collective-permute-start(f32[2,2,64,256]{3,2,1,0:T(8,128)S(1)} %get-tuple-element.40), channel_id=1, source_target_pairs={{0,4},{4,8},{8,12},{12,16},{16,20},{20,24},{24,28},{28,0},{1,5},{5... | collective-permute-start | bytes 786440 | tf_op jit(solution)/shard_map/ppermute | solution.py:276
  380.5 13.0 %collective-permute-start.8 = (f32[2,2,64,256]{3,2,1,0:T(8,128)S(1)}, f32[2,2,64,256]{3,2,1,0:T(8,128)S(1)}, u32[]{:S(2)}, u32[]{:S(2)}) collective-permute-start(f32[2,2,64,256]{3,2,1,0:T(8,128)S(1)} %get-tuple-element.41), channel_id=1, source_target_pairs={{0,28},{4,0},{8,4},{12,8},{16,12},{20,16},{24,20},{28,24},{1,29},{... | collective-permute-start | bytes 786440 | tf_op jit(solution)/shard_map/ppermute | solution.py:276
  382.8 5.7 %collective-permute-start.9 = (f32[2,32,2,256]{3,2,1,0:T(2,128)S(1)}, f32[2,32,2,256]{3,2,1,0:T(2,128)S(1)}, u32[]{:S(2)}, u32[]{:S(2)}) collective-permute-start(f32[2,32,2,256]{3,2,1,0:T(2,128)S(1)} %get-tuple-element.42), channel_id=1, source_target_pairs={{0,1},{1,2},{2,3},{3,0},{4,5},{5,6},{6,7},{7,4},{8,9},{9,10},{10,1... | collective-permute-start | bytes 393224 | tf_op jit(solution)/shard_map/ppermute | solution.py:276
  385.5 4.7 %collective-permute-start.10 = (f32[2,32,2,256]{3,2,1,0:T(2,128)S(1)}, f32[2,32,2,256]{3,2,1,0:T(2,128)S(1)}, u32[]{:S(2)}, u32[]{:S(2)}) collective-permute-start(f32[2,32,2,256]{3,2,1,0:T(2,128)S(1)} %get-tuple-element.43), channel_id=1, source_target_pairs={{0,3},{1,0},{2,1},{3,2},{4,7},{5,4},{6,5},{7,6},{8,11},{9,8},{10,9... | collective-permute-start | bytes 393224 | tf_op jit(solution)/shard_map/ppermute | solution.py:276
  (5 other events, 5.6 us)

commit v3 on v2

v3 whole, which is shorter than its diff:
```python
import functools
import math

import jax
import jax.numpy as jnp
import numpy as np
from jax import lax
from jax.experimental import pallas as pl
from jax.experimental.pallas import tpu as pltpu
from jax.sharding import PartitionSpec as P

NZ = 256
BLOCK_ROWS = 16
HALF = NZ // 2
STEP = 8
SLOTS_AT_ONCE = 256
MIB = 1024 * 1024
NEW = object()
AXES = ("slab", "pen")


def kernel_weight(distance):
    magnitude = jnp.abs(distance)
    inner_part = 1.0 - 2.5 * magnitude * magnitude + 1.5 * magnitude * magnitude * magnitude
    outer_part = 0.5 * (2.0 - magnitude) * (2.0 - magnitude) * (1.0 - magnitude)
    return jnp.where(magnitude < 1.0, inner_part, jnp.where(magnitude < 2.0, outer_part, 0.0))


def vmem(limit=48, **extra):
    return pltpu.CompilerParams(vmem_limit_bytes=limit * MIB, **extra)


def cost(flops, moved):
    return pl.CostEstimate(flops=int(flops), bytes_accessed=int(moved), transcendentals=0)


def two_parts(table):
    table = np.asarray(table, np.float32)
    high = table.astype(jnp.bfloat16)
    low = (table - high.astype(np.float32)).astype(jnp.bfloat16)
    return high, low


def right_table(table):
    high, low = two_parts(table)
    return jnp.asarray(np.concatenate([high, high, low], axis=0))


def left_table(table):
    high, low = two_parts(table)
    return jnp.asarray(np.concatenate([high, high, low], axis=1))


def waves(length):
    index = np.arange(length)
    angle = 2.0 * np.pi / length * (index[:, None] * index[None, :] % length)
    return np.cos(angle), np.sin(angle)


def z_forward_table():
    cosine, sine = waves(NZ)
    real_part, imaginary = cosine[:, :HALF].copy(), -sine[:, :HALF]
    imaginary[:, 0] = cosine[:, HALF]
    return np.concatenate([real_part, imaginary], axis=1)


def z_inverse_table():
    cosine, sine = waves(NZ)
    real_part, imaginary = 2.0 * cosine[:HALF], -2.0 * sine[:HALF]
    real_part[0] = 1.0
    imaginary[0] = cosine[HALF]
    return np.concatenate([real_part, imaginary], axis=0)


def y_forward_table(length, parts):
    cosine, sine = waves(length)
    width = length // parts
    rows = []
    for part in range(parts):
        here = slice(part * width, (part + 1) * width)
        rows.append(np.concatenate([cosine[here], -sine[here]], axis=1))
        rows.append(np.concatenate([sine[here], cosine[here]], axis=1))
    return np.concatenate(rows, axis=0)


def y_inverse_table(length, parts):
    cosine, sine = waves(length)
    width = length // parts
    columns = []
    for part in range(parts):
        here = slice(part * width, (part + 1) * width)
        columns.append(np.concatenate([cosine[:, here], -sine[:, here]], axis=0))
        columns.append(np.concatenate([sine[:, here], cosine[:, here]], axis=0))
    return np.concatenate(columns, axis=1)


def x_table(length, sign):
    cosine, sine = waves(length)
    return np.concatenate(
        [
            np.concatenate([cosine, -sign * sine], axis=1),
            np.concatenate([sign * sine, cosine], axis=1),
        ],
        axis=0,
    )


def split_values(values):
    high = values.astype(jnp.bfloat16)
    low = (values - high.astype(jnp.float32)).astype(jnp.bfloat16)
    return high, low


def times_right(values, table):
    high, low = split_values(values)
    return jnp.dot(
        jnp.concatenate([high, low, high], axis=1), table, preferred_element_type=jnp.float32
    )


def times_left(table, values):
    high, low = split_values(values)
    return jnp.dot(
        table, jnp.concatenate([high, low, high], axis=0), preferred_element_type=jnp.float32
    )


def deposit_kernel(begin, end, counts, row_base, z_base, fractions, strength, *refs):
    planes, blocks, slots = row_base.shape
    first_source = max(begin - 3, 0)
    last = end == planes
    width = min(SLOTS_AT_ONCE, slots)
    rows_local = blocks * BLOCK_ROWS
    ext = BLOCK_ROWS + 8
    if last:
        grid, ghost_y, ghost_x, ghost_xy = refs[:4]
    else:
        grid, ghost_y = refs[:2]
    rows, row_here, z_here, fractions_here, strength_here, arrived = refs[-6:]
    taken = slice(first_source, end)
    copies = [
        pltpu.make_async_copy(row_base.at[taken], row_here, arrived.at[0]),
        pltpu.make_async_copy(z_base.at[taken], z_here, arrived.at[1]),
        pltpu.make_async_copy(fractions.at[:, taken], fractions_here, arrived.at[2]),
        pltpu.make_async_copy(strength.at[:, taken], strength_here, arrived.at[3]),
    ]
    for copy in copies:
        copy.start()

    def clear(plane, _):
        grid[:, plane] = jnp.zeros((3,) + grid.shape[2:], jnp.float32)
        return 0

    lax.fori_loop(0, grid.shape[1], clear, 0)
    z_rows = 16
    z_iota = lax.broadcasted_iota(jnp.int32, (z_rows, width), 0)
    j_iota = lax.broadcasted_iota(jnp.int32, (ext, width), 0).astype(jnp.float32)
    z_tiles = [
        (z_iota + z_rows * t).astype(jnp.float32).astype(jnp.bfloat16) for t in range(NZ // z_rows)
    ]
    for copy in copies:
        copy.wait()

    def one_plane(offsets, source, _):
        plane = source + first_source
        slot = lax.broadcasted_iota(jnp.int32, (blocks, slots), 1)
        group = lax.broadcasted_iota(jnp.int32, (blocks, slots), 0)
        count = jnp.zeros((blocks, slots), jnp.int32)
        for block in range(blocks):
            count = jnp.where(group == block, counts[plane, block], count)
        live = slot < count
        row_cell = row_here[source].astype(jnp.float32)
        z_cell = z_here[source]
        for offset in range(4):
            weight_x = kernel_weight(float(offset - 1) - fractions_here[0, source])
            for part in range(3):
                rows[part * 4 + offset] = jnp.where(live, strength_here[part, source] * weight_x, 0.0)
            rows[12 + offset] = kernel_weight(float(offset - 1) - fractions_here[1, source])
            rows[16 + offset] = row_cell + float(offset)
            rows[20 + offset] = kernel_weight(float(offset - 1) - fractions_here[2, source])
            rows[24 + offset] = jnp.bitwise_and(z_cell + offset, NZ - 1).astype(jnp.float32)

        used = [(part, offset) for part in range(3) for offset in offsets]

        def spread(block, first):
            here = slice(first, first + width)

            def row(index):
                return rows[index, block : block + 1, here]

            weight_y = jnp.zeros((ext, width), jnp.float32)
            for offset in range(4):
                weight_y = jnp.where(j_iota == row(16 + offset), row(12 + offset), weight_y)
            coefs = jnp.concatenate([row(p * 4 + o) * weight_y for p, o in used], axis=0)
            coefs = coefs.astype(jnp.bfloat16)
            z_weight = [
                jnp.broadcast_to(row(20 + offset), (z_rows, width)).astype(jnp.bfloat16)
                for offset in range(4)
            ]
            z_place = [
                jnp.broadcast_to(row(24 + offset), (z_rows, width)).astype(jnp.bfloat16)
                for offset in range(4)
            ]
            tiles = []
            for z_tile in z_tiles:
                tile = jnp.zeros((z_rows, width), jnp.bfloat16)
                for offset in range(4):
                    tile = jnp.where(z_tile == z_place[offset], z_weight[offset], tile)
                tiles.append(tile)
            weight_z = jnp.concatenate(tiles, axis=0)
            result = lax.dot_general(
                coefs, weight_z, (((1,), (1,)), ((), ())), preferred_element_type=jnp.float32
            )
            low = block * BLOCK_ROWS
            for index, (part, offset) in enumerate(used):
                grid[part, plane + offset - begin, low : low + ext, :] += result[
                    index * ext : (index + 1) * ext
                ]

        for block in range(blocks):
            spread(block, 0)
        for first in range(width, slots, width):
            for block in range(blocks):
                pl.when(counts[plane, block] > first)(functools.partial(spread, block, first))
        return 0

    top = end + 3 if last else end
    inner_begin, inner_end = begin, top - 3
    for plane in range(first_source, begin):
        offsets = [o for o in range(4) if begin <= plane + o]
        one_plane(offsets, plane - first_source, 0)
    lax.fori_loop(
        inner_begin - first_source,
        inner_end - first_source,
        functools.partial(one_plane, list(range(4))),
        0,
    )
    for plane in range(inner_end, end):
        offsets = [o for o in range(4) if plane + o < top]
        one_plane(offsets, plane - first_source, 0)

    def side(plane, _):
        ghost_y[:, plane] = grid[:, plane, rows_local : rows_local + 3, :]
        return 0

    lax.fori_loop(0, end - begin, side, 0)
    if last:
        for part in range(3):
            for offset in range(3):
                plane = end - begin + offset
                ghost_x[part, offset] = grid[part, plane, :rows_local, :]
                ghost_xy[part, offset] = grid[part, plane, rows_local : rows_local + 3, :]


def deposit(particles, begin, end):
    planes, blocks, slots = particles[1].shape
    sources = end - max(begin - 3, 0)
    rows_local = blocks * BLOCK_ROWS
    whole = pl.BlockSpec(memory_space=pltpu.VMEM)
    last = end == planes
    shapes = [(3, end - begin + (3 if last else 0), rows_local + 8, NZ), (3, end - begin, 3, NZ)]
    if last:
        shapes += [(3, 3, rows_local, NZ), (3, 3, 3, NZ)]
    return pl.pallas_call(
        functools.partial(deposit_kernel, begin, end),
        out_shape=[jax.ShapeDtypeStruct(shape, jnp.float32) for shape in shapes],
        in_specs=[pl.BlockSpec(memory_space=pltpu.SMEM)]
        + [pl.BlockSpec(memory_space=pltpu.HBM)] * 4,
        out_specs=[whole] * len(shapes),
        scratch_shapes=[
            pltpu.VMEM((28, blocks, slots), jnp.float32),
            pltpu.VMEM((sources, blocks, slots), jnp.int32),
            pltpu.VMEM((sources, blocks, slots), jnp.int32),
            pltpu.VMEM((3, sources, blocks, slots), jnp.float32),
            pltpu.VMEM((3, sources, blocks, slots), jnp.float32),
            pltpu.SemaphoreType.DMA((4,)),
        ],
        compiler_params=vmem(),
        cost_estimate=cost(10 * sources * blocks * 288 * slots * NZ, 12 * MIB),
        name="deposit",
    )(*particles)


def next_over(block, axes):
    counts = [lax.axis_size(axis) for axis in AXES]
    route = []
    for slab in range(counts[0]):
        for pen in range(counts[1]):
            to_slab = (slab + 1) % counts[0] if "slab" in axes else slab
            to_pen = (pen + 1) % counts[1] if "pen" in axes else pen
            route.append((slab * counts[1] + pen, to_slab * counts[1] + to_pen))
    return lax.ppermute(block, AXES, route)


def shifted(block, axis, distance):
    count = lax.axis_size(axis)
    return lax.ppermute(block, axis, [(i, (i + distance) % count) for i in range(count)])


def z_forward_body(with_x, grid, ghost_y, *refs):
    vorticity, send = refs[-2:]
    table = refs[-3]
    rows_local = vorticity.shape[2]
    vorticity[0] = grid[0, :, :rows_local, :]
    vorticity[0, :, 0:3, :] += ghost_y[0]
    if with_x:
        ghost_x, ghost_xy = refs[:2]

        @pl.when(pl.program_id(1) == 0)
        def _():
            vorticity[0, 0:3] += ghost_x[0]
            vorticity[0, 0:3, 0:3, :] += ghost_xy[0]

    spectrum = times_right(vorticity[0].reshape(STEP * rows_local, NZ), table[...])
    lines = send.reshape(HALF * STEP, 2 * rows_local)
    for plane in range(STEP):
        here = spectrum[plane * rows_local : (plane + 1) * rows_local]
        stacked = jnp.concatenate([here[:, :HALF], here[:, HALF:]], axis=0)
        lines[pl.ds(plane, HALF, stride=STEP), :] = stacked.T


def z_forward(parts, cell_range, deposited, ghosts_x, vorticity, send, shape):
    devices, depth, planes, width = shape
    begin, end = cell_range
    grid, ghost_y = deposited
    rows_local = width // 2
    count = len(parts)
    part = parts[0]
    table = right_table(z_forward_table())
    here = (end - begin) // STEP
    at = begin // STEP
    joined = send is not None
    send_at = at if joined else 0
    send_planes = planes if joined else end - begin
    specs = [
        pl.BlockSpec((1, STEP, rows_local + 8, NZ), lambda c, i: (part + c, i, 0, 0)),
        pl.BlockSpec((1, STEP, 3, NZ), lambda c, i: (part + c, i, 0, 0)),
    ]
    operands = [grid, ghost_y]
    if ghosts_x is not None:
        operands += list(ghosts_x)
        specs += [
            pl.BlockSpec((1, 3, rows_local, NZ), lambda c, i: (part + c, 0, 0, 0)),
            pl.BlockSpec((1, 3, 3, NZ), lambda c, i: (part + c, 0, 0, 0)),
        ]
    operands.append(table)
    specs.append(pl.BlockSpec(table.shape, lambda c, i: (0, 0)))
    aliases = {}
    for index, output in enumerate((vorticity, send)):
        if output is not None and output is not NEW:
            aliases[len(operands)] = index
            specs.append(pl.BlockSpec(memory_space=pl.ANY))
            operands.append(output)
    used = 5 if ghosts_x is not None else 3

    def kernel(*refs):
        z_forward_body(ghosts_x is not None, *refs[:used], *refs[-2:])

    return pl.pallas_call(
        kernel,
        grid=(count, here),
        in_specs=specs,
        out_specs=(
            pl.BlockSpec((1, STEP, rows_local, NZ), lambda c, i: (part + c, at + i, 0, 0)),
            pl.BlockSpec(
                (devices, None, depth, STEP, width), lambda c, i: (0, c, 0, send_at + i, 0)
            ),
        ),
        out_shape=(
            jax.ShapeDtypeStruct((3, planes, rows_local, NZ), jnp.float32),
            jax.ShapeDtypeStruct((devices, count, depth, send_planes, width), jnp.float32),
        ),
        input_output_aliases=aliases,
        compiler_params=vmem(),
        cost_estimate=cost(
            6 * count * here * STEP * rows_local * NZ * NZ,
            3 * count * here * STEP * rows_local * NZ * 4,
        ),
        name="z_forward",
    )(*operands)


def z_inverse_kernel(received, table, field, low_x, high_x, low_y, high_y):
    rows_local = field.shape[1]
    lines = received.reshape(HALF * STEP, 2 * rows_local)
    pieces = []
    for plane in range(STEP):
        turned = lines[pl.ds(plane, HALF, stride=STEP), :].T
        pieces.append(jnp.concatenate([turned[:rows_local], turned[rows_local:]], axis=1))
    values = times_right(jnp.concatenate(pieces, axis=0), table[...])
    field[...] = values.reshape(STEP, rows_local, NZ)
    low_y[...] = field[:, 0:2, :]
    high_y[...] = field[:, rows_local - 2 : rows_local, :]

    @pl.when(pl.program_id(0) == 0)
    def _():
        low_x[...] = field[0:2]

    @pl.when(pl.program_id(0) == pl.num_programs(0) - 1)
    def _():
        high_x[...] = field[STEP - 2 : STEP]


def z_inverse(received):
    devices, depth, planes, width = received.shape
    rows_local = width // 2
    table = right_table(z_inverse_table())
    layer = pl.BlockSpec((2, rows_local, NZ), lambda i: (0, 0, 0))
    edge = pl.BlockSpec((STEP, 2, NZ), lambda i: (i, 0, 0))
    return pl.pallas_call(
        z_inverse_kernel,
        grid=(planes // STEP,),
        in_specs=[
            pl.BlockSpec((devices, depth, STEP, width), lambda i: (0, 0, i, 0)),
            pl.BlockSpec(table.shape, lambda i: (0, 0)),
        ],
        out_specs=(
            pl.BlockSpec((STEP, rows_local, NZ), lambda i: (i, 0, 0)),
            layer,
            layer,
            edge,
            edge,
        ),
        out_shape=(
            jax.ShapeDtypeStruct((planes, rows_local, NZ), jnp.float32),
            jax.ShapeDtypeStruct((2, rows_local, NZ), jnp.float32),
            jax.ShapeDtypeStruct((2, rows_local, NZ), jnp.float32),
            jax.ShapeDtypeStruct((planes, 2, NZ), jnp.float32),
            jax.ShapeDtypeStruct((planes, 2, NZ), jnp.float32),
        ),
        compiler_params=vmem(),
        cost_estimate=cost(
            6 * planes * rows_local * NZ * NZ, 2 * planes * rows_local * NZ * 4
        ),
        name="z_inverse",
    )(received, table)


def plane_forward_kernel(start, *refs):
    y_table, x_table_ref, spectrum = refs[-3:]
    received = refs[:-3]
    step = pl.program_id(1)
    depth = pl.num_programs(1) - 1
    has_first = start[0] == 0

    @pl.when(jnp.logical_or(step < depth, has_first))
    def _():
        slabs, pens, _, width = received[0].shape
        pieces = []
        for pen in range(pens):
            piece = jnp.concatenate([cells[:, pen] for cells in received], axis=1)
            pieces.append(piece.reshape(slabs * piece.shape[1], width))
        lane = lax.broadcasted_iota(jnp.int32, (1, width), 1)
        real_side = lane < width // 2
        keep_real = jnp.logical_or(real_side, jnp.logical_not(jnp.logical_and(has_first, step == 0)))
        keep_imaginary = jnp.logical_or(jnp.logical_not(real_side), step < depth)
        keep = jnp.logical_and(keep_real, keep_imaginary).astype(jnp.float32)
        lines = jnp.concatenate([piece * keep for piece in pieces], axis=1)
        along_y = times_right(lines, y_table[...])
        rows_y = along_y.shape[1] // 2
        stacked = jnp.concatenate([along_y[:, :rows_y], along_y[:, rows_y:]], axis=0)
        spectrum[...] = times_left(x_table_ref[...], stacked)


def plane_forward(start, received):
    slabs, pens, count, depth, _, width = received[0].shape
    size_x = slabs * sum(cells.shape[4] for cells in received)
    size_y = pens * (width // 2)
    y_table = right_table(y_forward_table(size_y, pens))
    x_matrix = left_table(x_table(size_x, -1.0))
    return pl.pallas_call(
        plane_forward_kernel,
        grid=(count, depth + 1),
        in_specs=[pl.BlockSpec(memory_space=pltpu.SMEM)]
        + [
            pl.BlockSpec(
                (slabs, pens, None, None, cells.shape[4], width),
                lambda c, j: (0, 0, c, jnp.where(j < depth, j, 0), 0, 0),
            )
            for cells in received
        ]
        + [
            pl.BlockSpec(y_table.shape, lambda c, j: (0, 0)),
            pl.BlockSpec(x_matrix.shape, lambda c, j: (0, 0)),
        ],
        out_specs=pl.BlockSpec((None, None, 2 * size_x, size_y), lambda c, j: (c, j, 0, 0)),
        out_shape=jax.ShapeDtypeStruct((count, depth + 1, 2 * size_x, size_y), jnp.float32),
        compiler_params=vmem(),
        cost_estimate=cost(
            24 * count * depth * size_x * size_y * (size_x + size_y),
            4 * count * depth * size_x * size_y * 4,
        ),
        name="plane_forward",
    )(start, *received, y_table, x_matrix)


def wave_pair(shape, dim, length):
    index = lax.broadcasted_iota(jnp.int32, shape, dim)
    signed_index = jnp.where(index < length // 2, index, index - length)
    full_wave = (2.0 * math.pi / length) * signed_index.astype(jnp.float32)
    return full_wave, jnp.where(index == length // 2, 0.0, full_wave)


def plane_inverse_kernel(parts, needs, start, *refs):
    spectra = dict(zip(needs, refs[: len(needs)]))
    extras = dict(zip(needs, refs[len(needs) : 2 * len(needs)]))
    y_table, x_table_ref = refs[2 * len(needs) : 2 * len(needs) + 2]
    backs, turned = refs[2 * len(needs) + 2 : -1], refs[-1]
    step = pl.program_id(0)
    size_x, size_y = turned.shape[1] // 2, turned.shape[2]
    full_x, curl_x = wave_pair((size_x, 1), 0, size_x)
    full_y, curl_y = wave_pair((1, size_y), 1, size_y)

    def curl(part, source, full_z, curl_z):
        curls = (curl_x, curl_y, curl_z)
        wave_left, wave_right = curls[(part + 1) % 3], curls[(part + 2) % 3]
        left, right = source[(part + 1) % 3], source[(part + 2) % 3]
        wave_squared = full_x * full_x + full_y * full_y + full_z * full_z
        present = wave_squared > 0.0
        scaling = jnp.where(present, 1.0 / jnp.where(present, wave_squared, 1.0), 0.0)
        scaling = scaling * (1.0 / float(size_x * size_y * NZ))
        real_part = wave_left * right[:size_x] - wave_right * left[:size_x]
        imaginary = wave_left * right[size_x:] - wave_right * left[size_x:]
        return -imaginary * scaling, real_part * scaling

    index_z = (start[0] + step).astype(jnp.float32)
    wave_z = (2.0 * math.pi / NZ) * index_z
    for at, part in enumerate(parts):
        real_part, imaginary = curl(part, spectra, wave_z, wave_z)
        turned[at, :size_x] = real_part
        turned[at, size_x:] = imaginary

    @pl.when(jnp.logical_and(start[0] == 0, step == 0))
    def _():
        for at, part in enumerate(parts):
            extra_real, extra_imaginary = curl(part, extras, -math.pi, 0.0)
            turned[at, :size_x] += extra_real
            turned[at, size_x:] += extra_imaginary

    slabs, pens, planes, width = backs[0].shape
    for at, back in enumerate(backs):
        along_x = times_left(x_table_ref[...], turned[at])
        lines = jnp.concatenate([along_x[:size_x], along_x[size_x:]], axis=1)
        result = times_right(lines, y_table[...])
        for pen in range(pens):
            piece = result[:, pen * width : (pen + 1) * width]
            back[:, pen] = piece.reshape(slabs, planes, width)


def plane_inverse(parts, start, spectra, shape):
    slabs, pens, depth, planes, width = shape
    count = len(parts)
    size_x = slabs * planes
    size_y = pens * (width // 2)
    y_table = right_table(y_inverse_table(size_y, pens))
    x_matrix = left_table(x_table(size_x, 1.0))
    needs = [c for c in range(3) if any(c != part for part in parts)]

    def at(index, extra):
        return pl.BlockSpec(
            (None, None, 2 * size_x, size_y),
            lambda j: (index, depth if extra else j, 0, 0),
        )

    return pl.pallas_call(
        functools.partial(plane_inverse_kernel, parts, needs),
        grid=(depth,),
        in_specs=[pl.BlockSpec(memory_space=pltpu.SMEM)]
        + [at(spectra[c][1], False) for c in needs]
        + [at(spectra[c][1], True) for c in needs]
        + [
            pl.BlockSpec(y_table.shape, lambda j: (0, 0)),
            pl.BlockSpec(x_matrix.shape, lambda j: (0, 0)),
        ],
        out_specs=[
            pl.BlockSpec((slabs, pens, None, planes, width), lambda j: (0, 0, j, 0, 0))
        ]
        * count,
        out_shape=[jax.ShapeDtypeStruct(shape, jnp.float32)] * count,
        scratch_shapes=[pltpu.VMEM((count, 2 * size_x, size_y), jnp.float32)],
        compiler_params=vmem(),
        cost_estimate=cost(
            24 * count * depth * size_x * size_y * (size_x + size_y),
            6 * count * depth * size_x * size_y * 4,
        ),
        name="plane_inverse",
    )(start, *([spectra[c][0] for c in needs] * 2), y_table, x_matrix)


def z_difference_table():
    table = np.zeros((NZ, NZ), np.float32)
    for cell in range(NZ):
        for shift, weight in ((1, 8.0), (-1, -8.0), (2, -1.0), (-2, 1.0)):
            table[(cell + shift) % NZ, cell] += weight
    table = table.astype(jnp.bfloat16)
    return jnp.asarray(np.concatenate([table, table], axis=0))


def stretch_kernel(vorticity, field, before, after, low_x, high_x, low_y, high_y, table, *refs):
    velocity, stretching, padded = refs[-3:]
    step = pl.program_id(0)
    rows_local = field.shape[1]
    first = step == 0
    last = step == pl.num_programs(0) - 1
    own = slice(8, 8 + rows_local)
    for plane in range(STEP):
        padded[plane, own, :] = field[plane]
        padded[plane, 6:8, :] = low_y[plane]
        padded[plane, 8 + rows_local : 10 + rows_local, :] = high_y[plane]
    high, low = split_values(field[...].reshape(STEP * rows_local, NZ))
    along_z = jnp.dot(
        jnp.concatenate([high, low], axis=1), table[...], preferred_element_type=jnp.float32
    )

    def difference(ahead, behind, ahead_2, behind_2):
        return 8.0 * (ahead - behind) - (ahead_2 - behind_2)

    def along(plane):
        if plane < 0:
            return jnp.where(first, low_x[plane + 2], before[plane + 2])
        if plane >= STEP:
            return jnp.where(last, high_x[plane - STEP], after[plane - STEP])
        return field[plane]

    for plane in range(STEP):
        velocity[0, plane] = field[plane]
        along_x = difference(*(along(plane + shift) for shift in (1, -1, 2, -2)))
        along_y = difference(
            *(padded[plane, 8 + shift : 8 + shift + rows_local, :] for shift in (1, -1, 2, -2))
        )
        total = vorticity[0, plane] * along_x + vorticity[1, plane] * along_y
        total = total + vorticity[2, plane] * along_z[plane * rows_local : (plane + 1) * rows_local]
        stretching[0, plane] = total * (1.0 / 12.0)


def stretch(part, vorticity, field, halos, outputs):
    planes, rows_local, _ = field.shape
    pairs = STEP // 2
    table = z_difference_table()
    layer = pl.BlockSpec((2, rows_local, NZ), lambda i: (0, 0, 0))
    edge = pl.BlockSpec((STEP, 2, NZ), lambda i: (i, 0, 0))
    block = pl.BlockSpec((1, STEP, rows_local, NZ), lambda i: (part, i, 0, 0))
    specs = [
        pl.BlockSpec((3, STEP, rows_local, NZ), lambda i: (0, i, 0, 0)),
        pl.BlockSpec((STEP, rows_local, NZ), lambda i: (i, 0, 0)),
        pl.BlockSpec((2, rows_local, NZ), lambda i: (jnp.maximum(i * pairs - 1, 0), 0, 0)),
        pl.BlockSpec(
            (2, rows_local, NZ), lambda i: (jnp.minimum((i + 1) * pairs, planes // 2 - 1), 0, 0)
        ),
        layer,
        layer,
        edge,
        edge,
        pl.BlockSpec(table.shape, lambda i: (0, 0)),
    ]
    operands = [vorticity, field, field, field, *halos, table]
    aliases = {}
    if outputs is not None:
        aliases = {len(operands): 0, len(operands) + 1: 1}
        specs += [pl.BlockSpec(memory_space=pl.ANY)] * 2
        operands += list(outputs)
    shape = jax.ShapeDtypeStruct((3, planes, rows_local, NZ), jnp.float32)
    return pl.pallas_call(
        stretch_kernel,
        grid=(planes // STEP,),
        in_specs=specs,
        out_specs=(block, block),
        out_shape=(shape, shape),
        input_output_aliases=aliases,
        scratch_shapes=[pltpu.VMEM((STEP, rows_local + 16, NZ), jnp.float32)],
        compiler_params=vmem(),
        cost_estimate=cost(600 * planes * rows_local * NZ, 7 * planes * rows_local * NZ * 4),
        name="stretch",
    )(*operands)


def per_device(counts, row_base, z_base, fractions, strength):
    slabs, pens = lax.axis_size("slab"), lax.axis_size("pen")
    devices = slabs * pens
    depth = HALF // devices
    planes, blocks, _ = row_base.shape
    rows_local = blocks * BLOCK_ROWS
    width = 2 * rows_local
    place = lax.axis_index("slab") * pens + lax.axis_index("pen")
    start = (place * depth).astype(jnp.int32).reshape(1)
    shape = (devices, depth, planes, width)

    def exchange(blocks_out, after=None):
        if after is not None:
            blocks_out, _ = lax.optimization_barrier((blocks_out, after))
        return lax.all_to_all(blocks_out, AXES, 0, 0, tiled=True)

    def unfold(received):
        return received.reshape((slabs, pens) + received.shape[1:])

    cut = planes - STEP
    particles = (counts, row_base, z_base, fractions, strength)
    grid, ghost_y, ghost_x, ghost_xy = deposit(particles, cut, planes)
    tail = (grid, next_over(ghost_y, ("pen",)))
    ghosts_x = (next_over(ghost_x, ("slab",)), next_over(ghost_xy, ("slab", "pen")))
    everything = (cut, planes)
    if cut == 0:
        vorticity, send = z_forward((1, 2), everything, tail, ghosts_x, None, None, shape)
        received = [exchange(send)]
        vorticity, send = z_forward((0,), everything, tail, ghosts_x, vorticity, None, shape)
    else:
        vorticity, send = z_forward((1, 2), everything, tail, None, None, None, shape)
        held, _ = lax.optimization_barrier((particles, send))
        grid, ghost_y = deposit(held, 0, cut)
        head = (grid, next_over(ghost_y, ("pen",)))
        received = [exchange(send)]
        vorticity, send = z_forward((1, 2), (0, cut), head, ghosts_x, vorticity, None, shape)
        received = [exchange(send, received[0])] + received
        vorticity, send = z_forward((0,), (0, cut), head, ghosts_x, vorticity, NEW, shape)
        vorticity, send = z_forward((0,), everything, tail, None, vorticity, send, shape)
    pair = plane_forward(start, [unfold(cells) for cells in received])
    single = plane_forward(start, [unfold(exchange(send, received[0]))])
    spectra = {1: (pair, 0), 2: (pair, 1), 0: (single, 0)}

    shape = (slabs, pens, depth, planes, width)
    backs = plane_inverse((0,), start, spectra, shape) + plane_inverse((1, 2), start, spectra, shape)
    outputs = received = None
    for part, back in enumerate(backs):
        received = exchange(back.reshape(devices, depth, planes, width), received)
        field, low_x, high_x, low_y, high_y = z_inverse(received)
        halos = (
            shifted(high_x, "slab", 1),
            shifted(low_x, "slab", -1),
            shifted(high_y, "pen", 1),
            shifted(low_y, "pen", -1),
        )
        outputs = stretch(part, vorticity, field, halos, outputs)
    return (vorticity, outputs[0], outputs[1])


def solution(mesh):
    in_specs = (
        P("slab", "pen"),
        P("slab", "pen", None),
        P("slab", "pen", None),
        P(None, "slab", "pen", None),
        P(None, "slab", "pen", None),
    )
    out_specs = (
        P(None, "slab", "pen", None),
        P(None, "slab", "pen", None),
        P(None, "slab", "pen", None),
    )
    return jax.shard_map(
        per_device, mesh=mesh, in_specs=in_specs, out_specs=out_specs, check_vma=False
    )
```

time: 409 us -> 395 us (0.966)
  waiting for transfers between devices: 223 us -> 140 us
  blocking collectives: 0 us -> 53.2 us
  starting transfers between devices: 38.1 us -> 52.8 us
  Pallas kernels: 129 us -> 119 us
  local copies, waits for them, and re-layouts: 14.3 us -> 24.2 us
    ppermute x8 -> x12, waiting for transfers between devices: 94.1 us -> 32.3 us  [shifted(): lax.ppermute(block, axis, [(i, (i + distance) % count) for i in range(cou...]
    all_to_all x0 -> x1, blocking collectives: none -> 53.2 us  [exchange(): return lax.all_to_all(blocks_out, AXES, 0, 0, tiled=True)]
    all_to_all x4 -> x5, waiting for transfers between devices: 129 us -> 106 us  [exchange(): return lax.all_to_all(blocks_out, AXES, 0, 0, tiled=True)]
    pallas_call x8 -> x12, Pallas kernels: 85 us -> 74.5 us  [the longest x2 32.9 us: deposit(): pl.pallas_call(functools.partial(deposit_kernel, begin, end), out_shape=[...]
    unnamed x29 -> x63, local copies, waits for them, and re-layouts: 14.3 us -> 24.1 us
    all_to_all x4 -> x5, starting transfers between devices: 24.6 us -> 32.3 us  [exchange(): return lax.all_to_all(blocks_out, AXES, 0, 0, tiled=True)]
    ppermute x8 -> x12, starting transfers between devices: 9.39 us -> 15 us  [shifted(): lax.ppermute(block, axis, [(i, (i + distance) % count) for i in range(cou...]
  transfers between devices with their start and end apart: 15 -> 21, of which waited for: 9 -> 7; matrix products, arithmetic and copies ran while one was open for 0% -> 0% of each run, Pallas kernels for 21% -> 26%
where the time goes in v3:
time: 395 us; the launch traced here: 390 us
  waiting for transfers between devices  140 us (35%)
  Pallas kernels  119 us (30%)
  blocking collectives  53.2 us (13%)
  starting transfers between devices  52.8 us (13%)
  local copies, waits for them, and re-layouts  24.2 us (6%)
    all_to_all x5, waiting for transfers between devices, exchange(): return lax.all_to_all(blocks_out, AXES, 0, 0, tiled=True)  106 us
    all_to_all x1, blocking collectives, exchange(): return lax.all_to_all(blocks_out, AXES, 0, 0, tiled=True)  53.2 us
    pallas_call x2, Pallas kernels, deposit(): pl.pallas_call(functools.partial(deposit_kernel, begin, end), out_shape=[...  32.9 us
    ppermute x12, waiting for transfers between devices, shifted(): lax.ppermute(block, axis, [(i, (i + distance) % count) for i in range(cou...  32.3 us
    all_to_all x5, starting transfers between devices, exchange(): return lax.all_to_all(blocks_out, AXES, 0, 0, tiled=True)  32.3 us
    pallas_call x2, Pallas kernels, plane_inverse(): pl.pallas_call(functools.partial(plane_inverse_kernel, parts, needs), gri...  24.5 us
    unnamed x63, local copies, waits for them, and re-layouts  24.1 us
    pallas_call x2, Pallas kernels, plane_forward(): pl.pallas_call(plane_forward_kernel, grid=(count, depth + 1), in_specs=[p...  19.6 us
  transfers between devices with their start and end apart: 21, of which 7 were waited for; matrix products, arithmetic and copies ran while one was open for 0% of the time, Pallas kernels for 26%

profile of v3, /device:TPU:17, one launch (start us, length us, event | category | flops | bytes accessed | tf_op | source)
XLA Modules:
  0.0 390.0 jit_solution(6451658842677682112)
XLA Ops:
  5.6 10.1 %deposit.2 = (f32[3,11,72,256]{3,2,1,0:T(8,128)S(1)}, f32[3,8,3,256]{3,2,1,0:T(4,128)S(1)}, f32[3,3,64,256]{3,2,1,0:T(8,128)}, f32[3,3,3,256]{3,2,1,0:T(4,128)S(1)}) custom-call(s32[32,4]{1,0:T(8,128)S(1)} %copy.34.counts, s32[32,4,512]{2,1,0:T(4,128)S(1)} %copy-done.17, s32[32,4,512]{2,1,0:T(4,128)S(1)} %copy-done.19, f32[3,32,4,512]{3,2,1,0:T(4,128)S(1)} %copy-done.13, ...), custom_call_target="tpu_custom_call" | custom-call | flops 16609443840 | bytes 12582912 | tf_op jit(solution)/shard_map/deposit/pallas_call | solution.py:264
  21.5 7.1 %all-to-all-start = ((f32[32,2,4,8,128]{4,3,2,1,0:T(8,128)}), f32[32,2,4,8,128]{4,3,2,1,0:T(8,128)}, u32[]{:S(2)}, u32[]{:S(2)}) async-start(f32[32,2,4,8,128]{4,3,2,1,0:T(8,128)} %copy-done.12), calls=%async_computation | async-start | bytes 2097152 | tf_op jit(solution)/shard_map/all_to_all | solution.py:691
  33.0 22.8 %deposit.3 = (f32[3,24,72,256]{3,2,1,0:T(8,128)}, f32[3,24,3,256]{3,2,1,0:T(4,128)S(1)}) custom-call(s32[32,4]{1,0:T(8,128)S(1)} %copy.35.counts, s32[32,4,512]{2,1,0:T(4,128)S(1)} %copy-done.18, s32[32,4,512]{2,1,0:T(4,128)S(1)} %copy-done.20, f32[3,32,4,512]{3,2,1,0:T(4,128)S(1)} %copy-done.14, f32[3,32,4,512]{3,2,1,0:T(4,128)S(1)} %copy-done.16), custom_call_target="tpu_custom_call" | custom-call | flops 36238786560 | bytes 12582912 | tf_op jit(solution)/shard_map/deposit/pallas_call | solution.py:264
  60.3 6.1 %z_forward.5 = (f32[3,32,64,256]{3,2,1,0:T(8,128)}, f32[32,2,4,24,128]{4,3,2,1,0:T(8,128)S(1)}) custom-call(f32[3,24,72,256]{3,2,1,0:T(8,128)} %get-tuple-element.57.refs_0_, f32[3,24,3,256]{3,2,1,0:T(4,128)S(1)} %collective-permute-done.1.refs_1_, f32[3,3,64,256]{3,2,1,0:T(8,128)S(1)} %collective-permute-done.2.refs_2_, ...), custom_call_target="tpu_custom_call", output_to_operand_aliasing={{0}: (5, {})} | custom-call | flops 1207959552 | bytes 9437184 | tf_op jit(solution)/shard_map/z_forward/pallas_call | solution.py:359
  68.7 8.1 %all-to-all-start.1 = ((f32[32,2,4,24,128]{4,3,2,1,0:T(8,128)}), f32[32,2,4,24,128]{4,3,2,1,0:T(8,128)}, u32[]{:S(2)}, u32[]{:S(2)}) async-start(f32[32,2,4,24,128]{4,3,2,1,0:T(8,128)} %copy-done.6), calls=%async_computation.1 | async-start | bytes 6291456 | tf_op jit(solution)/shard_map/all_to_all | solution.py:691
  77.8 3.8 z_forward.6
  83.8 62.1 %all-to-all-done.1 = f32[32,2,4,24,128]{4,3,2,1,0:T(8,128)} async-done(((f32[32,2,4,24,128]{4,3,2,1,0:T(8,128)}), f32[32,2,4,24,128]{4,3,2,1,0:T(8,128)}, u32[]{:S(2)}, u32[]{:S(2)}) %all-to-all-start.1) | async-done | bytes 3145760 | tf_op jit(solution)/shard_map/all_to_all | solution.py:691
  146.0 6.4 %all-to-all-start.2 = ((f32[32,1,4,32,128]{4,3,2,1,0:T(8,128)}), f32[32,1,4,32,128]{4,3,2,1,0:T(8,128)}, u32[]{:S(2)}, u32[]{:S(2)}) async-start(f32[32,1,4,32,128]{4,3,2,1,0:T(8,128)} %copy-done.2), calls=%async_computation.2 | async-start | bytes 4194304 | tf_op jit(solution)/shard_map/all_to_all | solution.py:691
  155.2 12.9 %plane_forward.3.refs_1_.refs_2_.refs_4_.refs_5_.refs_0_.refs_3_ = f32[2,5,512,256]{3,2,1,0:T(8,128)} custom-call(s32[1]{0:T(128)} %bitcast.start, f32[8,4,2,4,24,128]{5,4,3,2,1,0:T(8,128)} %bitcast.2.refs_0_, f32[8,4,2,4,8,128]{5,4,3,2,1,0:T(8,128)} %bitcast.3.refs_1_, bf16[1536,512]{1,0:T(8,128)(2,1)S(1)} %copy-done.25, bf16[512,1536]{1,0:T(8,128)(2,1)S(1)} %copy-done.23), custom_call_target="tpu_custom_call" | custom-call | flops 6442450944 | bytes 8388608 | tf_op jit(solution)/shard_map/plane_forward/pallas_call | solution.py:471
  168.1 10.2 %plane_inverse.3 = f32[8,4,4,32,128]{4,3,2,1,0:T(8,128)} custom-call(s32[1]{0:T(128)} %bitcast.start, f32[2,5,512,256]{3,2,1,0:T(8,128)} %plane_forward.3.refs_1_.refs_2_.refs_4_.refs_5_.refs_0_.refs_3_, f32[2,5,512,256]{3,2,1,0:T(8,128)} %plane_forward.3.refs_1_.refs_2_.refs_4_.refs_5_.refs_0_.refs_3_, ...), custom_call_target="tpu_custom_call" | custom-call | flops 3221225472 | bytes 6291456 | tf_op jit(solution)/shard_map/plane_inverse/pallas_call | solution.py:565
  178.3 21.4 %all-to-all-done.2 = f32[32,1,4,32,128]{4,3,2,1,0:T(8,128)} async-done(((f32[32,1,4,32,128]{4,3,2,1,0:T(8,128)}), f32[32,1,4,32,128]{4,3,2,1,0:T(8,128)}, u32[]{:S(2)}, u32[]{:S(2)}) %all-to-all-start.2) | async-done | bytes 2097184 | tf_op jit(solution)/shard_map/all_to_all | solution.py:691
  199.7 5.7 %all-to-all-start.3 = ((f32[32,4,32,128]{3,2,1,0:T(8,128)}), f32[32,4,32,128]{3,2,1,0:T(8,128)}, u32[]{:S(2)}, u32[]{:S(2)}) async-start(f32[32,4,32,128]{3,2,1,0:T(8,128)} %bitcast.6), calls=%async_computation.3 | async-start | bytes 4194304 | tf_op jit(solution)/shard_map/all_to_all | solution.py:691
  208.2 6.7 %plane_forward.2.refs_0_.refs_3_ = f32[1,5,512,256]{3,2,1,0:T(8,128)} custom-call(s32[1]{0:T(128)} %bitcast.start, f32[8,4,1,4,32,128]{5,4,3,2,1,0:T(8,128)} %bitcast.1.refs_0_, bf16[1536,512]{1,0:T(8,128)(2,1)S(1)} %copy-done.26, bf16[512,1536]{1,0:T(8,128)(2,1)S(1)} %copy-done.24), custom_call_target="tpu_custom_call" | custom-call | flops 3221225472 | bytes 4194304 | tf_op jit(solution)/shard_map/plane_forward/pallas_call | solution.py:471
  214.9 14.3 %plane_inverse.2 = (f32[8,4,4,32,128]{4,3,2,1,0:T(8,128)S(1)}, f32[8,4,4,32,128]{4,3,2,1,0:T(8,128)}) custom-call(s32[1]{0:T(128)} %bitcast.start, f32[1,5,512,256]{3,2,1,0:T(8,128)} %plane_forward.2.refs_0_.refs_3_, f32[2,5,512,256]{3,2,1,0:T(8,128)} %plane_forward.3.refs_1_.refs_2_.refs_4_.refs_5_.refs_0_.refs_3_, ...), custom_call_target="tpu_custom_call" | custom-call | flops 6442450944 | bytes 12582912 | tf_op jit(solution)/shard_map/plane_inverse/pallas_call | solution.py:565
  230.6 22.2 %all-to-all-done.3.received = f32[32,4,32,128]{3,2,1,0:T(8,128)} async-done(((f32[32,4,32,128]{3,2,1,0:T(8,128)}), f32[32,4,32,128]{3,2,1,0:T(8,128)}, u32[]{:S(2)}, u32[]{:S(2)}) %all-to-all-start.3) | async-done | bytes 2097184 | tf_op jit(solution)/shard_map/all_to_all | solution.py:691
  252.7 53.2 %all_to_all.30.received = f32[32,4,32,128]{3,2,1,0:T(8,128)} all-to-all(f32[32,4,32,128]{3,2,1,0:T(8,128)} %bitcast.7), channel_id=1, replica_groups=mesh['slab'=8,'pen'=4] {'slab','pen'}, dimensions={0} | all-to-all | bytes 4194304 | tf_op jit(solution)/shard_map/all_to_all | solution.py:691
  305.9 5.0 %all-to-all-start.5 = ((f32[32,4,32,128]{3,2,1,0:T(8,128)}), f32[32,4,32,128]{3,2,1,0:T(8,128)}, u32[]{:S(2)}, u32[]{:S(2)}) async-start(f32[32,4,32,128]{3,2,1,0:T(8,128)} %bitcast.4), calls=%async_computation.5 | async-start | bytes 4194304 | tf_op jit(solution)/shard_map/all_to_all | solution.py:691
  310.9 3.7 z_inverse.5
  318.8 2.9 z_inverse.4
  329.7 31.3 %collective-permute-done.12.low_x = f32[2,64,256]{2,1,0:T(8,128)S(1)} collective-permute-done((f32[2,64,256]{2,1,0:T(8,128)S(1)}, f32[2,64,256]{2,1,0:T(8,128)S(1)}, u32[]{:S(2)}, u32[]{:S(2)}) %collective-permute-start.12) | collective-permute-done | bytes 131104 | tf_op jit(solution)/shard_map/ppermute | solution.py:297
  362.1 3.5 z_inverse.3
  370.8 6.5 %stretch.3 = (f32[3,32,64,256]{3,2,1,0:T(8,128)}, f32[3,32,64,256]{3,2,1,0:T(8,128)}) custom-call(f32[3,32,64,256]{3,2,1,0:T(8,128)} %get-tuple-element.46.vorticity, f32[32,64,256]{2,1,0:T(8,128)S(1)} %get-tuple-element.84.field.before.after, f32[32,64,256]{2,1,0:T(8,128)S(1)} %get-tuple-element.84.field.before.after, ...), custom_call_target="tpu_custom_call" | custom-call | flops 314572800 | bytes 14680064 | tf_op jit(solution)/shard_map/stretch/pallas_call | solution.py:663
  377.3 6.3 %stretch.4 = (f32[3,32,64,256]{3,2,1,0:T(8,128)}, f32[3,32,64,256]{3,2,1,0:T(8,128)}) custom-call(f32[3,32,64,256]{3,2,1,0:T(8,128)} %get-tuple-element.46.vorticity, f32[32,64,256]{2,1,0:T(8,128)S(1)} %copy-done.1, f32[32,64,256]{2,1,0:T(8,128)S(1)} %copy-done.1, f32[32,64,256]{2,1,0:T(8,128)S(1)} %copy-done.1, ...), custom_call_target="tpu_custom_call", output_to_operand_aliasing={{0}: (9, {}), {1}: (10, {})} | custom-call | flops 314572800 | bytes 14680064 | tf_op jit(solution)/shard_map/stretch/pallas_call | solution.py:663
  383.7 6.3 %stretch.5 = (f32[3,32,64,256]{3,2,1,0:T(8,128)}, f32[3,32,64,256]{3,2,1,0:T(8,128)}) custom-call(f32[3,32,64,256]{3,2,1,0:T(8,128)} %get-tuple-element.46.vorticity, f32[32,64,256]{2,1,0:T(8,128)S(1)} %get-tuple-element.74.field.before.after, ...), custom_call_target="tpu_custom_call", output_to_operand_aliasing={{0}: (9, {}), {1}: (10, {})} | custom-call | flops 314572800 | bytes 14680064 | tf_op jit(solution)/shard_map/stretch/pallas_call | solution.py:663
  (99 shorter events, 50.4 us)
Async XLA Ops:
  5.6 13.5 %copy-start.3 = (bf16[768,256]{1,0:T(8,128)(2,1)S(1)}, bf16[768,256]{1,0:T(8,128)(2,1)}, u32[]{:S(2)}) copy-start(bf16[768,256]{1,0:T(8,128)(2,1)} %constant.25.clone.refs_2_.refs_4_) | copy-start | bytes 1179652
  15.7 3.3 collective-permute-start
  17.4 42.9 %collective-permute-start.2 = (f32[3,3,64,256]{3,2,1,0:T(8,128)}, f32[3,3,64,256]{3,2,1,0:T(8,128)S(1)}, u32[]{:S(2)}, u32[]{:S(2)}) collective-permute-start(f32[3,3,64,256]{3,2,1,0:T(8,128)} %get-tuple-element.59), channel_id=1, source_target_pairs={{0,4},{1,5},{2,6},{3,7},{4,8},{5,9},{6,10},{7,11},{8,12},{9,13},{1... | collective-permute-start | bytes 1769480 | tf_op jit(solution)/shard_map/ppermute | solution.py:292
  21.5 47.2 %all-to-all-start = ((f32[32,2,4,8,128]{4,3,2,1,0:T(8,128)}), f32[32,2,4,8,128]{4,3,2,1,0:T(8,128)}, u32[]{:S(2)}, u32[]{:S(2)}) async-start(f32[32,2,4,8,128]{4,3,2,1,0:T(8,128)} %copy-done.12), calls=%async_computation | async-start | bytes 2097152 | tf_op jit(solution)/shard_map/all_to_all | solution.py:691
  33.0 22.9 %copy-start.22 = (f32[3,3,3,256]{3,2,1,0:T(4,128)S(1)}, f32[3,3,3,256]{3,2,1,0:T(4,128)}, u32[]{:S(2)}) copy-start(f32[3,3,3,256]{3,2,1,0:T(4,128)} %copy-done.21) | copy-start | bytes 82948
  55.8 4.5 %collective-permute-start.1 = (f32[3,24,3,256]{3,2,1,0:T(4,128)S(1)}, f32[3,24,3,256]{3,2,1,0:T(4,128)S(1)}, u32[]{:S(2)}, u32[]{:S(2)}) collective-permute-start(f32[3,24,3,256]{3,2,1,0:T(4,128)S(1)} %get-tuple-element.58), channel_id=1, source_target_pairs={{0,1},{1,2},{2,3},{3,0},{4,5},{5,6},{6,7},{7,4},{8,9},{9,10},{10,1... | collective-permute-start | bytes 663560 | tf_op jit(solution)/shard_map/ppermute | solution.py:292
  55.8 4.4 %collective-permute-start.3 = (f32[3,3,3,256]{3,2,1,0:T(4,128)S(1)}, f32[3,3,3,256]{3,2,1,0:T(4,128)S(1)}, u32[]{:S(2)}, u32[]{:S(2)}) collective-permute-start(f32[3,3,3,256]{3,2,1,0:T(4,128)S(1)} %copy-done.22), channel_id=1, source_target_pairs={{0,5},{1,6},{2,7},{3,4},{4,9},{5,10},{6,11},{7,8},{8,13},{9,14},{1... | collective-permute-start | bytes 82952 | tf_op jit(solution)/shard_map/ppermute | solution.py:292
  68.7 77.2 %all-to-all-start.1 = ((f32[32,2,4,24,128]{4,3,2,1,0:T(8,128)}), f32[32,2,4,24,128]{4,3,2,1,0:T(8,128)}, u32[]{:S(2)}, u32[]{:S(2)}) async-start(f32[32,2,4,24,128]{4,3,2,1,0:T(8,128)} %copy-done.6), calls=%async_computation.1 | async-start | bytes 6291456 | tf_op jit(solution)/shard_map/all_to_all | solution.py:691
  146.0 53.7 %all-to-all-start.2 = ((f32[32,1,4,32,128]{4,3,2,1,0:T(8,128)}), f32[32,1,4,32,128]{4,3,2,1,0:T(8,128)}, u32[]{:S(2)}, u32[]{:S(2)}) async-start(f32[32,1,4,32,128]{4,3,2,1,0:T(8,128)} %copy-done.2), calls=%async_computation.2 | async-start | bytes 4194304 | tf_op jit(solution)/shard_map/all_to_all | solution.py:691
  199.7 53.0 %all-to-all-start.3 = ((f32[32,4,32,128]{3,2,1,0:T(8,128)}), f32[32,4,32,128]{3,2,1,0:T(8,128)}, u32[]{:S(2)}, u32[]{:S(2)}) async-start(f32[32,4,32,128]{3,2,1,0:T(8,128)} %bitcast.6), calls=%async_computation.3 | async-start | bytes 4194304 | tf_op jit(solution)/shard_map/all_to_all | solution.py:691
  305.9 55.2 %all-to-all-start.5 = ((f32[32,4,32,128]{3,2,1,0:T(8,128)}), f32[32,4,32,128]{3,2,1,0:T(8,128)}, u32[]{:S(2)}, u32[]{:S(2)}) async-start(f32[32,4,32,128]{3,2,1,0:T(8,128)} %bitcast.4), calls=%async_computation.5 | async-start | bytes 4194304 | tf_op jit(solution)/shard_map/all_to_all | solution.py:691
  314.7 46.4 %collective-permute-start.12 = (f32[2,64,256]{2,1,0:T(8,128)S(1)}, f32[2,64,256]{2,1,0:T(8,128)S(1)}, u32[]{:S(2)}, u32[]{:S(2)}) collective-permute-start(f32[2,64,256]{2,1,0:T(8,128)S(1)} %get-tuple-element.85), channel_id=1, source_target_pairs={{0,4},{4,8},{8,12},{12,16},{16,20},{20,24},{24,28},{28,0},{1,5},{5... | collective-permute-start | bytes 393224 | tf_op jit(solution)/shard_map/ppermute | solution.py:297
  315.9 9.1 %collective-permute-start.14 = (f32[32,2,256]{2,1,0:T(2,128)S(1)}, f32[32,2,256]{2,1,0:T(2,128)S(1)}, u32[]{:S(2)}, u32[]{:S(2)}) collective-permute-start(f32[32,2,256]{2,1,0:T(2,128)S(1)} %get-tuple-element.87), channel_id=1, source_target_pairs={{0,1},{1,2},{2,3},{3,0},{4,5},{5,6},{6,7},{7,4},{8,9},{9,10},{10,1... | collective-permute-start | bytes 196616 | tf_op jit(solution)/shard_map/ppermute | solution.py:297
  317.6 10.1 %collective-permute-start.15 = (f32[32,2,256]{2,1,0:T(2,128)S(1)}, f32[32,2,256]{2,1,0:T(2,128)S(1)}, u32[]{:S(2)}, u32[]{:S(2)}) collective-permute-start(f32[32,2,256]{2,1,0:T(2,128)S(1)} %get-tuple-element.88), channel_id=1, source_target_pairs={{0,3},{1,0},{2,1},{3,2},{4,7},{5,4},{6,5},{7,6},{8,11},{9,8},{10,9... | collective-permute-start | bytes 196616 | tf_op jit(solution)/shard_map/ppermute | solution.py:297
  317.6 53.2 %copy-start.7 = (bf16[512,256]{1,0:T(8,128)(2,1)S(1)}, bf16[512,256]{1,0:T(8,128)(2,1)}, u32[]{:S(2)}) copy-start(bf16[512,256]{1,0:T(8,128)(2,1)} %constant.31.clone.table) | copy-start | bytes 786436
  317.6 48.0 %collective-permute-start.13 = (f32[2,64,256]{2,1,0:T(8,128)S(1)}, f32[2,64,256]{2,1,0:T(8,128)S(1)}, u32[]{:S(2)}, u32[]{:S(2)}) collective-permute-start(f32[2,64,256]{2,1,0:T(8,128)S(1)} %get-tuple-element.86), channel_id=1, source_target_pairs={{0,28},{4,0},{8,4},{12,8},{16,12},{20,16},{24,20},{28,24},{1,29},{... | collective-permute-start | bytes 393224 | tf_op jit(solution)/shard_map/ppermute | solution.py:297
  323.0 44.4 %collective-permute-start.10 = (f32[32,2,256]{2,1,0:T(2,128)}, f32[32,2,256]{2,1,0:T(2,128)S(1)}, u32[]{:S(2)}, u32[]{:S(2)}) collective-permute-start(f32[32,2,256]{2,1,0:T(2,128)} %get-tuple-element.82), channel_id=1, source_target_pairs={{0,1},{1,2},{2,3},{3,0},{4,5},{5,6},{6,7},{7,4},{8,9},{9,10},{10,1... | collective-permute-start | bytes 196616 | tf_op jit(solution)/shard_map/ppermute | solution.py:297
  325.0 43.0 %collective-permute-start.11 = (f32[32,2,256]{2,1,0:T(2,128)}, f32[32,2,256]{2,1,0:T(2,128)S(1)}, u32[]{:S(2)}, u32[]{:S(2)}) collective-permute-start(f32[32,2,256]{2,1,0:T(2,128)} %get-tuple-element.83), channel_id=1, source_target_pairs={{0,3},{1,0},{2,1},{3,2},{4,7},{5,4},{6,5},{7,6},{8,11},{9,8},{10,9... | collective-permute-start | bytes 196616 | tf_op jit(solution)/shard_map/ppermute | solution.py:297
  327.7 43.1 %collective-permute-start.8 = (f32[2,64,256]{2,1,0:T(8,128)S(1)}, f32[2,64,256]{2,1,0:T(8,128)S(1)}, u32[]{:S(2)}, u32[]{:S(2)}) collective-permute-start(f32[2,64,256]{2,1,0:T(8,128)S(1)} %get-tuple-element.80), channel_id=1, source_target_pairs={{0,4},{4,8},{8,12},{12,16},{16,20},{20,24},{24,28},{28,0},{1,5},{5... | collective-permute-start | bytes 393224 | tf_op jit(solution)/shard_map/ppermute | solution.py:297
  361.1 16.2 %collective-permute-start.9 = (f32[2,64,256]{2,1,0:T(8,128)S(1)}, f32[2,64,256]{2,1,0:T(8,128)S(1)}, u32[]{:S(2)}, u32[]{:S(2)}) collective-permute-start(f32[2,64,256]{2,1,0:T(8,128)S(1)} %get-tuple-element.81), channel_id=1, source_target_pairs={{0,28},{4,0},{8,4},{12,8},{16,12},{20,16},{24,20},{28,24},{1,29},{... | collective-permute-start | bytes 393224 | tf_op jit(solution)/shard_map/ppermute | solution.py:297
  365.6 18.0 %collective-permute-start.4 = (f32[2,64,256]{2,1,0:T(8,128)S(1)}, f32[2,64,256]{2,1,0:T(8,128)S(1)}, u32[]{:S(2)}, u32[]{:S(2)}) collective-permute-start(f32[2,64,256]{2,1,0:T(8,128)S(1)} %get-tuple-element.75), channel_id=1, source_target_pairs={{0,4},{4,8},{8,12},{12,16},{16,20},{20,24},{24,28},{28,0},{1,5},{5... | collective-permute-start | bytes 393224 | tf_op jit(solution)/shard_map/ppermute | solution.py:297
  367.5 16.2 %collective-permute-start.5 = (f32[2,64,256]{2,1,0:T(8,128)S(1)}, f32[2,64,256]{2,1,0:T(8,128)S(1)}, u32[]{:S(2)}, u32[]{:S(2)}) collective-permute-start(f32[2,64,256]{2,1,0:T(8,128)S(1)} %get-tuple-element.76), channel_id=1, source_target_pairs={{0,28},{4,0},{8,4},{12,8},{16,12},{20,16},{24,20},{28,24},{1,29},{... | collective-permute-start | bytes 393224 | tf_op jit(solution)/shard_map/ppermute | solution.py:297
  368.1 15.6 %collective-permute-start.6 = (f32[32,2,256]{2,1,0:T(2,128)S(1)}, f32[32,2,256]{2,1,0:T(2,128)S(1)}, u32[]{:S(2)}, u32[]{:S(2)}) collective-permute-start(f32[32,2,256]{2,1,0:T(2,128)S(1)} %get-tuple-element.77), channel_id=1, source_target_pairs={{0,1},{1,2},{2,3},{3,0},{4,5},{5,6},{6,7},{7,4},{8,9},{9,10},{10,1... | collective-permute-start | bytes 196616 | tf_op jit(solution)/shard_map/ppermute | solution.py:297
  370.8 12.9 %collective-permute-start.7 = (f32[32,2,256]{2,1,0:T(2,128)S(1)}, f32[32,2,256]{2,1,0:T(2,128)S(1)}, u32[]{:S(2)}, u32[]{:S(2)}) collective-permute-start(f32[32,2,256]{2,1,0:T(2,128)S(1)} %get-tuple-element.78), channel_id=1, source_target_pairs={{0,3},{1,0},{2,1},{3,2},{4,7},{5,4},{6,5},{7,6},{8,11},{9,8},{10,9... | collective-permute-start | bytes 196616 | tf_op jit(solution)/shard_map/ppermute | solution.py:297
  (28 other events, 90.9 us)

commit v4 on v3

--- a/solution.py
+++ b/solution.py
@@ -693,7 +693,7 @@
     def unfold(received):
         return received.reshape((slabs, pens) + received.shape[1:])
 
-    cut = planes - STEP
+    cut = (planes // STEP // 2) * STEP
     particles = (counts, row_base, z_base, fractions, strength)
     grid, ghost_y, ghost_x, ghost_xy = deposit(particles, cut, planes)
     tail = (grid, next_over(ghost_y, ("pen",)))
@@ -720,8 +720,12 @@
     shape = (slabs, pens, depth, planes, width)
     backs = plane_inverse((0,), start, spectra, shape) + plane_inverse((1, 2), start, spectra, shape)
     outputs = received = None
+    layers = []
     for part, back in enumerate(backs):
-        received = exchange(back.reshape(devices, depth, planes, width), received)
+        back = back.reshape(devices, depth, planes, width)
+        received = exchange(back, None if part == 0 else (received, layers[: part - 1]))
+        if part == 2:
+            received, outputs = lax.optimization_barrier((received, outputs))
         field, low_x, high_x, low_y, high_y = z_inverse(received)
         halos = (
             shifted(high_x, "slab", 1),
@@ -729,6 +733,7 @@
             shifted(high_y, "pen", 1),
             shifted(low_y, "pen", -1),
         )
+        layers.append(halos)
         outputs = stretch(part, vorticity, field, halos, outputs)
     return (vorticity, outputs[0], outputs[1])
 

time: 395 us -> 403 us (1.020)
  waiting for transfers between devices: 140 us -> 206 us
  blocking collectives: 53.2 us -> 0 us
  local copies, waits for them, and re-layouts: 24.2 us -> 20 us
    all_to_all x1 -> x0, blocking collectives: 53.2 us -> none  [exchange(): return lax.all_to_all(blocks_out, AXES, 0, 0, tiled=True)]
    ppermute x12, waiting for transfers between devices: 32.3 us -> 81.7 us  [shifted(): lax.ppermute(block, axis, [(i, (i + distance) % count) for i in range(cou...]
    ppermute x4, waiting for transfers between devices: 2.26 us -> 41 us  [next_over(): return lax.ppermute(block, AXES, route)]
    all_to_all x5 -> x6, waiting for transfers between devices: 106 us -> 83.7 us  [exchange(): return lax.all_to_all(blocks_out, AXES, 0, 0, tiled=True)]
    pallas_call x2, Pallas kernels: 32.9 us -> 28.4 us  [deposit(): pl.pallas_call(functools.partial(deposit_kernel, begin, end), out_shape=[...]
    unnamed x63 -> x47, local copies, waits for them, and re-layouts: 24.1 us -> 19.9 us
    all_to_all x5 -> x6, starting transfers between devices: 32.3 us -> 34.8 us  [exchange(): return lax.all_to_all(blocks_out, AXES, 0, 0, tiled=True)]
  transfers between devices with their start and end apart: 21 -> 22, of which waited for: 7 -> 12; matrix products, arithmetic and copies ran while one was open for 0% -> 0% of each run, Pallas kernels for 26% -> 22%
where the time goes in v4:
time: 403 us; the launch traced here: 401 us
  waiting for transfers between devices  206 us (51%)
  Pallas kernels  117 us (29%)
  starting transfers between devices  56.5 us (14%)
  local copies, waits for them, and re-layouts  20 us (5%)
    all_to_all x6, waiting for transfers between devices, exchange(): return lax.all_to_all(blocks_out, AXES, 0, 0, tiled=True)  83.7 us
    ppermute x12, waiting for transfers between devices, shifted(): lax.ppermute(block, axis, [(i, (i + distance) % count) for i in range(cou...  81.7 us
    ppermute x4, waiting for transfers between devices, next_over(): return lax.ppermute(block, AXES, route)  41 us
    all_to_all x6, starting transfers between devices, exchange(): return lax.all_to_all(blocks_out, AXES, 0, 0, tiled=True)  34.8 us
    pallas_call x2, Pallas kernels, deposit(): pl.pallas_call(functools.partial(deposit_kernel, begin, end), out_shape=[...  28.4 us
    pallas_call x2, Pallas kernels, plane_inverse(): pl.pallas_call(functools.partial(plane_inverse_kernel, parts, needs), gri...  24.5 us
    unnamed x47, local copies, waits for them, and re-layouts  19.9 us
    pallas_call x2, Pallas kernels, plane_forward(): pl.pallas_call(plane_forward_kernel, grid=(count, depth + 1), in_specs=[p...  19.3 us
  transfers between devices with their start and end apart: 22, of which 12 were waited for; matrix products, arithmetic and copies ran while one was open for 0% of the time, Pallas kernels for 22%

profile of v4, /device:TPU:17, one launch (start us, length us, event | category | flops | bytes accessed | tf_op | source)
XLA Modules:
  0.0 400.6 jit_solution(2892092811317390080)
XLA Ops:
  5.6 16.0 %deposit.2 = (f32[3,19,72,256]{3,2,1,0:T(8,128)}, f32[3,16,3,256]{3,2,1,0:T(4,128)S(1)}, f32[3,3,64,256]{3,2,1,0:T(8,128)S(1)}, f32[3,3,3,256]{3,2,1,0:T(4,128)S(1)}) custom-call(s32[32,4]{1,0:T(8,128)S(1)} %copy.34.counts, s32[32,4,512]{2,1,0:T(4,128)S(1)} %copy-done.13, s32[32,4,512]{2,1,0:T(4,128)S(1)} %copy-done.15, f32[3,32,4,512]{3,2,1,0:T(4,128)S(1)} %copy-done.9, ...), custom_call_target="tpu_custom_call" | custom-call | flops 28689039360 | bytes 12582912 | tf_op jit(solution)/shard_map/deposit/pallas_call | solution.py:264
  26.0 4.9 %z_forward.4 = (f32[3,32,64,256]{3,2,1,0:T(8,128)}, f32[32,2,4,16,128]{4,3,2,1,0:T(8,128)}) custom-call(f32[3,19,72,256]{3,2,1,0:T(8,128)} %get-tuple-element.52.refs_0_, f32[3,16,3,256]{3,2,1,0:T(4,128)S(1)} %collective-permute-done.refs_1_, bf16[768,256]{1,0:T(8,128)(2,1)S(1)} %copy-done.1), custom_call_target="tpu_custom_call" | custom-call | flops 805306368 | bytes 6291456 | tf_op jit(solution)/shard_map/z_forward/pallas_call | solution.py:359
  30.8 8.2 %all-to-all-start = ((f32[32,2,4,16,128]{4,3,2,1,0:T(8,128)}), f32[32,2,4,16,128]{4,3,2,1,0:T(8,128)}, u32[]{:S(2)}, u32[]{:S(2)}) async-start(f32[32,2,4,16,128]{4,3,2,1,0:T(8,128)} %get-tuple-element.54), calls=%async_computation | async-start | bytes 4194304 | tf_op jit(solution)/shard_map/all_to_all | solution.py:691
  42.3 12.4 %deposit.3 = (f32[3,16,72,256]{3,2,1,0:T(8,128)S(1)}, f32[3,16,3,256]{3,2,1,0:T(4,128)S(1)}) custom-call(s32[32,4]{1,0:T(8,128)S(1)} %copy.35.counts, s32[32,4,512]{2,1,0:T(4,128)S(1)} %copy-done.14, s32[32,4,512]{2,1,0:T(4,128)S(1)} %copy-done.16, f32[3,32,4,512]{3,2,1,0:T(4,128)S(1)} %copy-done.10, f32[3,32,4,512]{3,2,1,0:T(4,128)S(1)} %copy-done.12), custom_call_target="tpu_custom_call" | custom-call | flops 24159191040 | bytes 12582912 | tf_op jit(solution)/shard_map/deposit/pallas_call | solution.py:264
  61.3 38.3 %collective-permute-done.3.refs_3_ = f32[3,3,3,256]{3,2,1,0:T(4,128)S(1)} collective-permute-done((f32[3,3,3,256]{3,2,1,0:T(4,128)S(1)}, f32[3,3,3,256]{3,2,1,0:T(4,128)S(1)}, u32[]{:S(2)}, u32[]{:S(2)}) %collective-permute-start.3) | collective-permute-done | bytes 27680 | tf_op jit(solution)/shard_map/ppermute | solution.py:292
  99.7 4.3 %z_forward.5 = (f32[3,32,64,256]{3,2,1,0:T(8,128)}, f32[32,2,4,16,128]{4,3,2,1,0:T(8,128)S(1)}) custom-call(f32[3,16,72,256]{3,2,1,0:T(8,128)} %copy-done, f32[3,16,3,256]{3,2,1,0:T(4,128)S(1)} %collective-permute-done.1.refs_1_, f32[3,3,64,256]{3,2,1,0:T(8,128)S(1)} %collective-permute-done.2.refs_2_, ...), custom_call_target="tpu_custom_call", output_to_operand_aliasing={{0}: (5, {})} | custom-call | flops 805306368 | bytes 6291456 | tf_op jit(solution)/shard_map/z_forward/pallas_call | solution.py:359
  105.4 4.9 %all-to-all-start.1 = ((f32[32,2,4,16,128]{4,3,2,1,0:T(8,128)}), f32[32,2,4,16,128]{4,3,2,1,0:T(8,128)S(1)}, u32[]{:S(2)}, u32[]{:S(2)}) async-start(f32[32,2,4,16,128]{4,3,2,1,0:T(8,128)} %copy-done.8), calls=%async_computation.1 | async-start | bytes 4194304 | tf_op jit(solution)/shard_map/all_to_all | solution.py:691
  116.1 41.4 %all-to-all-done.1 = f32[32,2,4,16,128]{4,3,2,1,0:T(8,128)S(1)} async-done(((f32[32,2,4,16,128]{4,3,2,1,0:T(8,128)}), f32[32,2,4,16,128]{4,3,2,1,0:T(8,128)S(1)}, u32[]{:S(2)}, u32[]{:S(2)}) %all-to-all-start.1) | async-done | bytes 2097184 | tf_op jit(solution)/shard_map/all_to_all | solution.py:691
  158.9 5.7 %all-to-all-start.2 = ((f32[32,1,4,32,128]{4,3,2,1,0:T(8,128)}), f32[32,1,4,32,128]{4,3,2,1,0:T(8,128)}, u32[]{:S(2)}, u32[]{:S(2)}) async-start(f32[32,1,4,32,128]{4,3,2,1,0:T(8,128)} %get-tuple-element.72), calls=%async_computation.2 | async-start | bytes 4194304 | tf_op jit(solution)/shard_map/all_to_all | solution.py:691
  169.0 12.6 %plane_forward.3.refs_1_.refs_2_.refs_4_.refs_5_.refs_0_.refs_3_ = f32[2,5,512,256]{3,2,1,0:T(8,128)} custom-call(s32[1]{0:T(128)} %bitcast.start, f32[8,4,2,4,16,128]{5,4,3,2,1,0:T(8,128)S(1)} %bitcast.8, f32[8,4,2,4,16,128]{5,4,3,2,1,0:T(8,128)} %bitcast.3.refs_1_, bf16[1536,512]{1,0:T(8,128)(2,1)S(1)} %copy-done.19, bf16[512,1536]{1,0:T(8,128)(2,1)S(1)} %copy-done.17), custom_call_target="tpu_custom_call" | custom-call | flops 6442450944 | bytes 8388608 | tf_op jit(solution)/shard_map/plane_forward/pallas_call | solution.py:471
  181.7 10.2 %plane_inverse.3 = f32[8,4,4,32,128]{4,3,2,1,0:T(8,128)} custom-call(s32[1]{0:T(128)} %bitcast.start, f32[2,5,512,256]{3,2,1,0:T(8,128)} %plane_forward.3.refs_1_.refs_2_.refs_4_.refs_5_.refs_0_.refs_3_, f32[2,5,512,256]{3,2,1,0:T(8,128)} %plane_forward.3.refs_1_.refs_2_.refs_4_.refs_5_.refs_0_.refs_3_, ...), custom_call_target="tpu_custom_call" | custom-call | flops 3221225472 | bytes 6291456 | tf_op jit(solution)/shard_map/plane_inverse/pallas_call | solution.py:565
  191.8 20.1 %all-to-all-done.2 = f32[32,1,4,32,128]{4,3,2,1,0:T(8,128)} async-done(((f32[32,1,4,32,128]{4,3,2,1,0:T(8,128)}), f32[32,1,4,32,128]{4,3,2,1,0:T(8,128)}, u32[]{:S(2)}, u32[]{:S(2)}) %all-to-all-start.2) | async-done | bytes 2097184 | tf_op jit(solution)/shard_map/all_to_all | solution.py:691
  211.9 5.7 %all-to-all-start.3 = ((f32[32,4,32,128]{3,2,1,0:T(8,128)}), f32[32,4,32,128]{3,2,1,0:T(8,128)}, u32[]{:S(2)}, u32[]{:S(2)}) async-start(f32[32,4,32,128]{3,2,1,0:T(8,128)} %bitcast.6), calls=%async_computation.3 | async-start | bytes 4194304 | tf_op jit(solution)/shard_map/all_to_all | solution.py:691
  220.4 6.7 %plane_forward.2.refs_0_.refs_3_ = f32[1,5,512,256]{3,2,1,0:T(8,128)} custom-call(s32[1]{0:T(128)} %bitcast.start, f32[8,4,1,4,32,128]{5,4,3,2,1,0:T(8,128)} %bitcast.1.refs_0_, bf16[1536,512]{1,0:T(8,128)(2,1)S(1)} %copy-done.20, bf16[512,1536]{1,0:T(8,128)(2,1)S(1)} %copy-done.18), custom_call_target="tpu_custom_call" | custom-call | flops 3221225472 | bytes 4194304 | tf_op jit(solution)/shard_map/plane_forward/pallas_call | solution.py:471
  227.1 14.3 %plane_inverse.2 = (f32[8,4,4,32,128]{4,3,2,1,0:T(8,128)S(1)}, f32[8,4,4,32,128]{4,3,2,1,0:T(8,128)}) custom-call(s32[1]{0:T(128)} %bitcast.start, f32[1,5,512,256]{3,2,1,0:T(8,128)} %plane_forward.2.refs_0_.refs_3_, f32[2,5,512,256]{3,2,1,0:T(8,128)} %plane_forward.3.refs_1_.refs_2_.refs_4_.refs_5_.refs_0_.refs_3_, ...), custom_call_target="tpu_custom_call" | custom-call | flops 6442450944 | bytes 12582912 | tf_op jit(solution)/shard_map/plane_inverse/pallas_call | solution.py:565
  242.7 22.2 %all-to-all-done.3.received = f32[32,4,32,128]{3,2,1,0:T(8,128)} async-done(((f32[32,4,32,128]{3,2,1,0:T(8,128)}), f32[32,4,32,128]{3,2,1,0:T(8,128)}, u32[]{:S(2)}, u32[]{:S(2)}) %all-to-all-start.3) | async-done | bytes 2097184 | tf_op jit(solution)/shard_map/all_to_all | solution.py:691
  264.9 5.7 %all-to-all-start.4 = ((f32[32,4,32,128]{3,2,1,0:T(8,128)}), f32[32,4,32,128]{3,2,1,0:T(8,128)}, u32[]{:S(2)}, u32[]{:S(2)}) async-start(f32[32,4,32,128]{3,2,1,0:T(8,128)} %bitcast.7), calls=%async_computation.4 | async-start | bytes 4194304 | tf_op jit(solution)/shard_map/all_to_all | solution.py:691
  278.6 5.4 %collective-permute-done.6.low_y = f32[32,2,256]{2,1,0:T(2,128)S(1)} collective-permute-done((f32[32,2,256]{2,1,0:T(2,128)S(1)}, f32[32,2,256]{2,1,0:T(2,128)S(1)}, u32[]{:S(2)}, u32[]{:S(2)}) %collective-permute-start.6) | collective-permute-done | bytes 65568 | tf_op jit(solution)/shard_map/ppermute | solution.py:297
  287.1 33.7 %collective-permute-done.4.low_x = f32[2,64,256]{2,1,0:T(8,128)S(1)} collective-permute-done((f32[2,64,256]{2,1,0:T(8,128)S(1)}, f32[2,64,256]{2,1,0:T(8,128)S(1)}, u32[]{:S(2)}, u32[]{:S(2)}) %collective-permute-start.4) | collective-permute-done | bytes 131104 | tf_op jit(solution)/shard_map/ppermute | solution.py:297
  320.8 4.7 %all-to-all-start.5 = ((f32[32,4,32,128]{3,2,1,0:T(8,128)}), f32[32,4,32,128]{3,2,1,0:T(8,128)}, u32[]{:S(2)}, u32[]{:S(2)}) async-start(f32[32,4,32,128]{3,2,1,0:T(8,128)} %bitcast.9), calls=%async_computation.5 | async-start | bytes 4194304 | tf_op jit(solution)/shard_map/all_to_all | solution.py:691
  333.5 6.3 %stretch.3 = (f32[3,32,64,256]{3,2,1,0:T(8,128)}, f32[3,32,64,256]{3,2,1,0:T(8,128)}) custom-call(f32[3,32,64,256]{3,2,1,0:T(8,128)} %get-tuple-element.49.vorticity, f32[32,64,256]{2,1,0:T(8,128)S(1)} %get-tuple-element.86.field.before.after, f32[32,64,256]{2,1,0:T(8,128)S(1)} %get-tuple-element.86.field.before.after, ...), custom_call_target="tpu_custom_call" | custom-call | flops 314572800 | bytes 14680064 | tf_op jit(solution)/shard_map/stretch/pallas_call | solution.py:663
  341.9 33.7 %collective-permute-done.8.low_x = f32[2,64,256]{2,1,0:T(8,128)S(1)} collective-permute-done((f32[2,64,256]{2,1,0:T(8,128)S(1)}, f32[2,64,256]{2,1,0:T(8,128)S(1)}, u32[]{:S(2)}, u32[]{:S(2)}) %collective-permute-start.8) | collective-permute-done | bytes 131104 | tf_op jit(solution)/shard_map/ppermute | solution.py:297
  375.6 6.3 %stretch.4 = (f32[3,32,64,256]{3,2,1,0:T(8,128)}, f32[3,32,64,256]{3,2,1,0:T(8,128)}) custom-call(f32[3,32,64,256]{3,2,1,0:T(8,128)} %get-tuple-element.49.vorticity, f32[32,64,256]{2,1,0:T(8,128)S(1)} %get-tuple-element.81.field.before.after, ...), custom_call_target="tpu_custom_call", output_to_operand_aliasing={{0}: (9, {}), {1}: (10, {})} | custom-call | flops 314572800 | bytes 14680064 | tf_op jit(solution)/shard_map/stretch/pallas_call | solution.py:663
  394.3 6.3 %stretch.5 = (f32[3,32,64,256]{3,2,1,0:T(8,128)}, f32[3,32,64,256]{3,2,1,0:T(8,128)}) custom-call(f32[3,32,64,256]{3,2,1,0:T(8,128)} %get-tuple-element.49.vorticity, f32[32,64,256]{2,1,0:T(8,128)S(1)} %get-tuple-element.92.field.before.after, ...), custom_call_target="tpu_custom_call", output_to_operand_aliasing={{0}: (9, {}), {1}: (10, {})} | custom-call | flops 314572800 | bytes 14680064 | tf_op jit(solution)/shard_map/stretch/pallas_call | solution.py:663
  (84 shorter events, 69.9 us)
Async XLA Ops:
  5.6 20.4 %copy-start.1 = (bf16[768,256]{1,0:T(8,128)(2,1)S(1)}, bf16[768,256]{1,0:T(8,128)(2,1)}, u32[]{:S(2)}) copy-start(bf16[768,256]{1,0:T(8,128)(2,1)} %constant.25.clone.refs_2_.refs_4_) | copy-start | bytes 1179652
  21.5 4.4 %collective-permute-start = (f32[3,16,3,256]{3,2,1,0:T(4,128)S(1)}, f32[3,16,3,256]{3,2,1,0:T(4,128)S(1)}, u32[]{:S(2)}, u32[]{:S(2)}) collective-permute-start(f32[3,16,3,256]{3,2,1,0:T(4,128)S(1)} %get-tuple-element.53), channel_id=1, source_target_pairs={{0,1},{1,2},{2,3},{3,0},{4,5},{5,6},{6,7},{7,4},{8,9},{9,10},{10,1... | collective-permute-start | bytes 442376 | tf_op jit(solution)/shard_map/ppermute | solution.py:292
  30.8 74.6 %all-to-all-start = ((f32[32,2,4,16,128]{4,3,2,1,0:T(8,128)}), f32[32,2,4,16,128]{4,3,2,1,0:T(8,128)}, u32[]{:S(2)}, u32[]{:S(2)}) async-start(f32[32,2,4,16,128]{4,3,2,1,0:T(8,128)} %get-tuple-element.54), calls=%async_computation | async-start | bytes 4194304 | tf_op jit(solution)/shard_map/all_to_all | solution.py:691
  39.0 60.6 %collective-permute-start.2 = (f32[3,3,64,256]{3,2,1,0:T(8,128)S(1)}, f32[3,3,64,256]{3,2,1,0:T(8,128)S(1)}, u32[]{:S(2)}, u32[]{:S(2)}) collective-permute-start(f32[3,3,64,256]{3,2,1,0:T(8,128)S(1)} %get-tuple-element.62), channel_id=1, source_target_pairs={{0,4},{1,5},{2,6},{3,7},{4,8},{5,9},{6,10},{7,11},{8,12},{9,13},{1... | collective-permute-start | bytes 1769480 | tf_op jit(solution)/shard_map/ppermute | solution.py:292
  56.5 43.2 %collective-permute-start.1 = (f32[3,16,3,256]{3,2,1,0:T(4,128)S(1)}, f32[3,16,3,256]{3,2,1,0:T(4,128)S(1)}, u32[]{:S(2)}, u32[]{:S(2)}) collective-permute-start(f32[3,16,3,256]{3,2,1,0:T(4,128)S(1)} %get-tuple-element.61), channel_id=1, source_target_pairs={{0,1},{1,2},{2,3},{3,0},{4,5},{5,6},{6,7},{7,4},{8,9},{9,10},{10,1... | collective-permute-start | bytes 442376 | tf_op jit(solution)/shard_map/ppermute | solution.py:292
  57.4 42.3 %collective-permute-start.3 = (f32[3,3,3,256]{3,2,1,0:T(4,128)S(1)}, f32[3,3,3,256]{3,2,1,0:T(4,128)S(1)}, u32[]{:S(2)}, u32[]{:S(2)}) collective-permute-start(f32[3,3,3,256]{3,2,1,0:T(4,128)S(1)} %get-tuple-element.63), channel_id=1, source_target_pairs={{0,5},{1,6},{2,7},{3,4},{4,9},{5,10},{6,11},{7,8},{8,13},{9,14},{1... | collective-permute-start | bytes 82952 | tf_op jit(solution)/shard_map/ppermute | solution.py:292
  105.4 52.2 %all-to-all-start.1 = ((f32[32,2,4,16,128]{4,3,2,1,0:T(8,128)}), f32[32,2,4,16,128]{4,3,2,1,0:T(8,128)S(1)}, u32[]{:S(2)}, u32[]{:S(2)}) async-start(f32[32,2,4,16,128]{4,3,2,1,0:T(8,128)} %copy-done.8), calls=%async_computation.1 | async-start | bytes 4194304 | tf_op jit(solution)/shard_map/all_to_all | solution.py:691
  158.9 53.0 %all-to-all-start.2 = ((f32[32,1,4,32,128]{4,3,2,1,0:T(8,128)}), f32[32,1,4,32,128]{4,3,2,1,0:T(8,128)}, u32[]{:S(2)}, u32[]{:S(2)}) async-start(f32[32,1,4,32,128]{4,3,2,1,0:T(8,128)} %get-tuple-element.72), calls=%async_computation.2 | async-start | bytes 4194304 | tf_op jit(solution)/shard_map/all_to_all | solution.py:691
  169.0 12.6 %copy-start.3 = (bf16[1536,512]{1,0:T(8,128)(2,1)S(1)}, bf16[1536,512]{1,0:T(8,128)(2,1)}, u32[]{:S(2)}) copy-start(bf16[1536,512]{1,0:T(8,128)(2,1)} %constant.28.clone.refs_6_.refs_4_) | copy-start | bytes 4718596
  211.9 53.0 %all-to-all-start.3 = ((f32[32,4,32,128]{3,2,1,0:T(8,128)}), f32[32,4,32,128]{3,2,1,0:T(8,128)}, u32[]{:S(2)}, u32[]{:S(2)}) async-start(f32[32,4,32,128]{3,2,1,0:T(8,128)} %bitcast.6), calls=%async_computation.3 | async-start | bytes 4194304 | tf_op jit(solution)/shard_map/all_to_all | solution.py:691
  264.9 55.9 %all-to-all-start.4 = ((f32[32,4,32,128]{3,2,1,0:T(8,128)}), f32[32,4,32,128]{3,2,1,0:T(8,128)}, u32[]{:S(2)}, u32[]{:S(2)}) async-start(f32[32,4,32,128]{3,2,1,0:T(8,128)} %bitcast.7), calls=%async_computation.4 | async-start | bytes 4194304 | tf_op jit(solution)/shard_map/all_to_all | solution.py:691
  274.2 46.6 %collective-permute-start.4 = (f32[2,64,256]{2,1,0:T(8,128)S(1)}, f32[2,64,256]{2,1,0:T(8,128)S(1)}, u32[]{:S(2)}, u32[]{:S(2)}) collective-permute-start(f32[2,64,256]{2,1,0:T(8,128)S(1)} %get-tuple-element.76), channel_id=1, source_target_pairs={{0,4},{4,8},{8,12},{12,16},{16,20},{20,24},{24,28},{28,0},{1,5},{5... | collective-permute-start | bytes 393224 | tf_op jit(solution)/shard_map/ppermute | solution.py:297
  275.4 45.3 %collective-permute-start.5 = (f32[2,64,256]{2,1,0:T(8,128)S(1)}, f32[2,64,256]{2,1,0:T(8,128)S(1)}, u32[]{:S(2)}, u32[]{:S(2)}) collective-permute-start(f32[2,64,256]{2,1,0:T(8,128)S(1)} %get-tuple-element.77), channel_id=1, source_target_pairs={{0,28},{4,0},{8,4},{12,8},{16,12},{20,16},{24,20},{28,24},{1,29},{... | collective-permute-start | bytes 393224 | tf_op jit(solution)/shard_map/ppermute | solution.py:297
  276.6 7.4 %collective-permute-start.6 = (f32[32,2,256]{2,1,0:T(2,128)S(1)}, f32[32,2,256]{2,1,0:T(2,128)S(1)}, u32[]{:S(2)}, u32[]{:S(2)}) collective-permute-start(f32[32,2,256]{2,1,0:T(2,128)S(1)} %get-tuple-element.78), channel_id=1, source_target_pairs={{0,1},{1,2},{2,3},{3,0},{4,5},{5,6},{6,7},{7,4},{8,9},{9,10},{10,1... | collective-permute-start | bytes 196616 | tf_op jit(solution)/shard_map/ppermute | solution.py:297
  278.6 8.5 %collective-permute-start.7 = (f32[32,2,256]{2,1,0:T(2,128)S(1)}, f32[32,2,256]{2,1,0:T(2,128)S(1)}, u32[]{:S(2)}, u32[]{:S(2)}) collective-permute-start(f32[32,2,256]{2,1,0:T(2,128)S(1)} %get-tuple-element.79), channel_id=1, source_target_pairs={{0,3},{1,0},{2,1},{3,2},{4,7},{5,4},{6,5},{7,6},{8,11},{9,8},{10,9... | collective-permute-start | bytes 196616 | tf_op jit(solution)/shard_map/ppermute | solution.py:297
  320.8 61.2 %all-to-all-start.5 = ((f32[32,4,32,128]{3,2,1,0:T(8,128)}), f32[32,4,32,128]{3,2,1,0:T(8,128)}, u32[]{:S(2)}, u32[]{:S(2)}) async-start(f32[32,4,32,128]{3,2,1,0:T(8,128)} %bitcast.9), calls=%async_computation.5 | async-start | bytes 4194304 | tf_op jit(solution)/shard_map/all_to_all | solution.py:691
  329.1 46.5 %collective-permute-start.8 = (f32[2,64,256]{2,1,0:T(8,128)S(1)}, f32[2,64,256]{2,1,0:T(8,128)S(1)}, u32[]{:S(2)}, u32[]{:S(2)}) collective-permute-start(f32[2,64,256]{2,1,0:T(8,128)S(1)} %get-tuple-element.82), channel_id=1, source_target_pairs={{0,4},{4,8},{8,12},{12,16},{16,20},{20,24},{24,28},{28,0},{1,5},{5... | collective-permute-start | bytes 393224 | tf_op jit(solution)/shard_map/ppermute | solution.py:297
  330.3 45.3 %collective-permute-start.9 = (f32[2,64,256]{2,1,0:T(8,128)S(1)}, f32[2,64,256]{2,1,0:T(8,128)S(1)}, u32[]{:S(2)}, u32[]{:S(2)}) collective-permute-start(f32[2,64,256]{2,1,0:T(8,128)S(1)} %get-tuple-element.83), channel_id=1, source_target_pairs={{0,28},{4,0},{8,4},{12,8},{16,12},{20,16},{24,20},{28,24},{1,29},{... | collective-permute-start | bytes 393224 | tf_op jit(solution)/shard_map/ppermute | solution.py:297
  331.5 8.3 %collective-permute-start.10 = (f32[32,2,256]{2,1,0:T(2,128)S(1)}, f32[32,2,256]{2,1,0:T(2,128)S(1)}, u32[]{:S(2)}, u32[]{:S(2)}) collective-permute-start(f32[32,2,256]{2,1,0:T(2,128)S(1)} %get-tuple-element.84), channel_id=1, source_target_pairs={{0,1},{1,2},{2,3},{3,0},{4,5},{5,6},{6,7},{7,4},{8,9},{9,10},{10,1... | collective-permute-start | bytes 196616 | tf_op jit(solution)/shard_map/ppermute | solution.py:297
  333.5 8.4 %collective-permute-start.11 = (f32[32,2,256]{2,1,0:T(2,128)S(1)}, f32[32,2,256]{2,1,0:T(2,128)S(1)}, u32[]{:S(2)}, u32[]{:S(2)}) collective-permute-start(f32[32,2,256]{2,1,0:T(2,128)S(1)} %get-tuple-element.85), channel_id=1, source_target_pairs={{0,3},{1,0},{2,1},{3,2},{4,7},{5,4},{6,5},{7,6},{8,11},{9,8},{10,9... | collective-permute-start | bytes 196616 | tf_op jit(solution)/shard_map/ppermute | solution.py:297
  385.5 8.8 %collective-permute-start.12 = (f32[2,64,256]{2,1,0:T(8,128)S(1)}, f32[2,64,256]{2,1,0:T(8,128)S(1)}, u32[]{:S(2)}, u32[]{:S(2)}) collective-permute-start(f32[2,64,256]{2,1,0:T(8,128)S(1)} %get-tuple-element.93), channel_id=1, source_target_pairs={{0,4},{4,8},{8,12},{12,16},{16,20},{20,24},{24,28},{28,0},{1,5},{5... | collective-permute-start | bytes 393224 | tf_op jit(solution)/shard_map/ppermute | solution.py:297
  385.6 8.7 %collective-permute-start.13 = (f32[2,64,256]{2,1,0:T(8,128)S(1)}, f32[2,64,256]{2,1,0:T(8,128)S(1)}, u32[]{:S(2)}, u32[]{:S(2)}) collective-permute-start(f32[2,64,256]{2,1,0:T(8,128)S(1)} %get-tuple-element.94), channel_id=1, source_target_pairs={{0,28},{4,0},{8,4},{12,8},{16,12},{20,16},{24,20},{28,24},{1,29},{... | collective-permute-start | bytes 393224 | tf_op jit(solution)/shard_map/ppermute | solution.py:297
  387.9 4.2 %collective-permute-start.14 = (f32[32,2,256]{2,1,0:T(2,128)S(1)}, f32[32,2,256]{2,1,0:T(2,128)S(1)}, u32[]{:S(2)}, u32[]{:S(2)}) collective-permute-start(f32[32,2,256]{2,1,0:T(2,128)S(1)} %get-tuple-element.95), channel_id=1, source_target_pairs={{0,1},{1,2},{2,3},{3,0},{4,5},{5,6},{6,7},{7,4},{8,9},{9,10},{10,1... | collective-permute-start | bytes 196616 | tf_op jit(solution)/shard_map/ppermute | solution.py:297
  390.6 3.7 collective-permute-start.15
  (21 other events, 74.0 us)

commit v5 on v4

--- a/solution.py
+++ b/solution.py
@@ -693,7 +693,7 @@
     def unfold(received):
         return received.reshape((slabs, pens) + received.shape[1:])
 
-    cut = (planes // STEP // 2) * STEP
+    cut = planes - STEP
     particles = (counts, row_base, z_base, fractions, strength)
     grid, ghost_y, ghost_x, ghost_xy = deposit(particles, cut, planes)
     tail = (grid, next_over(ghost_y, ("pen",)))

time: 403 us -> 391 us (0.970)
  waiting for transfers between devices: 206 us -> 189 us
  starting transfers between devices: 56.5 us -> 62.8 us
    ppermute x4, waiting for transfers between devices: 41 us -> 1.31 us  [next_over(): return lax.ppermute(block, AXES, route)]
    all_to_all x6, waiting for transfers between devices: 83.7 us -> 106 us  [exchange(): return lax.all_to_all(blocks_out, AXES, 0, 0, tiled=True)]
    all_to_all x6, starting transfers between devices: 34.8 us -> 39.1 us  [exchange(): return lax.all_to_all(blocks_out, AXES, 0, 0, tiled=True)]
    unnamed x47 -> x53, local copies, waits for them, and re-layouts: 19.9 us -> 21.8 us
  transfers between devices with their start and end apart: 22 -> 22, of which waited for: 12 -> 12; matrix products, arithmetic and copies ran while one was open for 0% -> 0% of each run, Pallas kernels for 22% -> 24%
where the time goes in v5:
time: 391 us
  waiting for transfers between devices  189 us (48%)
  Pallas kernels  116 us (30%)
  starting transfers between devices  62.8 us (16%)
  local copies, waits for them, and re-layouts  21.8 us (6%)
    all_to_all x6, waiting for transfers between devices, exchange(): return lax.all_to_all(blocks_out, AXES, 0, 0, tiled=True)  106 us
    ppermute x12, waiting for transfers between devices, shifted(): lax.ppermute(block, axis, [(i, (i + distance) % count) for i in range(cou...  81.7 us
    all_to_all x6, starting transfers between devices, exchange(): return lax.all_to_all(blocks_out, AXES, 0, 0, tiled=True)  39.1 us
    pallas_call x2, Pallas kernels, deposit(): pl.pallas_call(functools.partial(deposit_kernel, begin, end), out_shape=[...  30.3 us
    pallas_call x2, Pallas kernels, plane_inverse(): pl.pallas_call(functools.partial(plane_inverse_kernel, parts, needs), gri...  24.5 us
    unnamed x53, local copies, waits for them, and re-layouts  21.8 us
    pallas_call x2, Pallas kernels, plane_forward(): pl.pallas_call(plane_forward_kernel, grid=(count, depth + 1), in_specs=[p...  19.6 us
    pallas_call x3, Pallas kernels, stretch(): pl.pallas_call(stretch_kernel, grid=(planes // STEP,), in_specs=specs, ou...  19 us
  transfers between devices with their start and end apart: 22, of which 12 were waited for; matrix products, arithmetic and copies ran while one was open for 0% of the time, Pallas kernels for 24%

profile of v5, /device:TPU:17, one launch (start us, length us, event | category | flops | bytes accessed | tf_op | source)
XLA Modules:
  0.0 390.6 jit_solution(192205730160658293)
XLA Ops:
  5.6 11.1 %deposit.2 = (f32[3,11,72,256]{3,2,1,0:T(8,128)S(1)}, f32[3,8,3,256]{3,2,1,0:T(4,128)S(1)}, f32[3,3,64,256]{3,2,1,0:T(8,128)}, f32[3,3,3,256]{3,2,1,0:T(4,128)S(1)}) custom-call(s32[32,4]{1,0:T(8,128)S(1)} %copy.34.counts, s32[32,4,512]{2,1,0:T(4,128)S(1)} %copy-done.14, s32[32,4,512]{2,1,0:T(4,128)S(1)} %copy-done.16, f32[3,32,4,512]{3,2,1,0:T(4,128)S(1)} %copy-done.10, ...), custom_call_target="tpu_custom_call" | custom-call | flops 16609443840 | bytes 12582912 | tf_op jit(solution)/shard_map/deposit/pallas_call | solution.py:264
  23.1 6.1 %all-to-all-start = ((f32[32,2,4,8,128]{4,3,2,1,0:T(8,128)}), f32[32,2,4,8,128]{4,3,2,1,0:T(8,128)}, u32[]{:S(2)}, u32[]{:S(2)}) async-start(f32[32,2,4,8,128]{4,3,2,1,0:T(8,128)} %copy-done.9), calls=%async_computation | async-start | bytes 2097152 | tf_op jit(solution)/shard_map/all_to_all | solution.py:691
  33.5 19.2 %deposit.3 = (f32[3,24,72,256]{3,2,1,0:T(8,128)}, f32[3,24,3,256]{3,2,1,0:T(4,128)S(1)}) custom-call(s32[32,4]{1,0:T(8,128)S(1)} %copy.35.counts, s32[32,4,512]{2,1,0:T(4,128)S(1)} %copy-done.15, s32[32,4,512]{2,1,0:T(4,128)S(1)} %copy-done.17, f32[3,32,4,512]{3,2,1,0:T(4,128)S(1)} %copy-done.11, f32[3,32,4,512]{3,2,1,0:T(4,128)S(1)} %copy-done.13), custom_call_target="tpu_custom_call" | custom-call | flops 36238786560 | bytes 12582912 | tf_op jit(solution)/shard_map/deposit/pallas_call | solution.py:264
  53.5 5.3 %collective-permute-start.3 = (f32[3,3,3,256]{3,2,1,0:T(4,128)S(1)}, f32[3,3,3,256]{3,2,1,0:T(4,128)S(1)}, u32[]{:S(2)}, u32[]{:S(2)}) collective-permute-start(f32[3,3,3,256]{3,2,1,0:T(4,128)S(1)} %copy-done.19), channel_id=1, source_target_pairs={{0,5},{1,6},{2,7},{3,4},{4,9},{5,10},{6,11},{7,8},{8,13},{9,14},{1... | collective-permute-start | bytes 82952 | tf_op jit(solution)/shard_map/ppermute | solution.py:292
  59.9 6.1 %z_forward.5 = (f32[3,32,64,256]{3,2,1,0:T(8,128)}, f32[32,2,4,24,128]{4,3,2,1,0:T(8,128)S(1)}) custom-call(f32[3,24,72,256]{3,2,1,0:T(8,128)} %get-tuple-element.60.refs_0_, f32[3,24,3,256]{3,2,1,0:T(4,128)S(1)} %collective-permute-done.1.refs_1_, f32[3,3,64,256]{3,2,1,0:T(8,128)S(1)} %collective-permute-done.2.refs_2_, ...), custom_call_target="tpu_custom_call", output_to_operand_aliasing={{0}: (5, {})} | custom-call | flops 1207959552 | bytes 9437184 | tf_op jit(solution)/shard_map/z_forward/pallas_call | solution.py:359
  68.4 10.6 %all-to-all-start.1 = ((f32[32,2,4,24,128]{4,3,2,1,0:T(8,128)}), f32[32,2,4,24,128]{4,3,2,1,0:T(8,128)}, u32[]{:S(2)}, u32[]{:S(2)}) async-start(f32[32,2,4,24,128]{4,3,2,1,0:T(8,128)} %copy-done.4), calls=%async_computation.1 | async-start | bytes 6291456 | tf_op jit(solution)/shard_map/all_to_all | solution.py:691
  80.0 3.7 z_forward.6
  86.0 62.1 %all-to-all-done.1 = f32[32,2,4,24,128]{4,3,2,1,0:T(8,128)} async-done(((f32[32,2,4,24,128]{4,3,2,1,0:T(8,128)}), f32[32,2,4,24,128]{4,3,2,1,0:T(8,128)}, u32[]{:S(2)}, u32[]{:S(2)}) %all-to-all-start.1) | async-done | bytes 3145760 | tf_op jit(solution)/shard_map/all_to_all | solution.py:691
  148.2 6.4 %all-to-all-start.2 = ((f32[32,1,4,32,128]{4,3,2,1,0:T(8,128)}), f32[32,1,4,32,128]{4,3,2,1,0:T(8,128)}, u32[]{:S(2)}, u32[]{:S(2)}) async-start(f32[32,1,4,32,128]{4,3,2,1,0:T(8,128)} %copy-done), calls=%async_computation.2 | async-start | bytes 4194304 | tf_op jit(solution)/shard_map/all_to_all | solution.py:691
  157.4 12.9 %plane_forward.3.refs_1_.refs_2_.refs_4_.refs_5_.refs_0_.refs_3_ = f32[2,5,512,256]{3,2,1,0:T(8,128)} custom-call(s32[1]{0:T(128)} %bitcast.start, f32[8,4,2,4,24,128]{5,4,3,2,1,0:T(8,128)} %bitcast.2.refs_0_, f32[8,4,2,4,8,128]{5,4,3,2,1,0:T(8,128)} %bitcast.3.refs_1_, bf16[1536,512]{1,0:T(8,128)(2,1)S(1)} %copy-done.22, bf16[512,1536]{1,0:T(8,128)(2,1)S(1)} %copy-done.20), custom_call_target="tpu_custom_call" | custom-call | flops 6442450944 | bytes 8388608 | tf_op jit(solution)/shard_map/plane_forward/pallas_call | solution.py:471
  170.3 10.1 %plane_inverse.3 = f32[8,4,4,32,128]{4,3,2,1,0:T(8,128)} custom-call(s32[1]{0:T(128)} %bitcast.start, f32[2,5,512,256]{3,2,1,0:T(8,128)} %plane_forward.3.refs_1_.refs_2_.refs_4_.refs_5_.refs_0_.refs_3_, f32[2,5,512,256]{3,2,1,0:T(8,128)} %plane_forward.3.refs_1_.refs_2_.refs_4_.refs_5_.refs_0_.refs_3_, ...), custom_call_target="tpu_custom_call" | custom-call | flops 3221225472 | bytes 6291456 | tf_op jit(solution)/shard_map/plane_inverse/pallas_call | solution.py:565
  180.4 21.5 %all-to-all-done.2 = f32[32,1,4,32,128]{4,3,2,1,0:T(8,128)} async-done(((f32[32,1,4,32,128]{4,3,2,1,0:T(8,128)}), f32[32,1,4,32,128]{4,3,2,1,0:T(8,128)}, u32[]{:S(2)}, u32[]{:S(2)}) %all-to-all-start.2) | async-done | bytes 2097184 | tf_op jit(solution)/shard_map/all_to_all | solution.py:691
  201.9 5.7 %all-to-all-start.3 = ((f32[32,4,32,128]{3,2,1,0:T(8,128)}), f32[32,4,32,128]{3,2,1,0:T(8,128)}, u32[]{:S(2)}, u32[]{:S(2)}) async-start(f32[32,4,32,128]{3,2,1,0:T(8,128)} %bitcast.6), calls=%async_computation.3 | async-start | bytes 4194304 | tf_op jit(solution)/shard_map/all_to_all | solution.py:691
  210.4 6.7 %plane_forward.2.refs_0_.refs_3_ = f32[1,5,512,256]{3,2,1,0:T(8,128)} custom-call(s32[1]{0:T(128)} %bitcast.start, f32[8,4,1,4,32,128]{5,4,3,2,1,0:T(8,128)} %bitcast.1.refs_0_, bf16[1536,512]{1,0:T(8,128)(2,1)S(1)} %copy-done.23, bf16[512,1536]{1,0:T(8,128)(2,1)S(1)} %copy-done.21), custom_call_target="tpu_custom_call" | custom-call | flops 3221225472 | bytes 4194304 | tf_op jit(solution)/shard_map/plane_forward/pallas_call | solution.py:471
  217.1 14.3 %plane_inverse.2 = (f32[8,4,4,32,128]{4,3,2,1,0:T(8,128)S(1)}, f32[8,4,4,32,128]{4,3,2,1,0:T(8,128)}) custom-call(s32[1]{0:T(128)} %bitcast.start, f32[1,5,512,256]{3,2,1,0:T(8,128)} %plane_forward.2.refs_0_.refs_3_, f32[2,5,512,256]{3,2,1,0:T(8,128)} %plane_forward.3.refs_1_.refs_2_.refs_4_.refs_5_.refs_0_.refs_3_, ...), custom_call_target="tpu_custom_call" | custom-call | flops 6442450944 | bytes 12582912 | tf_op jit(solution)/shard_map/plane_inverse/pallas_call | solution.py:565
  232.8 22.1 %all-to-all-done.3.received = f32[32,4,32,128]{3,2,1,0:T(8,128)} async-done(((f32[32,4,32,128]{3,2,1,0:T(8,128)}), f32[32,4,32,128]{3,2,1,0:T(8,128)}, u32[]{:S(2)}, u32[]{:S(2)}) %all-to-all-start.3) | async-done | bytes 2097184 | tf_op jit(solution)/shard_map/all_to_all | solution.py:691
  254.9 5.7 %all-to-all-start.4 = ((f32[32,4,32,128]{3,2,1,0:T(8,128)}), f32[32,4,32,128]{3,2,1,0:T(8,128)}, u32[]{:S(2)}, u32[]{:S(2)}) async-start(f32[32,4,32,128]{3,2,1,0:T(8,128)} %bitcast.7), calls=%async_computation.4 | async-start | bytes 4194304 | tf_op jit(solution)/shard_map/all_to_all | solution.py:691
  268.6 5.4 %collective-permute-done.6.low_y = f32[32,2,256]{2,1,0:T(2,128)S(1)} collective-permute-done((f32[32,2,256]{2,1,0:T(2,128)S(1)}, f32[32,2,256]{2,1,0:T(2,128)S(1)}, u32[]{:S(2)}, u32[]{:S(2)}) %collective-permute-start.6) | collective-permute-done | bytes 65568 | tf_op jit(solution)/shard_map/ppermute | solution.py:297
  277.1 33.7 %collective-permute-done.4.low_x = f32[2,64,256]{2,1,0:T(8,128)S(1)} collective-permute-done((f32[2,64,256]{2,1,0:T(8,128)S(1)}, f32[2,64,256]{2,1,0:T(8,128)S(1)}, u32[]{:S(2)}, u32[]{:S(2)}) %collective-permute-start.4) | collective-permute-done | bytes 131104 | tf_op jit(solution)/shard_map/ppermute | solution.py:297
  310.8 4.7 %all-to-all-start.5 = ((f32[32,4,32,128]{3,2,1,0:T(8,128)}), f32[32,4,32,128]{3,2,1,0:T(8,128)}, u32[]{:S(2)}, u32[]{:S(2)}) async-start(f32[32,4,32,128]{3,2,1,0:T(8,128)} %bitcast.8), calls=%async_computation.5 | async-start | bytes 4194304 | tf_op jit(solution)/shard_map/all_to_all | solution.py:691
  323.5 6.3 %stretch.3 = (f32[3,32,64,256]{3,2,1,0:T(8,128)}, f32[3,32,64,256]{3,2,1,0:T(8,128)}) custom-call(f32[3,32,64,256]{3,2,1,0:T(8,128)} %get-tuple-element.49.vorticity, f32[32,64,256]{2,1,0:T(8,128)S(1)} %get-tuple-element.86.field.before.after, f32[32,64,256]{2,1,0:T(8,128)S(1)} %get-tuple-element.86.field.before.after, ...), custom_call_target="tpu_custom_call" | custom-call | flops 314572800 | bytes 14680064 | tf_op jit(solution)/shard_map/stretch/pallas_call | solution.py:663
  331.9 33.7 %collective-permute-done.8.low_x = f32[2,64,256]{2,1,0:T(8,128)S(1)} collective-permute-done((f32[2,64,256]{2,1,0:T(8,128)S(1)}, f32[2,64,256]{2,1,0:T(8,128)S(1)}, u32[]{:S(2)}, u32[]{:S(2)}) %collective-permute-start.8) | collective-permute-done | bytes 131104 | tf_op jit(solution)/shard_map/ppermute | solution.py:297
  365.6 6.3 %stretch.4 = (f32[3,32,64,256]{3,2,1,0:T(8,128)}, f32[3,32,64,256]{3,2,1,0:T(8,128)}) custom-call(f32[3,32,64,256]{3,2,1,0:T(8,128)} %get-tuple-element.49.vorticity, f32[32,64,256]{2,1,0:T(8,128)S(1)} %get-tuple-element.81.field.before.after, ...), custom_call_target="tpu_custom_call", output_to_operand_aliasing={{0}: (9, {}), {1}: (10, {})} | custom-call | flops 314572800 | bytes 14680064 | tf_op jit(solution)/shard_map/stretch/pallas_call | solution.py:663
  384.3 6.3 %stretch.5 = (f32[3,32,64,256]{3,2,1,0:T(8,128)}, f32[3,32,64,256]{3,2,1,0:T(8,128)}) custom-call(f32[3,32,64,256]{3,2,1,0:T(8,128)} %get-tuple-element.49.vorticity, f32[32,64,256]{2,1,0:T(8,128)S(1)} %get-tuple-element.92.field.before.after, ...), custom_call_target="tpu_custom_call", output_to_operand_aliasing={{0}: (9, {}), {1}: (10, {})} | custom-call | flops 314572800 | bytes 14680064 | tf_op jit(solution)/shard_map/stretch/pallas_call | solution.py:663
  (90 shorter events, 63.6 us)
Async XLA Ops:
  16.7 3.9 collective-permute-start
  19.0 41.0 %collective-permute-start.2 = (f32[3,3,64,256]{3,2,1,0:T(8,128)}, f32[3,3,64,256]{3,2,1,0:T(8,128)S(1)}, u32[]{:S(2)}, u32[]{:S(2)}) collective-permute-start(f32[3,3,64,256]{3,2,1,0:T(8,128)} %get-tuple-element.62), channel_id=1, source_target_pairs={{0,4},{1,5},{2,6},{3,7},{4,8},{5,9},{6,10},{7,11},{8,12},{9,13},{1... | collective-permute-start | bytes 1769480 | tf_op jit(solution)/shard_map/ppermute | solution.py:292
  23.1 45.3 %all-to-all-start = ((f32[32,2,4,8,128]{4,3,2,1,0:T(8,128)}), f32[32,2,4,8,128]{4,3,2,1,0:T(8,128)}, u32[]{:S(2)}, u32[]{:S(2)}) async-start(f32[32,2,4,8,128]{4,3,2,1,0:T(8,128)} %copy-done.9), calls=%async_computation | async-start | bytes 2097152 | tf_op jit(solution)/shard_map/all_to_all | solution.py:691
  33.5 20.1 %copy-start.19 = (f32[3,3,3,256]{3,2,1,0:T(4,128)S(1)}, f32[3,3,3,256]{3,2,1,0:T(4,128)}, u32[]{:S(2)}) copy-start(f32[3,3,3,256]{3,2,1,0:T(4,128)} %copy-done.18) | copy-start | bytes 82948
  52.7 7.2 %collective-permute-start.1 = (f32[3,24,3,256]{3,2,1,0:T(4,128)S(1)}, f32[3,24,3,256]{3,2,1,0:T(4,128)S(1)}, u32[]{:S(2)}, u32[]{:S(2)}) collective-permute-start(f32[3,24,3,256]{3,2,1,0:T(4,128)S(1)} %get-tuple-element.61), channel_id=1, source_target_pairs={{0,1},{1,2},{2,3},{3,0},{4,5},{5,6},{6,7},{7,4},{8,9},{9,10},{10,1... | collective-permute-start | bytes 663560 | tf_op jit(solution)/shard_map/ppermute | solution.py:292
  53.5 6.4 %collective-permute-start.3 = (f32[3,3,3,256]{3,2,1,0:T(4,128)S(1)}, f32[3,3,3,256]{3,2,1,0:T(4,128)S(1)}, u32[]{:S(2)}, u32[]{:S(2)}) collective-permute-start(f32[3,3,3,256]{3,2,1,0:T(4,128)S(1)} %copy-done.19), channel_id=1, source_target_pairs={{0,5},{1,6},{2,7},{3,4},{4,9},{5,10},{6,11},{7,8},{8,13},{9,14},{1... | collective-permute-start | bytes 82952 | tf_op jit(solution)/shard_map/ppermute | solution.py:292
  68.4 79.8 %all-to-all-start.1 = ((f32[32,2,4,24,128]{4,3,2,1,0:T(8,128)}), f32[32,2,4,24,128]{4,3,2,1,0:T(8,128)}, u32[]{:S(2)}, u32[]{:S(2)}) async-start(f32[32,2,4,24,128]{4,3,2,1,0:T(8,128)} %copy-done.4), calls=%async_computation.1 | async-start | bytes 6291456 | tf_op jit(solution)/shard_map/all_to_all | solution.py:691
  148.2 53.7 %all-to-all-start.2 = ((f32[32,1,4,32,128]{4,3,2,1,0:T(8,128)}), f32[32,1,4,32,128]{4,3,2,1,0:T(8,128)}, u32[]{:S(2)}, u32[]{:S(2)}) async-start(f32[32,1,4,32,128]{4,3,2,1,0:T(8,128)} %copy-done), calls=%async_computation.2 | async-start | bytes 4194304 | tf_op jit(solution)/shard_map/all_to_all | solution.py:691
  201.9 53.0 %all-to-all-start.3 = ((f32[32,4,32,128]{3,2,1,0:T(8,128)}), f32[32,4,32,128]{3,2,1,0:T(8,128)}, u32[]{:S(2)}, u32[]{:S(2)}) async-start(f32[32,4,32,128]{3,2,1,0:T(8,128)} %bitcast.6), calls=%async_computation.3 | async-start | bytes 4194304 | tf_op jit(solution)/shard_map/all_to_all | solution.py:691
  232.8 27.8 %copy-start.24 = (bf16[768,256]{1,0:T(8,128)(2,1)S(1)}, bf16[768,256]{1,0:T(8,128)(2,1)}, u32[]{:S(2)}) copy-start(bf16[768,256]{1,0:T(8,128)(2,1)} %constant.30.clone.table) | copy-start | bytes 1179652
  254.9 55.9 %all-to-all-start.4 = ((f32[32,4,32,128]{3,2,1,0:T(8,128)}), f32[32,4,32,128]{3,2,1,0:T(8,128)}, u32[]{:S(2)}, u32[]{:S(2)}) async-start(f32[32,4,32,128]{3,2,1,0:T(8,128)} %bitcast.7), calls=%async_computation.4 | async-start | bytes 4194304 | tf_op jit(solution)/shard_map/all_to_all | solution.py:691
  264.2 46.6 %collective-permute-start.4 = (f32[2,64,256]{2,1,0:T(8,128)S(1)}, f32[2,64,256]{2,1,0:T(8,128)S(1)}, u32[]{:S(2)}, u32[]{:S(2)}) collective-permute-start(f32[2,64,256]{2,1,0:T(8,128)S(1)} %get-tuple-element.76), channel_id=1, source_target_pairs={{0,4},{4,8},{8,12},{12,16},{16,20},{20,24},{24,28},{28,0},{1,5},{5... | collective-permute-start | bytes 393224 | tf_op jit(solution)/shard_map/ppermute | solution.py:297
  265.4 45.3 %collective-permute-start.5 = (f32[2,64,256]{2,1,0:T(8,128)S(1)}, f32[2,64,256]{2,1,0:T(8,128)S(1)}, u32[]{:S(2)}, u32[]{:S(2)}) collective-permute-start(f32[2,64,256]{2,1,0:T(8,128)S(1)} %get-tuple-element.77), channel_id=1, source_target_pairs={{0,28},{4,0},{8,4},{12,8},{16,12},{20,16},{24,20},{28,24},{1,29},{... | collective-permute-start | bytes 393224 | tf_op jit(solution)/shard_map/ppermute | solution.py:297
  266.6 7.4 %collective-permute-start.6 = (f32[32,2,256]{2,1,0:T(2,128)S(1)}, f32[32,2,256]{2,1,0:T(2,128)S(1)}, u32[]{:S(2)}, u32[]{:S(2)}) collective-permute-start(f32[32,2,256]{2,1,0:T(2,128)S(1)} %get-tuple-element.78), channel_id=1, source_target_pairs={{0,1},{1,2},{2,3},{3,0},{4,5},{5,6},{6,7},{7,4},{8,9},{9,10},{10,1... | collective-permute-start | bytes 196616 | tf_op jit(solution)/shard_map/ppermute | solution.py:297
  268.6 8.5 %collective-permute-start.7 = (f32[32,2,256]{2,1,0:T(2,128)S(1)}, f32[32,2,256]{2,1,0:T(2,128)S(1)}, u32[]{:S(2)}, u32[]{:S(2)}) collective-permute-start(f32[32,2,256]{2,1,0:T(2,128)S(1)} %get-tuple-element.79), channel_id=1, source_target_pairs={{0,3},{1,0},{2,1},{3,2},{4,7},{5,4},{6,5},{7,6},{8,11},{9,8},{10,9... | collective-permute-start | bytes 196616 | tf_op jit(solution)/shard_map/ppermute | solution.py:297
  310.8 61.2 %all-to-all-start.5 = ((f32[32,4,32,128]{3,2,1,0:T(8,128)}), f32[32,4,32,128]{3,2,1,0:T(8,128)}, u32[]{:S(2)}, u32[]{:S(2)}) async-start(f32[32,4,32,128]{3,2,1,0:T(8,128)} %bitcast.8), calls=%async_computation.5 | async-start | bytes 4194304 | tf_op jit(solution)/shard_map/all_to_all | solution.py:691
  319.1 46.5 %collective-permute-start.8 = (f32[2,64,256]{2,1,0:T(8,128)S(1)}, f32[2,64,256]{2,1,0:T(8,128)S(1)}, u32[]{:S(2)}, u32[]{:S(2)}) collective-permute-start(f32[2,64,256]{2,1,0:T(8,128)S(1)} %get-tuple-element.82), channel_id=1, source_target_pairs={{0,4},{4,8},{8,12},{12,16},{16,20},{20,24},{24,28},{28,0},{1,5},{5... | collective-permute-start | bytes 393224 | tf_op jit(solution)/shard_map/ppermute | solution.py:297
  320.3 45.3 %collective-permute-start.9 = (f32[2,64,256]{2,1,0:T(8,128)S(1)}, f32[2,64,256]{2,1,0:T(8,128)S(1)}, u32[]{:S(2)}, u32[]{:S(2)}) collective-permute-start(f32[2,64,256]{2,1,0:T(8,128)S(1)} %get-tuple-element.83), channel_id=1, source_target_pairs={{0,28},{4,0},{8,4},{12,8},{16,12},{20,16},{24,20},{28,24},{1,29},{... | collective-permute-start | bytes 393224 | tf_op jit(solution)/shard_map/ppermute | solution.py:297
  321.5 8.3 %collective-permute-start.10 = (f32[32,2,256]{2,1,0:T(2,128)S(1)}, f32[32,2,256]{2,1,0:T(2,128)S(1)}, u32[]{:S(2)}, u32[]{:S(2)}) collective-permute-start(f32[32,2,256]{2,1,0:T(2,128)S(1)} %get-tuple-element.84), channel_id=1, source_target_pairs={{0,1},{1,2},{2,3},{3,0},{4,5},{5,6},{6,7},{7,4},{8,9},{9,10},{10,1... | collective-permute-start | bytes 196616 | tf_op jit(solution)/shard_map/ppermute | solution.py:297
  323.5 8.5 %collective-permute-start.11 = (f32[32,2,256]{2,1,0:T(2,128)S(1)}, f32[32,2,256]{2,1,0:T(2,128)S(1)}, u32[]{:S(2)}, u32[]{:S(2)}) collective-permute-start(f32[32,2,256]{2,1,0:T(2,128)S(1)} %get-tuple-element.85), channel_id=1, source_target_pairs={{0,3},{1,0},{2,1},{3,2},{4,7},{5,4},{6,5},{7,6},{8,11},{9,8},{10,9... | collective-permute-start | bytes 196616 | tf_op jit(solution)/shard_map/ppermute | solution.py:297
  375.5 8.8 %collective-permute-start.12 = (f32[2,64,256]{2,1,0:T(8,128)S(1)}, f32[2,64,256]{2,1,0:T(8,128)S(1)}, u32[]{:S(2)}, u32[]{:S(2)}) collective-permute-start(f32[2,64,256]{2,1,0:T(8,128)S(1)} %get-tuple-element.93), channel_id=1, source_target_pairs={{0,4},{4,8},{8,12},{12,16},{16,20},{20,24},{24,28},{28,0},{1,5},{5... | collective-permute-start | bytes 393224 | tf_op jit(solution)/shard_map/ppermute | solution.py:297
  375.5 8.7 %collective-permute-start.13 = (f32[2,64,256]{2,1,0:T(8,128)S(1)}, f32[2,64,256]{2,1,0:T(8,128)S(1)}, u32[]{:S(2)}, u32[]{:S(2)}) collective-permute-start(f32[2,64,256]{2,1,0:T(8,128)S(1)} %get-tuple-element.94), channel_id=1, source_target_pairs={{0,28},{4,0},{8,4},{12,8},{16,12},{20,16},{24,20},{28,24},{1,29},{... | collective-permute-start | bytes 393224 | tf_op jit(solution)/shard_map/ppermute | solution.py:297
  377.9 4.3 %collective-permute-start.14 = (f32[32,2,256]{2,1,0:T(2,128)S(1)}, f32[32,2,256]{2,1,0:T(2,128)S(1)}, u32[]{:S(2)}, u32[]{:S(2)}) collective-permute-start(f32[32,2,256]{2,1,0:T(2,128)S(1)} %get-tuple-element.95), channel_id=1, source_target_pairs={{0,1},{1,2},{2,3},{3,0},{4,5},{5,6},{6,7},{7,4},{8,9},{9,10},{10,1... | collective-permute-start | bytes 196616 | tf_op jit(solution)/shard_map/ppermute | solution.py:297
  380.6 3.7 collective-permute-start.15
  (24 other events, 83.8 us)

commit v6 on v5

--- a/solution.py
+++ b/solution.py
@@ -275,7 +275,7 @@
             pltpu.VMEM((3, sources, blocks, slots), jnp.float32),
             pltpu.SemaphoreType.DMA((4,)),
         ],
-        compiler_params=vmem(),
+        compiler_params=vmem(60),
         cost_estimate=cost(10 * sources * blocks * 288 * slots * NZ, 12 * MIB),
         name="deposit",
     )(*particles)

time: 391 us -> 385 us (0.985)
  local copies, waits for them, and re-layouts: 21.8 us -> 13 us
    unnamed x53 -> x33, local copies, waits for them, and re-layouts: 21.8 us -> 12.3 us
  transfers between devices with their start and end apart: 22 -> 22, of which waited for: 12 -> 11; matrix products, arithmetic and copies ran while one was open for 0% -> 0% of each run, Pallas kernels for 24% -> 26%
where the time goes in v6:
time: 385 us; the launch traced here: 382 us
  waiting for transfers between devices  189 us (49%)
  Pallas kernels  119 us (31%)
  starting transfers between devices  59.5 us (15%)
  local copies, waits for them, and re-layouts  13 us (3%)
    all_to_all x6, waiting for transfers between devices, exchange(): return lax.all_to_all(blocks_out, AXES, 0, 0, tiled=True)  106 us
    ppermute x12, waiting for transfers between devices, shifted(): lax.ppermute(block, axis, [(i, (i + distance) % count) for i in range(cou...  81.7 us
    all_to_all x6, starting transfers between devices, exchange(): return lax.all_to_all(blocks_out, AXES, 0, 0, tiled=True)  36.3 us
    pallas_call x2, Pallas kernels, deposit(): pl.pallas_call(functools.partial(deposit_kernel, begin, end), out_shape=[...  31.1 us
    pallas_call x2, Pallas kernels, plane_inverse(): pl.pallas_call(functools.partial(plane_inverse_kernel, parts, needs), gri...  24.5 us
    pallas_call x2, Pallas kernels, plane_forward(): pl.pallas_call(plane_forward_kernel, grid=(count, depth + 1), in_specs=[p...  19.5 us
    pallas_call x3, Pallas kernels, stretch(): pl.pallas_call(stretch_kernel, grid=(planes // STEP,), in_specs=specs, ou...  19 us
    pallas_call x4, Pallas kernels, z_forward(): pl.pallas_call(kernel, grid=(count, here), in_specs=specs, out_specs=(pl....  14.6 us
  transfers between devices with their start and end apart: 22, of which 11 were waited for; matrix products, arithmetic and copies ran while one was open for 0% of the time, Pallas kernels for 26%

profile of v6, /device:TPU:17, one launch (start us, length us, event | category | flops | bytes accessed | tf_op | source)
XLA Modules:
  0.0 382.2 jit_solution(5590956501655518011)
XLA Ops:
  2.0 10.2 %deposit.2 = (f32[3,11,72,256]{3,2,1,0:T(8,128)}, f32[3,8,3,256]{3,2,1,0:T(4,128)}, f32[3,3,64,256]{3,2,1,0:T(8,128)}, f32[3,3,3,256]{3,2,1,0:T(4,128)}) custom-call(s32[32,4]{1,0:T(8,128)} %copy.34.counts, s32[32,4,512]{2,1,0:T(4,128)} %row_base.2, s32[32,4,512]{2,1,0:T(4,128)} %z_base.2, f32[3,32,4,512]{3,2,1,0:T(4,128)} %fractions.2, ...), custom_call_target="tpu_custom_call" | custom-call | flops 16609443840 | bytes 12582912 | tf_op jit(solution)/shard_map/deposit/pallas_call | solution.py:264
  20.2 6.7 %all-to-all-start = ((f32[32,2,4,8,128]{4,3,2,1,0:T(8,128)}), f32[32,2,4,8,128]{4,3,2,1,0:T(8,128)S(1)}, u32[]{:S(2)}, u32[]{:S(2)}) async-start(f32[32,2,4,8,128]{4,3,2,1,0:T(8,128)} %get-tuple-element.54), calls=%async_computation | async-start | bytes 2097152 | tf_op jit(solution)/shard_map/all_to_all | solution.py:691
  27.6 20.9 %deposit.3 = (f32[3,24,72,256]{3,2,1,0:T(8,128)}, f32[3,24,3,256]{3,2,1,0:T(4,128)}) custom-call(s32[32,4]{1,0:T(8,128)} %copy.35.counts, s32[32,4,512]{2,1,0:T(4,128)} %row_base.2, s32[32,4,512]{2,1,0:T(4,128)} %z_base.2, f32[3,32,4,512]{3,2,1,0:T(4,128)} %fractions.2, f32[3,32,4,512]{3,2,1,0:T(4,128)} %strength.2), custom_call_target="tpu_custom_call" | custom-call | flops 36238786560 | bytes 12582912 | tf_op jit(solution)/shard_map/deposit/pallas_call | solution.py:264
  55.4 6.9 %z_forward.5 = (f32[3,32,64,256]{3,2,1,0:T(8,128)}, f32[32,2,4,24,128]{4,3,2,1,0:T(8,128)}) custom-call(f32[3,24,72,256]{3,2,1,0:T(8,128)} %get-tuple-element.60.refs_0_, f32[3,24,3,256]{3,2,1,0:T(4,128)S(1)} %collective-permute-done.1.refs_1_, f32[3,3,64,256]{3,2,1,0:T(8,128)S(1)} %collective-permute-done.2.refs_2_, ...), custom_call_target="tpu_custom_call", output_to_operand_aliasing={{0}: (5, {})} | custom-call | flops 1207959552 | bytes 9437184 | tf_op jit(solution)/shard_map/z_forward/pallas_call | solution.py:359
  63.4 7.2 %all-to-all-start.1 = ((f32[32,2,4,24,128]{4,3,2,1,0:T(8,128)}), f32[32,2,4,24,128]{4,3,2,1,0:T(8,128)}, u32[]{:S(2)}, u32[]{:S(2)}) async-start(f32[32,2,4,24,128]{4,3,2,1,0:T(8,128)} %get-tuple-element.71), calls=%async_computation.1 | async-start | bytes 6291456 | tf_op jit(solution)/shard_map/all_to_all | solution.py:691
  70.7 4.6 %z_forward.6 = (f32[3,32,64,256]{3,2,1,0:T(8,128)}, f32[32,1,4,32,128]{4,3,2,1,0:T(8,128)}) custom-call(f32[3,24,72,256]{3,2,1,0:T(8,128)} %get-tuple-element.60.refs_0_, f32[3,24,3,256]{3,2,1,0:T(4,128)S(1)} %collective-permute-done.1.refs_1_, f32[3,3,64,256]{3,2,1,0:T(8,128)S(1)} %collective-permute-done.2.refs_2_, ...), custom_call_target="tpu_custom_call", output_to_operand_aliasing={{0}: (5, {})} | custom-call | flops 603979776 | bytes 4718592 | tf_op jit(solution)/shard_map/z_forward/pallas_call | solution.py:359
  76.6 63.2 %all-to-all-done.1 = f32[32,2,4,24,128]{4,3,2,1,0:T(8,128)} async-done(((f32[32,2,4,24,128]{4,3,2,1,0:T(8,128)}), f32[32,2,4,24,128]{4,3,2,1,0:T(8,128)}, u32[]{:S(2)}, u32[]{:S(2)}) %all-to-all-start.1) | async-done | bytes 3145760 | tf_op jit(solution)/shard_map/all_to_all | solution.py:691
  139.8 6.4 %all-to-all-start.2 = ((f32[32,1,4,32,128]{4,3,2,1,0:T(8,128)}), f32[32,1,4,32,128]{4,3,2,1,0:T(8,128)}, u32[]{:S(2)}, u32[]{:S(2)}) async-start(f32[32,1,4,32,128]{4,3,2,1,0:T(8,128)} %get-tuple-element.72), calls=%async_computation.2 | async-start | bytes 4194304 | tf_op jit(solution)/shard_map/all_to_all | solution.py:691
  150.3 12.8 %plane_forward.3.refs_1_.refs_2_.refs_4_.refs_5_.refs_0_.refs_3_ = f32[2,5,512,256]{3,2,1,0:T(8,128)} custom-call(s32[1]{0:T(128)} %bitcast.start, f32[8,4,2,4,24,128]{5,4,3,2,1,0:T(8,128)} %bitcast.2.refs_0_, f32[8,4,2,4,8,128]{5,4,3,2,1,0:T(8,128)S(1)} %bitcast.8, bf16[1536,512]{1,0:T(8,128)(2,1)S(1)} %copy-done.11, bf16[512,1536]{1,0:T(8,128)(2,1)S(1)} %copy-done.9), custom_call_target="tpu_custom_call" | custom-call | flops 6442450944 | bytes 8388608 | tf_op jit(solution)/shard_map/plane_forward/pallas_call | solution.py:471
  163.1 10.2 %plane_inverse.3 = f32[8,4,4,32,128]{4,3,2,1,0:T(8,128)} custom-call(s32[1]{0:T(128)} %bitcast.start, f32[2,5,512,256]{3,2,1,0:T(8,128)} %plane_forward.3.refs_1_.refs_2_.refs_4_.refs_5_.refs_0_.refs_3_, f32[2,5,512,256]{3,2,1,0:T(8,128)} %plane_forward.3.refs_1_.refs_2_.refs_4_.refs_5_.refs_0_.refs_3_, ...), custom_call_target="tpu_custom_call" | custom-call | flops 3221225472 | bytes 6291456 | tf_op jit(solution)/shard_map/plane_inverse/pallas_call | solution.py:565
  173.3 20.3 %all-to-all-done.2 = f32[32,1,4,32,128]{4,3,2,1,0:T(8,128)} async-done(((f32[32,1,4,32,128]{4,3,2,1,0:T(8,128)}), f32[32,1,4,32,128]{4,3,2,1,0:T(8,128)}, u32[]{:S(2)}, u32[]{:S(2)}) %all-to-all-start.2) | async-done | bytes 2097184 | tf_op jit(solution)/shard_map/all_to_all | solution.py:691
  193.5 5.7 %all-to-all-start.3 = ((f32[32,4,32,128]{3,2,1,0:T(8,128)}), f32[32,4,32,128]{3,2,1,0:T(8,128)}, u32[]{:S(2)}, u32[]{:S(2)}) async-start(f32[32,4,32,128]{3,2,1,0:T(8,128)} %bitcast.6), calls=%async_computation.3 | async-start | bytes 4194304 | tf_op jit(solution)/shard_map/all_to_all | solution.py:691
  202.0 6.7 %plane_forward.2.refs_0_.refs_3_ = f32[1,5,512,256]{3,2,1,0:T(8,128)} custom-call(s32[1]{0:T(128)} %bitcast.start, f32[8,4,1,4,32,128]{5,4,3,2,1,0:T(8,128)} %bitcast.1.refs_0_, bf16[1536,512]{1,0:T(8,128)(2,1)S(1)} %copy-done.12, bf16[512,1536]{1,0:T(8,128)(2,1)S(1)} %copy-done.10), custom_call_target="tpu_custom_call" | custom-call | flops 3221225472 | bytes 4194304 | tf_op jit(solution)/shard_map/plane_forward/pallas_call | solution.py:471
  208.7 14.4 %plane_inverse.2 = (f32[8,4,4,32,128]{4,3,2,1,0:T(8,128)S(1)}, f32[8,4,4,32,128]{4,3,2,1,0:T(8,128)}) custom-call(s32[1]{0:T(128)} %bitcast.start, f32[1,5,512,256]{3,2,1,0:T(8,128)} %plane_forward.2.refs_0_.refs_3_, f32[2,5,512,256]{3,2,1,0:T(8,128)} %plane_forward.3.refs_1_.refs_2_.refs_4_.refs_5_.refs_0_.refs_3_, ...), custom_call_target="tpu_custom_call" | custom-call | flops 6442450944 | bytes 12582912 | tf_op jit(solution)/shard_map/plane_inverse/pallas_call | solution.py:565
  224.4 22.1 %all-to-all-done.3.received = f32[32,4,32,128]{3,2,1,0:T(8,128)} async-done(((f32[32,4,32,128]{3,2,1,0:T(8,128)}), f32[32,4,32,128]{3,2,1,0:T(8,128)}, u32[]{:S(2)}, u32[]{:S(2)}) %all-to-all-start.3) | async-done | bytes 2097184 | tf_op jit(solution)/shard_map/all_to_all | solution.py:691
  246.5 5.7 %all-to-all-start.4 = ((f32[32,4,32,128]{3,2,1,0:T(8,128)}), f32[32,4,32,128]{3,2,1,0:T(8,128)}, u32[]{:S(2)}, u32[]{:S(2)}) async-start(f32[32,4,32,128]{3,2,1,0:T(8,128)} %bitcast.7), calls=%async_computation.4 | async-start | bytes 4194304 | tf_op jit(solution)/shard_map/all_to_all | solution.py:691
  260.2 5.4 %collective-permute-done.6.low_y = f32[32,2,256]{2,1,0:T(2,128)S(1)} collective-permute-done((f32[32,2,256]{2,1,0:T(2,128)S(1)}, f32[32,2,256]{2,1,0:T(2,128)S(1)}, u32[]{:S(2)}, u32[]{:S(2)}) %collective-permute-start.6) | collective-permute-done | bytes 65568 | tf_op jit(solution)/shard_map/ppermute | solution.py:297
  268.7 33.7 %collective-permute-done.4.low_x = f32[2,64,256]{2,1,0:T(8,128)S(1)} collective-permute-done((f32[2,64,256]{2,1,0:T(8,128)S(1)}, f32[2,64,256]{2,1,0:T(8,128)S(1)}, u32[]{:S(2)}, u32[]{:S(2)}) %collective-permute-start.4) | collective-permute-done | bytes 131104 | tf_op jit(solution)/shard_map/ppermute | solution.py:297
  302.4 4.7 %all-to-all-start.5 = ((f32[32,4,32,128]{3,2,1,0:T(8,128)}), f32[32,4,32,128]{3,2,1,0:T(8,128)}, u32[]{:S(2)}, u32[]{:S(2)}) async-start(f32[32,4,32,128]{3,2,1,0:T(8,128)} %bitcast.9), calls=%async_computation.5 | async-start | bytes 4194304 | tf_op jit(solution)/shard_map/all_to_all | solution.py:691
  307.1 3.6 z_inverse.4
  315.1 6.3 %stretch.3 = (f32[3,32,64,256]{3,2,1,0:T(8,128)}, f32[3,32,64,256]{3,2,1,0:T(8,128)}) custom-call(f32[3,32,64,256]{3,2,1,0:T(8,128)} %get-tuple-element.49.vorticity, f32[32,64,256]{2,1,0:T(8,128)S(1)} %get-tuple-element.86.field.before.after, f32[32,64,256]{2,1,0:T(8,128)S(1)} %get-tuple-element.86.field.before.after, ...), custom_call_target="tpu_custom_call" | custom-call | flops 314572800 | bytes 14680064 | tf_op jit(solution)/shard_map/stretch/pallas_call | solution.py:663
  323.6 33.7 %collective-permute-done.8.low_x = f32[2,64,256]{2,1,0:T(8,128)S(1)} collective-permute-done((f32[2,64,256]{2,1,0:T(8,128)S(1)}, f32[2,64,256]{2,1,0:T(8,128)S(1)}, u32[]{:S(2)}, u32[]{:S(2)}) %collective-permute-start.8) | collective-permute-done | bytes 131104 | tf_op jit(solution)/shard_map/ppermute | solution.py:297
  357.2 6.3 %stretch.4 = (f32[3,32,64,256]{3,2,1,0:T(8,128)}, f32[3,32,64,256]{3,2,1,0:T(8,128)}) custom-call(f32[3,32,64,256]{3,2,1,0:T(8,128)} %get-tuple-element.49.vorticity, f32[32,64,256]{2,1,0:T(8,128)S(1)} %get-tuple-element.81.field.before.after, ...), custom_call_target="tpu_custom_call", output_to_operand_aliasing={{0}: (9, {}), {1}: (10, {})} | custom-call | flops 314572800 | bytes 14680064 | tf_op jit(solution)/shard_map/stretch/pallas_call | solution.py:663
  375.9 6.3 %stretch.5 = (f32[3,32,64,256]{3,2,1,0:T(8,128)}, f32[3,32,64,256]{3,2,1,0:T(8,128)}) custom-call(f32[3,32,64,256]{3,2,1,0:T(8,128)} %get-tuple-element.49.vorticity, f32[32,64,256]{2,1,0:T(8,128)S(1)} %get-tuple-element.92.field.before.after, ...), custom_call_target="tpu_custom_call", output_to_operand_aliasing={{0}: (9, {}), {1}: (10, {})} | custom-call | flops 314572800 | bytes 14680064 | tf_op jit(solution)/shard_map/stretch/pallas_call | solution.py:663
  (70 shorter events, 57.5 us)
Async XLA Ops:
  12.2 4.5 %collective-permute-start = (f32[3,8,3,256]{3,2,1,0:T(4,128)}, f32[3,8,3,256]{3,2,1,0:T(4,128)S(1)}, u32[]{:S(2)}, u32[]{:S(2)}) collective-permute-start(f32[3,8,3,256]{3,2,1,0:T(4,128)} %get-tuple-element.53), channel_id=1, source_target_pairs={{0,1},{1,2},{2,3},{3,0},{4,5},{5,6},{6,7},{7,4},{8,9},{9,10},{10,1... | collective-permute-start | bytes 221192 | tf_op jit(solution)/shard_map/ppermute | solution.py:292
  13.8 41.6 %collective-permute-start.2 = (f32[3,3,64,256]{3,2,1,0:T(8,128)}, f32[3,3,64,256]{3,2,1,0:T(8,128)S(1)}, u32[]{:S(2)}, u32[]{:S(2)}) collective-permute-start(f32[3,3,64,256]{3,2,1,0:T(8,128)} %get-tuple-element.62), channel_id=1, source_target_pairs={{0,4},{1,5},{2,6},{3,7},{4,8},{5,9},{6,10},{7,11},{8,12},{9,13},{1... | collective-permute-start | bytes 1769480 | tf_op jit(solution)/shard_map/ppermute | solution.py:292
  20.2 42.1 %all-to-all-start = ((f32[32,2,4,8,128]{4,3,2,1,0:T(8,128)}), f32[32,2,4,8,128]{4,3,2,1,0:T(8,128)S(1)}, u32[]{:S(2)}, u32[]{:S(2)}) async-start(f32[32,2,4,8,128]{4,3,2,1,0:T(8,128)} %get-tuple-element.54), calls=%async_computation | async-start | bytes 2097152 | tf_op jit(solution)/shard_map/all_to_all | solution.py:691
  27.6 23.0 %copy-start.15 = (f32[3,3,3,256]{3,2,1,0:T(4,128)S(1)}, f32[3,3,3,256]{3,2,1,0:T(4,128)}, u32[]{:S(2)}) copy-start(f32[3,3,3,256]{3,2,1,0:T(4,128)} %get-tuple-element.63) | copy-start | bytes 82948
  48.5 6.9 %collective-permute-start.1 = (f32[3,24,3,256]{3,2,1,0:T(4,128)}, f32[3,24,3,256]{3,2,1,0:T(4,128)S(1)}, u32[]{:S(2)}, u32[]{:S(2)}) collective-permute-start(f32[3,24,3,256]{3,2,1,0:T(4,128)} %get-tuple-element.61), channel_id=1, source_target_pairs={{0,1},{1,2},{2,3},{3,0},{4,5},{5,6},{6,7},{7,4},{8,9},{9,10},{10,1... | collective-permute-start | bytes 663560 | tf_op jit(solution)/shard_map/ppermute | solution.py:292
  50.6 4.8 %collective-permute-start.3 = (f32[3,3,3,256]{3,2,1,0:T(4,128)S(1)}, f32[3,3,3,256]{3,2,1,0:T(4,128)S(1)}, u32[]{:S(2)}, u32[]{:S(2)}) collective-permute-start(f32[3,3,3,256]{3,2,1,0:T(4,128)S(1)} %copy-done.15), channel_id=1, source_target_pairs={{0,5},{1,6},{2,7},{3,4},{4,9},{5,10},{6,11},{7,8},{8,13},{9,14},{1... | collective-permute-start | bytes 82952 | tf_op jit(solution)/shard_map/ppermute | solution.py:292
  63.4 76.4 %all-to-all-start.1 = ((f32[32,2,4,24,128]{4,3,2,1,0:T(8,128)}), f32[32,2,4,24,128]{4,3,2,1,0:T(8,128)}, u32[]{:S(2)}, u32[]{:S(2)}) async-start(f32[32,2,4,24,128]{4,3,2,1,0:T(8,128)} %get-tuple-element.71), calls=%async_computation.1 | async-start | bytes 6291456 | tf_op jit(solution)/shard_map/all_to_all | solution.py:691
  139.8 53.7 %all-to-all-start.2 = ((f32[32,1,4,32,128]{4,3,2,1,0:T(8,128)}), f32[32,1,4,32,128]{4,3,2,1,0:T(8,128)}, u32[]{:S(2)}, u32[]{:S(2)}) async-start(f32[32,1,4,32,128]{4,3,2,1,0:T(8,128)} %get-tuple-element.72), calls=%async_computation.2 | async-start | bytes 4194304 | tf_op jit(solution)/shard_map/all_to_all | solution.py:691
  193.5 53.0 %all-to-all-start.3 = ((f32[32,4,32,128]{3,2,1,0:T(8,128)}), f32[32,4,32,128]{3,2,1,0:T(8,128)}, u32[]{:S(2)}, u32[]{:S(2)}) async-start(f32[32,4,32,128]{3,2,1,0:T(8,128)} %bitcast.6), calls=%async_computation.3 | async-start | bytes 4194304 | tf_op jit(solution)/shard_map/all_to_all | solution.py:691
  224.4 27.8 %copy-start.13 = (bf16[768,256]{1,0:T(8,128)(2,1)S(1)}, bf16[768,256]{1,0:T(8,128)(2,1)}, u32[]{:S(2)}) copy-start(bf16[768,256]{1,0:T(8,128)(2,1)} %constant.30.clone.table) | copy-start | bytes 1179652
  246.5 55.9 %all-to-all-start.4 = ((f32[32,4,32,128]{3,2,1,0:T(8,128)}), f32[32,4,32,128]{3,2,1,0:T(8,128)}, u32[]{:S(2)}, u32[]{:S(2)}) async-start(f32[32,4,32,128]{3,2,1,0:T(8,128)} %bitcast.7), calls=%async_computation.4 | async-start | bytes 4194304 | tf_op jit(solution)/shard_map/all_to_all | solution.py:691
  255.8 46.6 %collective-permute-start.4 = (f32[2,64,256]{2,1,0:T(8,128)S(1)}, f32[2,64,256]{2,1,0:T(8,128)S(1)}, u32[]{:S(2)}, u32[]{:S(2)}) collective-permute-start(f32[2,64,256]{2,1,0:T(8,128)S(1)} %get-tuple-element.76), channel_id=1, source_target_pairs={{0,4},{4,8},{8,12},{12,16},{16,20},{20,24},{24,28},{28,0},{1,5},{5... | collective-permute-start | bytes 393224 | tf_op jit(solution)/shard_map/ppermute | solution.py:297
  257.1 45.3 %collective-permute-start.5 = (f32[2,64,256]{2,1,0:T(8,128)S(1)}, f32[2,64,256]{2,1,0:T(8,128)S(1)}, u32[]{:S(2)}, u32[]{:S(2)}) collective-permute-start(f32[2,64,256]{2,1,0:T(8,128)S(1)} %get-tuple-element.77), channel_id=1, source_target_pairs={{0,28},{4,0},{8,4},{12,8},{16,12},{20,16},{24,20},{28,24},{1,29},{... | collective-permute-start | bytes 393224 | tf_op jit(solution)/shard_map/ppermute | solution.py:297
  258.2 7.4 %collective-permute-start.6 = (f32[32,2,256]{2,1,0:T(2,128)S(1)}, f32[32,2,256]{2,1,0:T(2,128)S(1)}, u32[]{:S(2)}, u32[]{:S(2)}) collective-permute-start(f32[32,2,256]{2,1,0:T(2,128)S(1)} %get-tuple-element.78), channel_id=1, source_target_pairs={{0,1},{1,2},{2,3},{3,0},{4,5},{5,6},{6,7},{7,4},{8,9},{9,10},{10,1... | collective-permute-start | bytes 196616 | tf_op jit(solution)/shard_map/ppermute | solution.py:297
  260.2 8.5 %collective-permute-start.7 = (f32[32,2,256]{2,1,0:T(2,128)S(1)}, f32[32,2,256]{2,1,0:T(2,128)S(1)}, u32[]{:S(2)}, u32[]{:S(2)}) collective-permute-start(f32[32,2,256]{2,1,0:T(2,128)S(1)} %get-tuple-element.79), channel_id=1, source_target_pairs={{0,3},{1,0},{2,1},{3,2},{4,7},{5,4},{6,5},{7,6},{8,11},{9,8},{10,9... | collective-permute-start | bytes 196616 | tf_op jit(solution)/shard_map/ppermute | solution.py:297
  302.4 61.2 %all-to-all-start.5 = ((f32[32,4,32,128]{3,2,1,0:T(8,128)}), f32[32,4,32,128]{3,2,1,0:T(8,128)}, u32[]{:S(2)}, u32[]{:S(2)}) async-start(f32[32,4,32,128]{3,2,1,0:T(8,128)} %bitcast.9), calls=%async_computation.5 | async-start | bytes 4194304 | tf_op jit(solution)/shard_map/all_to_all | solution.py:691
  310.7 46.5 %collective-permute-start.8 = (f32[2,64,256]{2,1,0:T(8,128)S(1)}, f32[2,64,256]{2,1,0:T(8,128)S(1)}, u32[]{:S(2)}, u32[]{:S(2)}) collective-permute-start(f32[2,64,256]{2,1,0:T(8,128)S(1)} %get-tuple-element.82), channel_id=1, source_target_pairs={{0,4},{4,8},{8,12},{12,16},{16,20},{20,24},{24,28},{28,0},{1,5},{5... | collective-permute-start | bytes 393224 | tf_op jit(solution)/shard_map/ppermute | solution.py:297
  311.9 45.3 %collective-permute-start.9 = (f32[2,64,256]{2,1,0:T(8,128)S(1)}, f32[2,64,256]{2,1,0:T(8,128)S(1)}, u32[]{:S(2)}, u32[]{:S(2)}) collective-permute-start(f32[2,64,256]{2,1,0:T(8,128)S(1)} %get-tuple-element.83), channel_id=1, source_target_pairs={{0,28},{4,0},{8,4},{12,8},{16,12},{20,16},{24,20},{28,24},{1,29},{... | collective-permute-start | bytes 393224 | tf_op jit(solution)/shard_map/ppermute | solution.py:297
  313.1 8.3 %collective-permute-start.10 = (f32[32,2,256]{2,1,0:T(2,128)S(1)}, f32[32,2,256]{2,1,0:T(2,128)S(1)}, u32[]{:S(2)}, u32[]{:S(2)}) collective-permute-start(f32[32,2,256]{2,1,0:T(2,128)S(1)} %get-tuple-element.84), channel_id=1, source_target_pairs={{0,1},{1,2},{2,3},{3,0},{4,5},{5,6},{6,7},{7,4},{8,9},{9,10},{10,1... | collective-permute-start | bytes 196616 | tf_op jit(solution)/shard_map/ppermute | solution.py:297
  315.1 8.5 %collective-permute-start.11 = (f32[32,2,256]{2,1,0:T(2,128)S(1)}, f32[32,2,256]{2,1,0:T(2,128)S(1)}, u32[]{:S(2)}, u32[]{:S(2)}) collective-permute-start(f32[32,2,256]{2,1,0:T(2,128)S(1)} %get-tuple-element.85), channel_id=1, source_target_pairs={{0,3},{1,0},{2,1},{3,2},{4,7},{5,4},{6,5},{7,6},{8,11},{9,8},{10,9... | collective-permute-start | bytes 196616 | tf_op jit(solution)/shard_map/ppermute | solution.py:297
  367.1 8.8 %collective-permute-start.12 = (f32[2,64,256]{2,1,0:T(8,128)S(1)}, f32[2,64,256]{2,1,0:T(8,128)S(1)}, u32[]{:S(2)}, u32[]{:S(2)}) collective-permute-start(f32[2,64,256]{2,1,0:T(8,128)S(1)} %get-tuple-element.93), channel_id=1, source_target_pairs={{0,4},{4,8},{8,12},{12,16},{16,20},{20,24},{24,28},{28,0},{1,5},{5... | collective-permute-start | bytes 393224 | tf_op jit(solution)/shard_map/ppermute | solution.py:297
  367.2 8.7 %collective-permute-start.13 = (f32[2,64,256]{2,1,0:T(8,128)S(1)}, f32[2,64,256]{2,1,0:T(8,128)S(1)}, u32[]{:S(2)}, u32[]{:S(2)}) collective-permute-start(f32[2,64,256]{2,1,0:T(8,128)S(1)} %get-tuple-element.94), channel_id=1, source_target_pairs={{0,28},{4,0},{8,4},{12,8},{16,12},{20,16},{24,20},{28,24},{1,29},{... | collective-permute-start | bytes 393224 | tf_op jit(solution)/shard_map/ppermute | solution.py:297
  369.5 4.3 %collective-permute-start.14 = (f32[32,2,256]{2,1,0:T(2,128)S(1)}, f32[32,2,256]{2,1,0:T(2,128)S(1)}, u32[]{:S(2)}, u32[]{:S(2)}) collective-permute-start(f32[32,2,256]{2,1,0:T(2,128)S(1)} %get-tuple-element.95), channel_id=1, source_target_pairs={{0,1},{1,2},{2,3},{3,0},{4,5},{5,6},{6,7},{7,4},{8,9},{9,10},{10,1... | collective-permute-start | bytes 196616 | tf_op jit(solution)/shard_map/ppermute | solution.py:297
  372.2 3.7 collective-permute-start.15
  (14 other events, 72.5 us)
